TPU v7x, 32 devices: a whole 2x2x4 slice. The times are simulated.
32 devices in a mesh: tower: 2 (over x), dp: 16 (over z, y, core).
Axes of the slice: x: 2, y: 2, z: 4, core: 2. Of those that a mesh axis runs over, the one named last changes fastest.
Arguments:
- img_tokens: bfloat16 [256, 50, 768], P(('tower', 'dp')), may hold values from -6 to 6
- txt_tokens: bfloat16 [256, 77, 512], P(('tower', 'dp')), may hold values from -6 to 6
- txt_ends: int32 [256], replicated, may hold values from 12 to 76
- valid: int32 [256, 256], P(('tower', 'dp')), may hold values from 0 to 1, as said below
- img_master: float32 [7481856], P(('tower', 'dp')), may hold values from -2 to 2, as said below
- img_moment: float32 [7481856], P(('tower', 'dp')), may hold values from -6 to 6
- img_average: float32 [7481856], P(('tower', 'dp')), may hold values from -2 to 2, as said below
- txt_master: float32 [3415040], P(('tower', 'dp')), may hold values from -2 to 2, as said below
- txt_moment: float32 [3415040], P(('tower', 'dp')), may hold values from -6 to 6
- txt_average: float32 [3415040], P(('tower', 'dp')), may hold values from -2 to 2, as said below
- scale_state: float32 [3], replicated, may hold values from -512 to 512
Outputs:
- loss: float32 [], replicated
- img_grad: float32 [256, 50, 768], P(('tower', 'dp'))
- txt_grad: float32 [256, 77, 512], P(('tower', 'dp'))
- img_master_new: float32 [7481856], P(('tower', 'dp'))
- img_moment_new: float32 [7481856], P(('tower', 'dp'))
- img_average_new: float32 [7481856], P(('tower', 'dp'))
- img_copy: bfloat16 [7481856], P(('tower', 'dp'))
- txt_master_new: float32 [3415040], P(('tower', 'dp'))
- txt_moment_new: float32 [3415040], P(('tower', 'dp'))
- txt_average_new: float32 [3415040], P(('tower', 'dp'))
- txt_copy: bfloat16 [3415040], P(('tower', 'dp'))
- scale_new: float32 [3], replicated
Inputs may be any that keep to these rules, and one draw needn't show every extreme that they name: valid[i][j] equals valid[j][i], and valid[i][i] is 1. `img_master`: laid out as the first step says. `img_average`: laid out as the first step says. `txt_master`: laid out as the first step says. `txt_average`: laid out as the first step says.
All inputs are finite; a program needn't handle non-finite values.
Results may differ from a plain program's by a relative error of at most 0.02.
Values may be sent and summed in bfloat16 or wider, within the bound.
A program may use at most 320 MiB of HBM per device.

v0:
```python
import math

import jax
import jax.numpy as jnp
from jax import lax
from jax.sharding import PartitionSpec as P

D_IMG = 768
FF_IMG = 3072
D_TXT = 512
FF_TXT = 2048
EMB = 512
HEAD = 64


momentum_rate = 0.5
average_rate = 0.5
step_rate = 0.08
scale_rate = 0.0001


def from_partner(value, axis, stride):
    mask = 2**stride
    pairs = [(source, source ^ mask) for source in range(lax.axis_size(axis))]
    return lax.ppermute(value, axis, pairs)


def round_value(v):
    return lax.optimization_barrier(v.astype(jnp.bfloat16)).astype(jnp.float32)


def make_low():

    def value_keep(v):
        return (round_value(v), None)

    def grad_pass(kept, grad):
        return (grad,)

    rounded = jax.custom_vjp(round_value)
    rounded.defvjp(value_keep, grad_pass)
    return rounded


def low(v):
    return make_low()(v)


def make_low_back():

    def identity(v):
        return v

    def value_pass(v):
        return (v, None)

    def grad_round(kept, grad):
        return (round_value(grad),)

    passed = jax.custom_vjp(identity)
    passed.defvjp(value_pass, grad_round)
    return passed


def low_back(v):
    return make_low_back()(v)


def both_ways(value):
    return low(low_back(value))


def product(left, right):
    return jnp.matmul(left, right)


def contract(form, left, right):
    return jnp.einsum(form, left, right)


def layer_norm(values, gain_row, shift_row):
    centred = values - jnp.mean(values, axis=-1, keepdims=True)
    spread = jnp.mean(centred * centred, axis=-1, keepdims=True)
    return centred * lax.rsqrt(spread + 1e-05) * gain_row + shift_row


def unpack(flat_weights, model_width, hidden_width, embed_width):
    piece_shapes = [
        (model_width, 3 * model_width),
        (model_width, model_width),
        (model_width, hidden_width),
        (hidden_width, model_width),
        (model_width, embed_width),
        (10, model_width),
        (hidden_width,),
    ]
    pieces = []
    offset = 0
    for piece_shape in piece_shapes:
        length = math.prod(piece_shape)
        pieces.append(flat_weights[offset : offset + length].reshape(piece_shape))
        offset = offset + length
    return pieces


def encode(tokens, flat_weights, positions, causal, model_width, hidden_width, embed_width):
    w_inputs, w_output, w_expand, w_reduce, w_embed, vectors, expand_bias = unpack(
        flat_weights, model_width, hidden_width, embed_width
    )
    groups = tokens.shape[0]
    length = tokens.shape[1]
    first = low(layer_norm(tokens, vectors[0], vectors[1]))
    bias_in = jnp.concatenate([vectors[2], jnp.zeros_like(vectors[2]), vectors[3]])
    joined = both_ways(product(first, w_inputs) + bias_in)
    joined = joined.reshape(groups, length, 3, model_width // HEAD, HEAD)
    scores = low_back(contract("gqhd,gkhd->ghqk", joined[:, :, 0], joined[:, :, 1]) * 0.125)
    if causal:
        row_index = lax.broadcasted_iota(jnp.int32, (length, length), 0)
        col_index = lax.broadcasted_iota(jnp.int32, (length, length), 1)
        scores = jnp.where(col_index <= row_index, scores, -1e30)
    row_top = jnp.max(scores, axis=-1, keepdims=True)
    raw_weights = jnp.exp(scores - row_top)
    attention = low(raw_weights / jnp.sum(raw_weights, axis=-1, keepdims=True))
    mixed_heads = both_ways(
        contract("ghqk,gkhd->gqhd", attention, joined[:, :, 2]).reshape(groups, length, model_width)
    )
    middle = tokens + low_back(product(mixed_heads, w_output) + vectors[4])
    second = low(layer_norm(middle, vectors[5], vectors[6]))
    raised = low_back(product(second, w_expand) + expand_bias)
    active = low(raised * jax.nn.sigmoid(1.702 * raised))
    final_rows = middle + low_back(product(active, w_reduce) + vectors[7])
    pooled = jnp.take_along_axis(final_rows, positions[:, None, None], axis=1)[:, 0]
    pooled = low(layer_norm(pooled, vectors[8], vectors[9]))
    projected = low_back(product(pooled, w_embed))
    return low(
        projected * lax.rsqrt(jnp.sum(projected * projected, axis=-1, keepdims=True) + 1e-06)
    )


def inner(left, right):
    return lax.dot_general(
        left, right, (((1,), (1,)), ((), ())), preferred_element_type=jnp.float32
    )


def across(left, right):
    return lax.dot_general(
        left, right, (((0,), (0,)), ((), ())), preferred_element_type=jnp.float32
    )


def softmax_total(logits, allowed):
    masked = jnp.where(allowed, logits, -1e30)
    row_top = jnp.max(masked, axis=1, keepdims=True)
    return jnp.log(jnp.sum(jnp.exp(masked - row_top), axis=1)) + row_top[:, 0]


def advance(master, moment, average, grads, rate):
    moment_new = momentum_rate * moment + grads
    master_new = master - rate * (grads + momentum_rate * moment_new)
    average_new = average_rate * average + (1.0 - average_rate) * master_new
    return (master_new, moment_new, average_new)


def padded_to(flat, length):
    return jnp.pad(flat, (0, length - flat.shape[0]))


def body(
    img_tokens,
    txt_tokens,
    txt_ends,
    valid,
    img_master,
    img_moment,
    img_average,
    txt_master,
    txt_moment,
    txt_average,
    scale_state,
):
    batch_rows = img_tokens.shape[0]
    total_rows = batch_rows * lax.axis_size(("tower", "dp"))
    device_at = lax.axis_index(("tower", "dp"))
    tower_at = lax.axis_index("tower")
    is_image = tower_at == 0
    img_share = img_master.shape[0]
    txt_share = txt_master.shape[0]
    img_count = img_tokens.size
    txt_count = txt_tokens.size
    shard_room = max(img_share, txt_share)
    token_room = max(img_count, txt_count)
    tower_count = lax.axis_size("dp")
    dp_at = lax.axis_index("dp")
    img_low = padded_to(img_master.astype(jnp.bfloat16), shard_room)
    txt_low = padded_to(txt_master.astype(jnp.bfloat16), shard_room)
    token_out = jnp.where(
        is_image,
        padded_to(txt_tokens.reshape(-1), token_room),
        padded_to(img_tokens.reshape(-1), token_room),
    )
    weight_out = jnp.where(is_image, txt_low, img_low)
    weight_mine = jnp.where(is_image, img_low, txt_low)
    token_in, weight_in = from_partner((token_out, weight_out), "tower", 0)
    stacked = jnp.where(
        is_image, jnp.stack([weight_mine, weight_in]), jnp.stack([weight_in, weight_mine])
    )
    gathered = lax.all_gather(stacked, "dp", axis=1, tiled=True)
    pair_ends = jnp.concatenate(
        [
            lax.dynamic_slice_in_dim(txt_ends, dp_at * batch_rows, batch_rows),
            lax.dynamic_slice_in_dim(txt_ends, (tower_count + dp_at) * batch_rows, batch_rows),
        ]
    )
    pair_zero = jnp.zeros((2 * batch_rows,), jnp.int32)

    def image_weights(whole):
        return whole.reshape(2, tower_count, shard_room).reshape(-1).astype(jnp.float32)

    def text_weights(whole):
        return (
            whole.reshape(2, tower_count, shard_room)[:, :, :txt_share]
            .reshape(-1)
            .astype(jnp.float32)
        )

    def image_rows(arrived):
        return jnp.concatenate(
            [img_tokens, arrived[:img_count].reshape(img_tokens.shape)], axis=0
        ).astype(jnp.float32)

    def text_rows(arrived):
        return jnp.concatenate([arrived.reshape(txt_tokens.shape), txt_tokens], axis=0).astype(
            jnp.float32
        )

    def image_encode(rows, flat):
        return encode(rows, flat, pair_zero, False, D_IMG, FF_IMG, EMB)

    def text_encode(rows, flat):
        return encode(rows, flat, pair_ends, True, D_TXT, FF_TXT, EMB)

    def image_forward(operands):
        return image_encode(image_rows(operands[1]), image_weights(operands[0]))

    def text_forward(operands):
        return text_encode(text_rows(operands[1]), text_weights(operands[0]))

    pair_emb = lax.cond(is_image, image_forward, text_forward, (gathered, token_in)).astype(
        jnp.bfloat16
    )
    emb_in = from_partner(pair_emb, "tower", 0)
    img_pair = jnp.where(is_image, pair_emb, emb_in)
    txt_pair = jnp.where(is_image, emb_in, pair_emb)
    row_start = tower_at * batch_rows
    img_local = lax.dynamic_slice_in_dim(img_pair, row_start, batch_rows)
    txt_local = lax.dynamic_slice_in_dim(txt_pair, row_start, batch_rows)
    img_all, txt_all = (
        lax.all_gather(img_local, ("tower", "dp"), axis=0, tiled=True),
        lax.all_gather(txt_local, ("tower", "dp"), axis=0, tiled=True),
    )
    logit_scale = jnp.exp(scale_state[0])
    offset = device_at * batch_rows
    row_index = lax.broadcasted_iota(jnp.int32, (batch_rows, total_rows), 0) + offset
    col_index = lax.broadcasted_iota(jnp.int32, (batch_rows, total_rows), 1)
    diagonal = (row_index == col_index).astype(jnp.float32)
    allowed = valid > 0
    row_logits = logit_scale * inner(img_local, txt_all)
    col_logits = logit_scale * inner(txt_local, img_all)
    row_lse = softmax_total(row_logits, allowed)
    col_lse = softmax_total(col_logits, allowed)
    partial_loss = 0.5 * (
        jnp.sum(row_lse)
        - jnp.sum(row_logits * diagonal)
        + jnp.sum(col_lse)
        - jnp.sum(col_logits * diagonal)
    )
    row_terms = 0.5 * (jnp.where(allowed, jnp.exp(row_logits - row_lse[:, None]), 0.0) - diagonal)
    col_terms = 0.5 * (jnp.where(allowed, jnp.exp(col_logits - col_lse[:, None]), 0.0) - diagonal)
    partial_scale = jnp.sum(row_terms * row_logits) + jnp.sum(col_terms * col_logits)
    row_back = (logit_scale * row_terms).astype(jnp.bfloat16)
    col_back = (logit_scale * col_terms).astype(jnp.bfloat16)
    img_emb_grad = jnp.dot(row_back, txt_all, preferred_element_type=jnp.float32)
    txt_emb_grad = jnp.dot(col_back, img_all, preferred_element_type=jnp.float32)
    img_extra, txt_extra = (
        lax.psum_scatter(
            across(col_back, txt_local), ("tower", "dp"), scatter_dimension=0, tiled=True
        ),
        lax.psum_scatter(
            across(row_back, img_local), ("tower", "dp"), scatter_dimension=0, tiled=True
        ),
    )
    img_emb_grad = img_emb_grad + img_extra
    txt_emb_grad = txt_emb_grad + txt_extra
    sums = lax.psum((partial_loss, partial_scale), ("tower", "dp"))
    grad_out = jnp.where(is_image, txt_emb_grad, img_emb_grad)
    grad_in = from_partner(grad_out, "tower", 0)
    pair_cot = jnp.where(
        is_image,
        jnp.concatenate([img_emb_grad, grad_in], axis=0),
        jnp.concatenate([grad_in, txt_emb_grad], axis=0),
    )

    def image_backward(operands):
        recomputed, tower_pullback = jax.vjp(
            image_encode, image_rows(operands[1]), image_weights(operands[0])
        )
        rows_grad, flat_grad = tower_pullback(operands[2])
        own_part = padded_to(rows_grad[:batch_rows].reshape(-1), token_room)
        sent_part = padded_to(rows_grad[batch_rows:].reshape(-1), token_room)
        stacked_grad = flat_grad.reshape(2, tower_count, img_share)
        return (own_part, sent_part, stacked_grad)

    def text_backward(operands):
        recomputed, tower_pullback = jax.vjp(
            text_encode, text_rows(operands[1]), text_weights(operands[0])
        )
        rows_grad, flat_grad = tower_pullback(operands[2])
        own_part = padded_to(rows_grad[batch_rows:].reshape(-1), token_room)
        sent_part = padded_to(rows_grad[:batch_rows].reshape(-1), token_room)
        stacked_grad = jnp.pad(
            flat_grad.reshape(2, tower_count, txt_share),
            ((0, 0), (0, 0), (0, shard_room - txt_share)),
        )
        return (own_part, sent_part, stacked_grad)

    own_part, sent_part, stacked_grad = lax.cond(
        is_image, image_backward, text_backward, (gathered, token_in, pair_cot)
    )
    summed = lax.psum_scatter(stacked_grad, "dp", scatter_dimension=1, tiled=True)
    kept_part = jnp.where(is_image, summed[0, 0], summed[1, 0])
    sent_share = jnp.where(is_image, summed[1, 0], summed[0, 0])
    home_weights, home_tokens = (
        from_partner(sent_share.astype(jnp.bfloat16), "tower", 0).astype(sent_share.dtype),
        from_partner(sent_part.astype(jnp.bfloat16), "tower", 0).astype(sent_part.dtype),
    )
    img_owned = jnp.where(is_image, kept_part, home_weights)
    txt_owned = jnp.where(is_image, home_weights, kept_part)[:txt_share]
    img_grad = jnp.where(is_image, own_part, home_tokens)[:img_count].reshape(img_tokens.shape)
    txt_grad = jnp.where(is_image, home_tokens, own_part).reshape(txt_tokens.shape)
    img_new = advance(img_master, img_moment, img_average, img_owned, step_rate)
    txt_new = advance(txt_master, txt_moment, txt_average, txt_owned, step_rate)
    scale_parts = advance(scale_state[0], scale_state[1], scale_state[2], sums[1], scale_rate)
    scale_new = jnp.stack([scale_parts[0], scale_parts[1], scale_parts[2]])
    return (
        sums[0] / total_rows,
        img_grad,
        txt_grad,
        img_new[0],
        img_new[1],
        img_new[2],
        img_new[0].astype(jnp.bfloat16),
        txt_new[0],
        txt_new[1],
        txt_new[2],
        txt_new[0].astype(jnp.bfloat16),
        scale_new,
    )


def solution(mesh):
    in_specs = (
        P(("tower", "dp"), None, None),
        P(("tower", "dp"), None, None),
        P(),
        P(("tower", "dp"), None),
        P(("tower", "dp")),
        P(("tower", "dp")),
        P(("tower", "dp")),
        P(("tower", "dp")),
        P(("tower", "dp")),
        P(("tower", "dp")),
        P(),
    )
    out_specs = (
        P(),
        P(("tower", "dp"), None, None),
        P(("tower", "dp"), None, None),
        P(("tower", "dp")),
        P(("tower", "dp")),
        P(("tower", "dp")),
        P(("tower", "dp")),
        P(("tower", "dp")),
        P(("tower", "dp")),
        P(("tower", "dp")),
        P(("tower", "dp")),
        P(),
    )
    return jax.shard_map(body, mesh=mesh, in_specs=in_specs, out_specs=out_specs, check_vma=False)
```

profile of v0, /device:TPU:3, one launch (start us, length us, event | category | flops | bytes accessed | tf_op | source)
XLA Modules:
  0.0 1918.5 jit_solution(16518095055721281748)
XLA Ops:
  35.7 115.5 %all-gather.3.cloned.1.call-done = bf16[16,233808,2]{1,2,0:T(2,128)(2,1)} async-done(((bf16[1,233808,2]{1,2,0:T(2,128)(2,1)}), bf16[16,233808,2]{1,2,0:T(2,128)(2,1)}) %all-gather.3.cloned.1.call-update) | async-done | bytes 14963728 | tf_op jit(solution)/shard_map/all_gather | solution.py:208
  151.2 14.9 copy.366
  166.1 34.6 %reshape.902 = bf16[7481856]{0:T(1024)(128)(2,1)} reshape(bf16[2,16,233808]{2,1,0:T(8,128)(2,1)} %bitcast.303) | data formatting | bytes 29927424
  200.7 36.6 %reshape.903 = bf16[2,3740928]{1,0:T(2,128)(2,1)} reshape(bf16[7481856]{0:T(1024)(128)(2,1)} %reshape.902) | data formatting | bytes 29927424
  237.3 13.1 bitcast_bitcast_fusion
  250.4 192.9 %conditional.2 = (bf16[16,512]{1,0:T(8,128)(2,1)S(1)}) conditional(s32[]{:T(128)} %convert_element_type.308, (s32[16]{0:T(128)S(1)}, bf16[315392]{0:T(1024)(128)(2,1)}, bf16[8,77,512]{2,0,1:T(8,128)(2,1)S(1)}, bf16[2,3740928]{1,0:T(2,128)(2,1)}) %tuple.178, (bf16[315392]{0:T(1024)(128)(2,1)}, bf16[8,50,768]{2,0,1:T(8,128)(2,1)S(1)}, ...), branch_computations={%region_0.10_spmd, %region_10.20_spmd} | conditional | flops 11503048704 | bytes 256032320 | solution.py:249
  250.9 31.8 %reshape.894 = bf16[7481856]{0:T(1024)(128)(2,1)} reshape(bf16[2,3740928]{1,0:T(2,128)(2,1)} %get-tuple-element.39) | data formatting | bytes 29927424 | tf_op jit(solution)/shard_map/cond
  282.6 32.0 %reshape.744 = bf16[2,16,233808]{2,1,0:T(8,128)(2,1)} reshape(bf16[7481856]{0:T(1024)(128)(2,1)} %reshape.894) | data formatting | bytes 29927424 | tf_op jit(solution)/shard_map/cond/branch_0_fun/reshape | solution.py:222
  320.7 16.0 reshape.745
  390.4 11.7 slice.300
  443.3 23.4 %collective-permute-start.2 = (bf16[16,512]{1,0:T(8,128)(2,1)S(1)}, bf16[16,512]{1,0:T(8,128)(2,1)S(1)}, u32[]{:S(2)}, u32[]{:S(2)}) collective-permute-start(bf16[16,512]{1,0:T(8,128)(2,1)S(1)} %get-tuple-element.345), channel_id=1, source_target_pairs={{0,16},{16,0},{1,17},{17,1},{2,18},{18,2},{3,19},{19,3},{4,20},{20... | collective-permute-start | bytes 49160 | tf_op jit(solution)/shard_map/ppermute | solution.py:25
  467.9 40.7 %all_gather.10 = bf16[256,512]{1,0:T(8,128)(2,1)S(1)} all-gather(bf16[8,512]{1,0:T(8,128)(2,1)S(1)} %get-tuple-element.330), channel_id=1, replica_groups=mesh['tower'=2,'dp'=16] {'tower','dp'}, dimensions={0}, use_global_device_ids=true | all-gather | bytes 270336 | tf_op jit(solution)/shard_map/all_gather | solution.py:260
  508.6 37.3 %all_gather.11 = bf16[256,512]{1,0:T(8,128)(2,1)S(1)} all-gather(bf16[8,512]{1,0:T(8,128)(2,1)S(1)} %get-tuple-element.329), channel_id=1, replica_groups=mesh['tower'=2,'dp'=16] {'tower','dp'}, dimensions={0}, use_global_device_ids=true | all-gather | bytes 270336 | tf_op jit(solution)/shard_map/all_gather | solution.py:259
  551.0 124.9 %reduce-scatter.3.cloned.1.call-done = f32[8,512]{1,0:T(8,128)} async-done(((f32[256,512]{1,0:T(8,128)}), f32[8,512]{1,0:T(8,128)}) %reduce-scatter.3.cloned.1.call-update) | async-done | bytes 16400 | tf_op jit(solution)/shard_map/reduce_scatter | solution.py:286
  676.8 132.4 %reduce-scatter.5.cloned.1.call-done = f32[8,512]{1,0:T(8,128)} async-done(((f32[256,512]{1,0:T(8,128)}), f32[8,512]{1,0:T(8,128)}) %reduce-scatter.5.cloned.1.call-update) | async-done | bytes 16400 | tf_op jit(solution)/shard_map/reduce_scatter | solution.py:289
  812.8 418.9 %conditional.3 = (f32[315392]{0:T(1024)S(1)}, bf16[315392]{0:T(1024)(128)(2,1)}, f32[2,16,233808]{2,1,0:T(8,128)}) conditional(s32[]{:T(128)} %convert_element_type.308, (s32[16]{0:T(128)S(1)}, bf16[315392]{0:T(1024)(128)(2,1)}, bf16[8,77,512]{2,0,1:T(8,128)(2,1)S(1)}, bf16[2,3740928]{1,0:T(2,128)(2,1)}, f32[16,512]{1,0:T(8,128)S(1)}) %tuple.181, ...), branch_computations={%region_31.62_spmd, %region_62.93_spmd} | conditional | flops 34562215936 | bytes 896888768 | solution.py:327
  815.7 40.5 %reshape.898 = bf16[7481856]{0:T(1024)(128)(2,1)} reshape(bf16[2,3740928]{1,0:T(2,128)(2,1)} %get-tuple-element.47) | data formatting | bytes 29927424 | tf_op jit(solution)/shard_map/cond
  856.2 31.8 %reshape.755 = bf16[2,16,233808]{2,1,0:T(8,128)(2,1)} reshape(bf16[7481856]{0:T(1024)(128)(2,1)} %reshape.898) | data formatting | bytes 29927424 | tf_op jit(solution)/shard_map/cond/branch_0_fun/reshape | solution.py:222
  894.1 16.0 reshape.756
  963.7 11.9 slice.343
  1009.6 11.6 fusion.46
  1066.0 15.2 copy.217
  1081.2 10.9 convert_element_type.265
  1137.1 35.8 %pad_add_fusion = f32[3415040]{0:T(1024)} fusion(f32[786432]{0:T(1024)} %reshape.771, f32[262144]{0:T(1024)} %bitcast.321, f32[1048576]{0:T(1024)} %bitcast.310, f32[1048576]{0:T(1024)S(1)} %bitcast.309, f32[262144]{0:T(1024)S(1)} %bitcast.320, f32[5120]{0:T(1024)S(1)} %reshape.766, f32[2048]{0:T(1024)S(1)} %convert_reduce_fusion.2), kind=kLoop, calls=%fused_computation.108 | loop fusion | flops 20490240 | bytes 27320320 | tf_op jit(solution)/shard_map/cond/branch_0_fun/transpose(jvp())/add_any | solution.py:101
  1172.9 18.5 reshape.772
  1191.4 16.6 pad.114
  1231.8 41.4 %copy.248 = f32[2,16,233808]{2,0,1:T(2,128)} copy(f32[2,16,233808]{2,1,0:T(8,128)} %get-tuple-element.69) | data formatting | bytes 59854848 | tf_op jit(solution)/shard_map/cond | solution.py:327
  1273.3 89.2 %collective-permute-start.4 = (bf16[315392]{0:T(1024)(128)(2,1)}, bf16[315392]{0:T(1024)(128)(2,1)S(1)}, u32[]{:S(2)}, u32[]{:S(2)}) collective-permute-start(bf16[315392]{0:T(1024)(128)(2,1)} %get-tuple-element.68), channel_id=1, source_target_pairs={{0,16},{16,0},{1,17},{17,1},{2,18},{18,2},{3,19},{19,3},{4,20},{20... | collective-permute-start | bytes 1892360 | tf_op jit(solution)/shard_map/ppermute | solution.py:25
  1368.2 46.3 %all-reduce.46 = (f32[]{:T(128)}, f32[]{:T(128)}) all-reduce(f32[]{:T(128)S(6)} %mul.749, f32[]{:T(128)S(6)} %add.621), channel_id=1, replica_groups=mesh['tower'=2,'dp'=16] {'tower','dp'}, use_global_device_ids=true, to_apply=%region_28.29 | all-reduce | flops 2 | bytes 16 | tf_op jit(solution)/shard_map/psum | solution.py:295
  1419.5 456.7 %all-reduce.49.cloned.1.call-done = f32[2,16,233808]{2,0,1:T(2,128)} async-done(((f32[2,16,233808]{2,0,1:T(2,128)}), f32[2,16,233808]{2,0,1:T(2,128)}) %all-reduce.49.cloned.1.call-update) | async-done | bytes 29927440
  1876.2 11.8 fusion.156
  1893.2 12.6 fusion.154
  (363 shorter events, 327.3 us)
Async XLA Ops:
  7.2 144.1 %all-gather.3.cloned.1.call-start = ((), (), s32[]{:S(2)}) async-start(), calls=%async_computation.4 | async-start | bytes 15902208 | tf_op jit(solution)/shard_map/all_gather | solution.py:208
  9.6 11.7 collective-permute-start.1
  15.0 18.0 copy-start.55
  33.0 642.9 %reduce-scatter.3.cloned.1.call-start = ((), (), s32[]{:S(2)}) async-start(), calls=%async_computation.2 | async-start | bytes 540672 | tf_op jit(solution)/shard_map/reduce_scatter | solution.py:286
  34.5 215.9 %collective-permute-start = (bf16[315392]{0:T(1024)(128)(2,1)S(1)}, bf16[315392]{0:T(1024)(128)(2,1)}, u32[]{:S(2)}, u32[]{:S(2)}) collective-permute-start(bf16[315392]{0:T(1024)(128)(2,1)S(1)} %pad_select_fusion), channel_id=1, source_target_pairs={{0,16},{16,0},{1,17},{17,1},{2,18},{18,2},{3,19},{19,3},{4,20},{20... | collective-permute-start | bytes 1892360 | tf_op jit(solution)/shard_map/ppermute | solution.py:25
  35.1 215.3 %copy-start.124 = (s32[16]{0:T(128)}, s32[16]{0:T(128)S(1)}, u32[]{:S(2)}) copy-start(s32[16]{0:T(128)S(1)} %pad_add_fusion.4) | copy-start | bytes 196
  443.3 369.5 %copy-start.54 = (bf16[8,77,512]{2,0,1:T(8,128)(2,1)S(1)}, bf16[8,77,512]{2,0,1:T(8,128)(2,1)}, u32[]{:S(2)}) copy-start(bf16[8,77,512]{2,0,1:T(8,128)(2,1)} %param.16) | copy-start | bytes 1892356
  443.3 369.4 %copy-start.125 = (s32[16]{0:T(128)S(1)}, s32[16]{0:T(128)}, u32[]{:S(2)}) copy-start(s32[16]{0:T(128)} %copy-done.124) | copy-start | bytes 196
  443.3 24.5 %collective-permute-start.2 = (bf16[16,512]{1,0:T(8,128)(2,1)S(1)}, bf16[16,512]{1,0:T(8,128)(2,1)S(1)}, u32[]{:S(2)}, u32[]{:S(2)}) collective-permute-start(bf16[16,512]{1,0:T(8,128)(2,1)S(1)} %get-tuple-element.345), channel_id=1, source_target_pairs={{0,16},{16,0},{1,17},{17,1},{2,18},{18,2},{3,19},{19,3},{4,20},{20... | collective-permute-start | bytes 49160 | tf_op jit(solution)/shard_map/ppermute | solution.py:25
  466.8 346.0 %copy-start.110 = (s32[8]{0:T(128)}, s32[8]{0:T(128)S(1)}, u32[]{:S(2)}) copy-start(s32[8]{0:T(128)S(1)} %iota_add_fusion) | copy-start | bytes 100
  546.0 266.7 %copy-start.94 = (f32[8,256]{1,0:T(8,128)}, f32[8,256]{1,0:T(8,128)S(1)}, u32[]{:S(2)}) copy-start(f32[8,256]{1,0:T(8,128)S(1)} %convolution_multiply_fusion.1) | copy-start | bytes 24580
  547.1 265.7 %copy-start.96 = (f32[8,256]{1,0:T(8,128)}, f32[8,256]{1,0:T(8,128)S(1)}, u32[]{:S(2)}) copy-start(f32[8,256]{1,0:T(8,128)S(1)} %get-tuple-element.336) | copy-start | bytes 24580
  547.1 265.7 %copy-start.102 = (pred[8,256]{1,0:T(8,128)(4,1)}, pred[8,256]{1,0:T(8,128)(4,1)S(1)}, u32[]{:S(2)}) copy-start(pred[8,256]{1,0:T(8,128)(4,1)S(1)} %get-tuple-element.232) | copy-start | bytes 6148
  548.0 264.9 %copy-start.112 = (f32[8]{0:T(128)}, f32[8]{0:T(128)S(1)}, u32[]{:S(2)}) copy-start(f32[8]{0:T(128)S(1)} %get-tuple-element.229) | copy-start | bytes 100
  549.1 260.0 %reduce-scatter.5.cloned.1.call-start = ((), (), s32[]{:S(2)}) async-start(), calls=%async_computation.3 | async-start | bytes 540672 | tf_op jit(solution)/shard_map/reduce_scatter | solution.py:289
  549.8 263.0 %copy-start.114 = (f32[8]{0:T(128)}, f32[8]{0:T(128)S(1)}, u32[]{:S(2)}) copy-start(f32[8]{0:T(128)S(1)} %get-tuple-element.231) | copy-start | bytes 100
  551.0 1325.3 %all-reduce.49.cloned.1.call-start = ((), (), s32[]{:S(2)}) async-start(), calls=%async_computation.5 | async-start | bytes 59867136
  810.0 2.7 collective-permute-start.3
  814.6 161.1 %copy-start.11 = (bf16[8,77,512]{2,1,0:T(8,128)(2,1)}, bf16[8,77,512]{2,1,0:T(8,128)(2,1)S(1)}, u32[]{:S(2)}) copy-start(bf16[8,77,512]{2,1,0:T(8,128)(2,1)S(1)} %reshape.754) | copy-start | bytes 1892356 | tf_op jit(solution)/shard_map/cond
  815.7 40.5 %copy-start.106 = (f32[16,77]{1,0:T(8,128)}, f32[16,77]{1,0:T(8,128)S(1)}, u32[]{:S(2)}) copy-start(f32[16,77]{1,0:T(8,128)S(1)} %fusion.67) | copy-start | bytes 14788 | tf_op jit(solution)/shard_map/cond
  1009.3 17.0 copy-start.4
  1191.4 16.7 copy-start.23
  1191.4 16.7 copy-start.48
  1273.2 89.9 %copy-start.95 = (f32[8,256]{1,0:T(8,128)S(1)}, f32[8,256]{1,0:T(8,128)}, u32[]{:S(2)}) copy-start(f32[8,256]{1,0:T(8,128)} %copy-done.94) | copy-start | bytes 24580
  1273.2 89.9 %copy-start.97 = (f32[8,256]{1,0:T(8,128)S(1)}, f32[8,256]{1,0:T(8,128)}, u32[]{:S(2)}) copy-start(f32[8,256]{1,0:T(8,128)} %copy-done.96) | copy-start | bytes 24580
  1273.2 89.9 %copy-start.103 = (pred[8,256]{1,0:T(8,128)(4,1)S(1)}, pred[8,256]{1,0:T(8,128)(4,1)}, u32[]{:S(2)}) copy-start(pred[8,256]{1,0:T(8,128)(4,1)} %copy-done.102) | copy-start | bytes 6148
  1273.2 89.9 %copy-start.111 = (s32[8]{0:T(128)S(1)}, s32[8]{0:T(128)}, u32[]{:S(2)}) copy-start(s32[8]{0:T(128)} %copy-done.110) | copy-start | bytes 100
  1273.2 89.9 %copy-start.113 = (f32[8]{0:T(128)S(1)}, f32[8]{0:T(128)}, u32[]{:S(2)}) copy-start(f32[8]{0:T(128)} %copy-done.112) | copy-start | bytes 100
  1273.3 89.9 %copy-start.115 = (f32[8]{0:T(128)S(1)}, f32[8]{0:T(128)}, u32[]{:S(2)}) copy-start(f32[8]{0:T(128)} %copy-done.114) | copy-start | bytes 100
  1273.3 94.3 %copy-start.123 = (u32[32]{0:T(128)S(1)}, u32[32]{0:T(128)}, u32[]{:S(2)}) copy-start(u32[32]{0:T(128)} %constant.458) | copy-start | bytes 388
  1273.3 145.0 %collective-permute-start.4 = (bf16[315392]{0:T(1024)(128)(2,1)}, bf16[315392]{0:T(1024)(128)(2,1)S(1)}, u32[]{:S(2)}, u32[]{:S(2)}) collective-permute-start(bf16[315392]{0:T(1024)(128)(2,1)} %get-tuple-element.68), channel_id=1, source_target_pairs={{0,16},{16,0},{1,17},{17,1},{2,18},{18,2},{3,19},{19,3},{4,20},{20... | collective-permute-start | bytes 1892360 | tf_op jit(solution)/shard_map/ppermute | solution.py:25
  1888.0 17.8 collective-permute-start.5
  (55 other events, 277.8 us)
Sparse Core Ops, SparseCore 0:
  33.1 118.1 all-gather.2
  549.3 126.5 reduce-scatter.2
  678.8 130.3 reduce-scatter.4
  1273.4 602.7 all-reduce.48
where the time goes:
time: 1940 us; the launch traced here: 1920 us
  waiting for transfers between devices  839 us (43%)
  local copies, waits for them, and re-layouts  533 us (27%)
  matrix products  125 us (6%)
  other arithmetic  124 us (6%)
  blocking collectives  124 us (6%)
  starting transfers between devices  114 us (6%)
  loops' own time  35.6 us (2%)
  between operations  24.2 us (1%)
    unnamed x5, waiting for transfers between devices  457 us
    reduce_scatter x1, waiting for transfers between devices, body(): lax.psum_scatter(across(row_back, img_local), ('tower', 'dp'), scatter_di...  132 us
    reduce_scatter x1, waiting for transfers between devices, body(): lax.psum_scatter(across(col_back, txt_local), ('tower', 'dp'), scatter_di...  125 us
    all_gather x1, waiting for transfers between devices, body(): gathered = lax.all_gather(stacked, 'dp', axis=1, tiled=True)  116 us
    ppermute x6, starting transfers between devices, from_partner(): return lax.ppermute(value, axis, pairs)  113 us
    cond x100, local copies, waits for them, and re-layouts  113 us
    dot_general x20, matrix products, product(): return jnp.matmul(left, right)  89.4 us
    unnamed x68, local copies, waits for them, and re-layouts  88.5 us
  transfers between devices with their start and end apart: 10, of which 7 were waited for; matrix products, arithmetic and copies ran while one was open for 7% of the time, Pallas kernels for 0%

commit v1 on v0

--- a/solution.py
+++ b/solution.py
@@ -1,8 +1,11 @@
+import functools
 import math
 
 import jax
 import jax.numpy as jnp
 from jax import lax
+from jax.experimental import pallas as pl
+from jax.experimental.pallas import tpu as pltpu
 from jax.sharding import PartitionSpec as P
 
 D_IMG = 768
@@ -17,6 +20,1531 @@
 average_rate = 0.5
 step_rate = 0.08
 scale_rate = 0.0001
+
+
+MESH = pl.DeviceIdType.MESH
+ANY = pl.BlockSpec(memory_space=pl.ANY)
+GRANT = 56 * 1024 * 1024
+LANES = 128
+
+
+def here():
+    return lax.axis_index("tower"), lax.axis_index("dp")
+
+
+def greet(devices):
+    barrier = pltpu.get_barrier_semaphore()
+    for device in devices:
+        pl.semaphore_signal(barrier, inc=1, device_id=device, device_id_type=MESH)
+    pl.semaphore_wait(barrier, len(devices))
+
+
+def remote(src, dst, send_sem, recv_sem, device):
+    return pltpu.make_async_remote_copy(
+        src_ref=src,
+        dst_ref=dst,
+        send_sem=send_sem,
+        recv_sem=recv_sem,
+        device_id=device,
+        device_id_type=MESH,
+    )
+
+
+def comm_params(number):
+    return pltpu.CompilerParams(
+        collective_id=number, has_side_effects=True, vmem_limit_bytes=GRANT
+    )
+
+
+def group_kernel(scattered, x_ref, o_ref, send_sem, recv_sem, own_sem):
+    tower, at = here()
+    chip, core = at // 2, at % 2
+    others = [(chip + k) % 8 for k in range(1, 8)]
+    greet([(tower, other * 2 + core) for other in others])
+    own = pltpu.make_async_copy(x_ref.at[chip] if scattered else x_ref, o_ref.at[chip], own_sem)
+    own.start()
+    sent = []
+    for k, other in enumerate(others):
+        copy = remote(
+            x_ref.at[other] if scattered else x_ref,
+            o_ref.at[chip],
+            send_sem.at[k],
+            recv_sem.at[k],
+            (tower, other * 2 + core),
+        )
+        copy.start()
+        sent.append(copy)
+    own.wait()
+    for k, copy in enumerate(sent):
+        copy.wait_send()
+        source = (chip + 7 - k) % 8
+        remote(
+            x_ref.at[chip] if scattered else x_ref,
+            o_ref.at[source],
+            send_sem.at[k],
+            recv_sem.at[k],
+            (tower, at),
+        ).wait_recv()
+
+
+def group_exchange(value, scattered, number, space=pl.ANY):
+    block = value.shape[1:] if scattered else value.shape
+    spec = pl.BlockSpec(memory_space=space)
+    return pl.pallas_call(
+        functools.partial(group_kernel, scattered),
+        out_shape=jax.ShapeDtypeStruct((8, *block), value.dtype),
+        in_specs=[spec],
+        out_specs=spec,
+        scratch_shapes=[
+            pltpu.SemaphoreType.DMA((7,)),
+            pltpu.SemaphoreType.DMA((7,)),
+            pltpu.SemaphoreType.DMA,
+        ],
+        compiler_params=comm_params(number),
+    )(value)
+
+
+def spread_kernel(x_ref, o_ref, send_sem, recv_sem, own_sem, core_sems):
+    tower, at = here()
+    chip, core = at // 2, at % 2
+    place = tower * 8 + chip
+    others = [(place + k) % 16 for k in range(1, 16)]
+    homes = [(other // 8, (other % 8) * 2 + core) for other in others]
+    sibling = (tower, chip * 2 + 1 - core)
+    greet([*homes, sibling])
+    own = pltpu.make_async_copy(x_ref, o_ref.at[core, place], own_sem)
+    own.start()
+    sent = []
+    for k, home in enumerate(homes):
+        copy = remote(
+            x_ref, o_ref.at[core, place], send_sem.at[k], recv_sem.at[k], home
+        )
+        copy.start()
+        sent.append(copy)
+    own.wait()
+    for k, copy in enumerate(sent):
+        source = (place + 15 - k) % 16
+        remote(
+            x_ref, o_ref.at[core, source], send_sem.at[k], recv_sem.at[k], sibling
+        ).wait_recv()
+    across = remote(o_ref.at[core], o_ref.at[core], core_sems.at[0], core_sems.at[1], sibling)
+    across.start()
+    for copy in sent:
+        copy.wait_send()
+    across.wait_send()
+    remote(
+        o_ref.at[1 - core], o_ref.at[1 - core], core_sems.at[0], core_sems.at[1], sibling
+    ).wait_recv()
+
+
+def spread(value, number, space=pl.ANY):
+    spec = pl.BlockSpec(memory_space=space)
+    return pl.pallas_call(
+        spread_kernel,
+        out_shape=jax.ShapeDtypeStruct((2, 16, *value.shape), value.dtype),
+        in_specs=[spec],
+        out_specs=spec,
+        scratch_shapes=[
+            pltpu.SemaphoreType.DMA((15,)),
+            pltpu.SemaphoreType.DMA((15,)),
+            pltpu.SemaphoreType.DMA,
+            pltpu.SemaphoreType.DMA((2,)),
+        ],
+        compiler_params=comm_params(number),
+    )(value)
+
+
+def exchange_kernel(count, *refs):
+    gather_src, sib_src, one_src, zero_src = refs[:4]
+    blocks_src = refs[4 : 4 + count]
+    gather_dst, sib_dst, one_dst, zero_dst = refs[4 + count : 8 + count]
+    blocks_dst = refs[8 + count : 8 + 2 * count]
+    (
+        ring_send,
+        ring_recv,
+        core_send,
+        core_recv,
+        block_send,
+        block_recv,
+        pair_sems,
+        own_sems,
+    ) = refs[8 + 2 * count :]
+    tower, at = here()
+    deep, row, core = at // 4, (at // 2) % 2, at % 2
+    sibling = (tower, at + 1 - 2 * core)
+    beside = (tower, deep * 4 + (1 - row) * 2 + core)
+    partner = (1 - tower, at)
+
+    def spot(z, y):
+        return (z % 4) * 4 + y * 2 + core
+
+    others = [(tower, (at + k) % 16) for k in range(1, 16)]
+    greet([*others, partner])
+
+    @pl.when(tower == 0)
+    def _():
+        remote(zero_src, zero_dst, pair_sems.at[0], pair_sems.at[1], partner).start()
+
+    @pl.when(tower == 1)
+    def _():
+        remote(one_src, one_dst, pair_sems.at[0], pair_sems.at[1], partner).start()
+
+    owns = [
+        pltpu.make_async_copy(gather_src, gather_dst.at[at], own_sems.at[0]),
+        pltpu.make_async_copy(sib_src, sib_dst.at[core], own_sems.at[1 + count]),
+    ]
+    for b in range(count):
+        owns.append(
+            pltpu.make_async_copy(
+                blocks_src[b].at[at], blocks_dst[b].at[at], own_sems.at[1 + b]
+            )
+        )
+    for own in owns:
+        own.start()
+    sent = []
+
+    def launch(copy):
+        copy.start()
+        sent.append(copy)
+
+    for k in (1, 3, 2):
+        launch(
+            remote(
+                gather_src,
+                gather_dst.at[at],
+                ring_send.at[k - 1],
+                ring_recv.at[k - 1],
+                (tower, spot(deep + k, row)),
+            )
+        )
+    launch(remote(gather_src, gather_dst.at[at], ring_send.at[3], ring_recv.at[3], beside))
+    launch(remote(gather_src, gather_dst.at[at], core_send.at[0], core_recv.at[0], sibling))
+    launch(remote(sib_src, sib_dst.at[core], core_send.at[8], core_recv.at[8], sibling))
+    for b in range(count):
+        for k in range(1, 16):
+            to = (at + k) % 16
+            launch(
+                remote(
+                    blocks_src[b].at[to],
+                    blocks_dst[b].at[at],
+                    block_send.at[b, k - 1],
+                    block_recv.at[b, k - 1],
+                    (tower, to),
+                )
+            )
+
+    def arrived(slot, sems, index):
+        remote(gather_src, gather_dst.at[slot], sems.at[index], sems.at[index], sibling).wait_recv()
+
+    for k in (1, 3, 2):
+        slot = spot(deep + 4 - k, row)
+        arrived(slot, ring_recv, k - 1)
+        launch(
+            remote(
+                gather_dst.at[slot],
+                gather_dst.at[slot],
+                ring_send.at[3 + k],
+                ring_recv.at[3 + k],
+                beside,
+            )
+        )
+        launch(
+            remote(
+                gather_dst.at[slot],
+                gather_dst.at[slot],
+                core_send.at[k],
+                core_recv.at[k],
+                sibling,
+            )
+        )
+    for k in (0, 1, 3, 2):
+        slot = spot(deep + 4 - k, 1 - row)
+        arrived(slot, ring_recv, 3 + k)
+        launch(
+            remote(
+                gather_dst.at[slot],
+                gather_dst.at[slot],
+                core_send.at[4 + k],
+                core_recv.at[4 + k],
+                sibling,
+            )
+        )
+    for y in range(2):
+        for k in range(4):
+            z = (deep + 4 - k) % 4
+            side = row if y == 0 else 1 - row
+            slot = z * 4 + side * 2 + 1 - core
+            arrived(slot, core_recv, 4 * y + k)
+    remote(sib_src, sib_dst.at[1 - core], core_send.at[8], core_recv.at[8], sibling).wait_recv()
+    for b in range(count):
+        for k in range(1, 16):
+            source = (at + 16 - k) % 16
+            remote(
+                blocks_src[b].at[at],
+                blocks_dst[b].at[source],
+                block_send.at[b, k - 1],
+                block_recv.at[b, k - 1],
+                sibling,
+            ).wait_recv()
+    for copy in sent:
+        copy.wait_send()
+    for own in owns:
+        own.wait()
+
+    @pl.when(tower == 0)
+    def _():
+        remote(zero_src, zero_dst, pair_sems.at[0], pair_sems.at[1], partner).wait_send()
+        remote(one_src, one_dst, pair_sems.at[0], pair_sems.at[1], partner).wait_recv()
+
+    @pl.when(tower == 1)
+    def _():
+        remote(one_src, one_dst, pair_sems.at[0], pair_sems.at[1], partner).wait_send()
+        remote(zero_src, zero_dst, pair_sems.at[0], pair_sems.at[1], partner).wait_recv()
+
+
+def exchange(gathered, sibling, from_one, from_zero, blocks, number):
+    count = len(blocks)
+    like = jax.ShapeDtypeStruct
+    return pl.pallas_call(
+        functools.partial(exchange_kernel, count),
+        out_shape=[
+            like((16, *gathered.shape), gathered.dtype),
+            like((2, *sibling.shape), sibling.dtype),
+            like(from_one.shape, from_one.dtype),
+            like(from_zero.shape, from_zero.dtype),
+            *[like(block.shape, block.dtype) for block in blocks],
+        ],
+        in_specs=[ANY] * (4 + count),
+        out_specs=[ANY] * (4 + count),
+        scratch_shapes=[
+            pltpu.SemaphoreType.DMA((7,)),
+            pltpu.SemaphoreType.DMA((7,)),
+            pltpu.SemaphoreType.DMA((9,)),
+            pltpu.SemaphoreType.DMA((9,)),
+            pltpu.SemaphoreType.DMA((count, 15)),
+            pltpu.SemaphoreType.DMA((count, 15)),
+            pltpu.SemaphoreType.DMA((2,)),
+            pltpu.SemaphoreType.DMA((2 + count,)),
+        ],
+        compiler_params=comm_params(number),
+    )(gathered, sibling, from_one, from_zero, *blocks)
+
+
+class Plan:
+    def __init__(self, tower, share, rows, per_device):
+        self.tower = tower
+        self.share = share
+        self.rows = rows
+        self.chunk = rows * LANES
+        self.per_device = per_device
+        self.slots = sum(per_device) + 1
+        self.total = 16 * sum(per_device) + 1
+        spans = [self.span(device) for device in range(32)]
+        self.counts = sorted({last - first + 1 for first, last in spans})
+        self.local = self.counts[-1]
+
+    def span(self, device):
+        first = device * self.share // self.chunk
+        last = ((device + 1) * self.share - 1) // self.chunk
+        return first, min(last, self.total - 1)
+
+    def bounds(self, device):
+        first = device * self.share // self.chunk
+        last = ((device + 1) * self.share - 1) // self.chunk
+        return first, jnp.minimum(last, self.total - 1)
+
+    def target(self, g):
+        base, slot_base = 0, 0
+        at, slot = jnp.int32(0), jnp.int32(0)
+        for n in self.per_device:
+            inside = g >= base
+            at = jnp.where(inside, (g - base) // n, at)
+            slot = jnp.where(inside, slot_base + (g - base) % n, slot)
+            base += 16 * n
+            slot_base += n
+        return at, slot
+
+    def global_chunk(self, at, slot):
+        base, slot_base = 0, 0
+        g = jnp.int32(0)
+        for n in self.per_device:
+            g = jnp.where(slot >= slot_base, base + at * n + (slot - slot_base), g)
+            base += 16 * n
+            slot_base += n
+        return jnp.where(slot == self.slots - 1, self.total - 1, g)
+
+
+def everyone(tower, at):
+    me = tower * 16 + at
+    result = []
+    for k in range(1, 32):
+        other = (me + k) % 32
+        result.append((other // 16, other % 16))
+    return result
+
+
+def deal_kernel(plans, *refs):
+    img_src, txt_src, valid_src = refs[:3]
+    img_dst, txt_dst, valid_dst = refs[3:6]
+    img_extra, txt_extra, img_last, txt_last = refs[6:10]
+    chunk_send, deal_recv, edge_sems, last_sems, valid_send, valid_recv = refs[10:]
+    tower, at = here()
+    me = tower * 16 + at
+    homes = everyone(tower, at)
+    greet(homes)
+    sides = [
+        (plans[0], img_src, img_dst, img_extra, img_last),
+        (plans[1], txt_src, txt_dst, txt_extra, txt_last),
+    ]
+    below = ((me + 31) % 32 // 16, (me + 31) % 32 % 16)
+
+    for s, (plan, src, dst, extra, last) in enumerate(sides):
+
+        @pl.when(me > 0)
+        def _():
+            remote(src.at[0], extra, edge_sems.at[s, 0], edge_sems.at[s, 1], below).start()
+
+    def to_block(plan, s, i, slot_src, dst, at_to, slot, wait):
+        far = jnp.logical_or(tower != plan.tower, at_to != at)
+
+        @pl.when(far)
+        def _():
+            copy = remote(
+                slot_src,
+                dst.at[slot],
+                chunk_send.at[s, i],
+                deal_recv.at[s],
+                (jnp.int32(plan.tower), at_to),
+            )
+            if wait:
+                copy.wait_send()
+            else:
+                copy.start()
+
+        if not wait:
+
+            @pl.when(jnp.logical_not(far))
+            def _():
+                pltpu.make_async_copy(slot_src, dst.at[slot], deal_recv.at[s]).start()
+
+    def whole_chunks(plan, s, src, dst, wait):
+        first, last_chunk = plan.bounds(me)
+
+        def step(i, carry):
+            g = first + i
+            inside = jnp.logical_and(
+                jnp.logical_or(i > 0, me == 0),
+                jnp.logical_and(g <= last_chunk, jnp.logical_or(g < last_chunk, me == 31)),
+            )
+            inside = jnp.logical_and(inside, g < plan.total - 1)
+
+            @pl.when(inside)
+            def _():
+                at_to, slot = plan.target(g)
+                to_block(plan, s, i, src.at[i], dst, at_to, slot, wait)
+
+            return carry
+
+        lax.fori_loop(0, plan.local, step, 0)
+
+        @pl.when(me == 31)
+        def _():
+            i = last_chunk - first
+
+            def each(k, carry):
+                to_block(
+                    plan, s, plan.local + k, src.at[i], dst, k, plan.slots - 1, wait
+                )
+                return carry
+
+            lax.fori_loop(0, 16, each, 0)
+
+    for s, (plan, src, dst, extra, last) in enumerate(sides):
+        whole_chunks(plan, s, src, dst, False)
+    for k, home in enumerate(homes):
+        remote(valid_src, valid_dst.at[me], valid_send.at[k], valid_recv.at[k], home).start()
+    own = pltpu.make_async_copy(valid_src, valid_dst.at[me], valid_send.at[31])
+    own.start()
+
+    for s, (plan, src, dst, extra, last) in enumerate(sides):
+        first, last_chunk = plan.bounds(me)
+
+        @pl.when(me < 31)
+        def _():
+            fetch = pltpu.make_async_copy(src.at[last_chunk - first], last, last_sems.at[s])
+            fetch.start()
+            fetch.wait()
+            remote(src.at[0], extra, edge_sems.at[s, 0], edge_sems.at[s, 1], below).wait_recv()
+            last[...] = last[...] + extra[...]
+            at_to, slot = plan.target(last_chunk)
+            to_block(plan, s, plan.local + 16, last, dst, at_to, slot, False)
+
+    for s, (plan, src, dst, extra, last) in enumerate(sides):
+
+        @pl.when(me > 0)
+        def _():
+            remote(src.at[0], extra, edge_sems.at[s, 0], edge_sems.at[s, 1], below).wait_send()
+
+        whole_chunks(plan, s, src, dst, True)
+        first, last_chunk = plan.bounds(me)
+
+        @pl.when(me < 31)
+        def _():
+            at_to, slot = plan.target(last_chunk)
+            to_block(plan, s, plan.local + 16, last, dst, at_to, slot, True)
+
+        @pl.when(tower == plan.tower)
+        def _():
+            pltpu.make_async_copy(dst, dst, deal_recv.at[s]).wait()
+
+    own.wait()
+    for k, home in enumerate(homes):
+        source = (me + 31 - k) % 32
+        copy = remote(
+            valid_src, valid_dst.at[source], valid_send.at[k], valid_recv.at[k], home
+        )
+        copy.wait_send()
+        copy.wait_recv()
+
+
+def deal(img_chunks, txt_chunks, valid, plans, number):
+    like = jax.ShapeDtypeStruct
+    low = jnp.bfloat16
+    most = max(plan.local for plan in plans) + 17
+    shapes = [(plan.rows, LANES) for plan in plans]
+    return pl.pallas_call(
+        functools.partial(deal_kernel, plans),
+        out_shape=[
+            like((plans[0].slots, *shapes[0]), low),
+            like((plans[1].slots, *shapes[1]), low),
+            like((32, *valid.shape), valid.dtype),
+        ],
+        in_specs=[ANY] * 3,
+        out_specs=[ANY] * 3,
+        scratch_shapes=[
+            pltpu.VMEM(shapes[0], low),
+            pltpu.VMEM(shapes[1], low),
+            pltpu.VMEM(shapes[0], low),
+            pltpu.VMEM(shapes[1], low),
+            pltpu.SemaphoreType.DMA((2, most)),
+            pltpu.SemaphoreType.DMA((2,)),
+            pltpu.SemaphoreType.DMA((2, 2)),
+            pltpu.SemaphoreType.DMA((2,)),
+            pltpu.SemaphoreType.DMA((32,)),
+            pltpu.SemaphoreType.DMA((31,)),
+        ],
+        compiler_params=comm_params(number),
+    )(img_chunks, txt_chunks, valid)
+
+
+def collect_kernel(plans, *refs):
+    sources, targets = refs[:2], refs[2:4]
+    send_sem, recv_sem = refs[4:]
+    tower, at = here()
+    me = tower * 16 + at
+    greet(everyone(tower, at))
+
+    def pass_over(plan, s, wait):
+        src, dst = sources[s], targets[s]
+
+        def one(owner, slot, i, which):
+            first, _ = plan.bounds(owner)
+            g = plan.global_chunk(at, slot)
+            far = owner != me
+
+            @pl.when(far)
+            def _():
+                copy = remote(
+                    src.at[slot],
+                    dst.at[g - first],
+                    send_sem.at[s, which, slot],
+                    recv_sem.at[s],
+                    (owner // 16, owner % 16),
+                )
+                if wait:
+                    copy.wait_send()
+                else:
+                    copy.start()
+
+            if not wait:
+
+                @pl.when(jnp.logical_not(far))
+                def _():
+                    pltpu.make_async_copy(
+                        src.at[slot], dst.at[g - first], recv_sem.at[s]
+                    ).start()
+
+        def step(slot, carry):
+            g = plan.global_chunk(at, slot)
+            low_owner = g * plan.chunk // plan.share
+            high_owner = jnp.minimum(((g + 1) * plan.chunk - 1) // plan.share, 31)
+            use = jnp.logical_or(slot < plan.slots - 1, at == 0)
+
+            @pl.when(use)
+            def _():
+                one(low_owner, slot, 0, 0)
+
+            @pl.when(jnp.logical_and(use, high_owner != low_owner))
+            def _():
+                one(high_owner, slot, 1, 1)
+
+            return carry
+
+        @pl.when(tower == plan.tower)
+        def _():
+            lax.fori_loop(0, plan.slots, step, 0)
+
+    for s in range(2):
+        pass_over(plans[s], s, False)
+    for s in range(2):
+        pass_over(plans[s], s, True)
+    for s in range(2):
+        plan, dst = plans[s], targets[s]
+        first, last = plan.bounds(me)
+        held = last - first + 1
+        for n in plan.counts:
+
+            @pl.when(held == n)
+            def _():
+                part = dst.at[pl.ds(0, n)]
+                pltpu.make_async_copy(part, part, recv_sem.at[s]).wait()
+
+
+def collect(img_slots, txt_slots, plans, number):
+    like = jax.ShapeDtypeStruct
+    most = max(plan.slots for plan in plans)
+    return pl.pallas_call(
+        functools.partial(collect_kernel, plans),
+        out_shape=[
+            like((plan.local, plan.rows, LANES), jnp.bfloat16) for plan in plans
+        ],
+        in_specs=[ANY] * 2,
+        out_specs=[ANY] * 2,
+        scratch_shapes=[
+            pltpu.SemaphoreType.DMA((2, 2, most)),
+            pltpu.SemaphoreType.DMA((2,)),
+        ],
+        compiler_params=comm_params(number),
+    )(img_slots, txt_slots)
+
+
+SEQS = 16
+HEADS = 16
+LOW = jnp.bfloat16
+WIDE = jnp.float32
+
+
+class Tower:
+    def __init__(self, index, width, hidden, length, room, causal):
+        self.index = index
+        self.width = width
+        self.hidden = hidden
+        self.length = length
+        self.room = room
+        self.causal = causal
+        self.heads = width // HEAD
+        self.block = width // 16
+        self.part = hidden // 8
+        self.reduce_rows = hidden // 16
+
+
+TOWERS = (
+    Tower(0, D_IMG, FF_IMG, 50, 64, False),
+    Tower(1, D_TXT, FF_TXT, 77, 80, True),
+)
+ROOM = 80
+WIDTH = D_IMG
+PART = FF_IMG // 8
+AT_OUTPUT = 3 * D_IMG
+AT_EMBED = 4 * D_IMG
+ATTENTION = 4 * D_IMG + EMB
+
+
+def each_tower(run):
+    tower = lax.axis_index("tower")
+    for kind in TOWERS:
+        pl.when(tower == kind.index)(functools.partial(run, kind))
+
+
+def dot_nn(a, b):
+    return lax.dot_general(a, b, (((1,), (0,)), ((), ())), preferred_element_type=WIDE)
+
+
+def dot_nt(a, b):
+    return lax.dot_general(a, b, (((1,), (1,)), ((), ())), preferred_element_type=WIDE)
+
+
+def dot_tn(a, b):
+    return lax.dot_general(a, b, (((0,), (0,)), ((), ())), preferred_element_type=WIDE)
+
+
+def standardise(rows):
+    centred = rows - jnp.mean(rows, axis=-1, keepdims=True)
+    spread = jnp.mean(centred * centred, axis=-1, keepdims=True)
+    rate = lax.rsqrt(spread + 1e-05)
+    return centred * rate, rate
+
+
+def norm_back(grad, gain, hat, rate):
+    scaled = grad * gain
+    return rate * (
+        scaled
+        - jnp.mean(scaled, axis=-1, keepdims=True)
+        - hat * jnp.mean(scaled * hat, axis=-1, keepdims=True)
+    )
+
+
+def head_mask(kind):
+    row = lax.broadcasted_iota(jnp.int32, (HEADS, kind.width), 0)
+    lane = lax.broadcasted_iota(jnp.int32, (HEADS, kind.width), 1)
+    return (lane // HEAD == row).astype(WIDE)
+
+
+def by_head(rows, mask):
+    n, width = rows.shape
+    return (rows[:, None, :] * mask[None]).reshape(n * HEADS, width)
+
+
+def from_heads(rows, mask):
+    width = rows.shape[1]
+    return jnp.sum(rows.reshape(SEQS, HEADS, width) * mask[None], axis=1)
+
+
+def matrix(ref, kind, start, width):
+    return ref[:, : kind.block, start : start + width].reshape(kind.width, width)
+
+
+def vector(vec_ref, kind, row):
+    return vec_ref[row : row + 1, : kind.width]
+
+
+def sequence(kind, refs, s):
+    own, arrived = refs
+    first, second = (own, arrived) if kind.index == 0 else (arrived, own)
+    return first, second
+
+
+def place_kernel(img_ref, txt_ref, att_ref, raise_ref, reduce_ref, vec_ref, flat):
+    def run(kind):
+        ref = img_ref if kind.index == 0 else txt_ref
+        n, rows, lanes = ref.shape
+        flat[: n * rows, :] = ref[...].reshape(n * rows, lanes).astype(WIDE)
+        block, width = kind.block, kind.width
+
+        def lift(base, height, pitch, c):
+            return flat[pl.ds(base + c, height, stride=pitch), :].astype(LOW)
+
+        base = 0
+        for start, wide in ((0, 3 * width), (AT_OUTPUT, width)):
+            pitch = wide // LANES
+            for c in range(pitch):
+                lane = start + c * LANES
+                att_ref[:block, lane : lane + LANES] = lift(base, block, pitch, c)
+            base += block * pitch
+        pitch = kind.hidden // LANES
+        per = kind.part // LANES
+        for c in range(pitch):
+            lane = c % per * LANES
+            raise_ref[c // per, :block, lane : lane + LANES] = lift(base, block, pitch, c)
+        base += block * pitch
+        pitch = width // LANES
+        for c in range(pitch):
+            lane = c * LANES
+            reduce_ref[: kind.reduce_rows, lane : lane + LANES] = lift(
+                base, kind.reduce_rows, pitch, c
+            )
+        base += kind.reduce_rows * pitch
+        pitch = EMB // LANES
+        for c in range(pitch):
+            lane = AT_EMBED + c * LANES
+            att_ref[:block, lane : lane + LANES] = lift(base, block, pitch, c)
+        base += block * pitch
+        pitch = width // LANES
+        for c in range(pitch):
+            vec_ref[:, c * LANES : (c + 1) * LANES] = flat[pl.ds(base + c, 16, stride=pitch), :]
+
+    each_tower(run)
+
+
+def attend_kernel(
+    ends_ref,
+    img_own,
+    img_in,
+    txt_own,
+    txt_in,
+    gat_ref,
+    vec_ref,
+    second_ref,
+    middle_ref,
+    query_ref,
+    keyed_ref,
+    mixture_ref,
+    weight_ref,
+    mixed_ref,
+    first_ref,
+    first_scr,
+    row_scr,
+    at_scr,
+):
+    def run(kind):
+        width, room = kind.width, kind.room
+        gain, shift = vector(vec_ref, kind, 0), vector(vec_ref, kind, 1)
+        refs = (img_own, img_in) if kind.index == 0 else (txt_own, txt_in)
+        halves = sequence(kind, refs, 0)
+        mask = head_mask(kind)
+        positions = lax.broadcasted_iota(jnp.int32, (room, 1), 0)
+        at = lax.axis_index("dp")
+
+        for half in range(2):
+
+            def normalise(i, carry):
+                rows = halves[half][i].astype(WIDE)
+                hat, _ = standardise(rows)
+                first = (hat * gain + shift).astype(LOW)
+                s = half * 8 + i
+                first_scr[s, :room, :width] = first
+                if kind.causal:
+                    chosen = positions == ends_ref[(half * 16 + at) * 8 + i]
+                    top = jnp.sum(jnp.where(chosen, first.astype(WIDE), 0.0), axis=0, keepdims=True)
+                    raw = jnp.sum(jnp.where(chosen, rows, 0.0), axis=0, keepdims=True)
+                else:
+                    top, raw = first[:1].astype(WIDE), rows[:1]
+                row_scr[pl.ds(s, 1), :width] = top
+                at_scr[pl.ds(s, 1), :width] = raw
+                return carry
+
+            lax.fori_loop(0, 8, normalise, 0)
+
+        tops = row_scr[:, :width].astype(LOW)
+        query = dot_nn(tops, matrix(gat_ref, kind, 0, width)) + vector(vec_ref, kind, 2)
+        query = query.astype(LOW)
+        spread_query = by_head(query.astype(WIDE), mask).astype(LOW)
+        keyed = dot_nt(spread_query, matrix(gat_ref, kind, width, width)) * 0.125
+        keyed_ref[:, :width] = keyed.astype(LOW)
+        query_ref[:, :width] = query
+        first_ref[:, :width] = tops
+        lane = lax.broadcasted_iota(jnp.int32, (HEADS, room), 1)
+        live = lax.broadcasted_iota(jnp.int32, (HEADS, room), 0) < kind.heads
+
+        for half in range(2):
+
+            def weigh(i, carry):
+                s = half * 8 + i
+                start = pl.multiple_of(s * HEADS, HEADS)
+                first = first_scr[s, :room, :width]
+                scores = dot_nt(keyed_ref[pl.ds(start, HEADS), :width], first)
+                if kind.causal:
+                    allowed = lane <= ends_ref[(half * 16 + at) * 8 + i]
+                else:
+                    allowed = lane < kind.length
+                scores = jnp.where(allowed, scores, -1e30)
+                raw = jnp.exp(scores - jnp.max(scores, axis=-1, keepdims=True))
+                weights = raw / jnp.sum(raw, axis=-1, keepdims=True)
+                weights = jnp.where(live, weights, 0.0)
+                weight_ref[s, :, :room] = weights
+                mixture_ref[pl.ds(start, HEADS), :width] = dot_nn(
+                    weights.astype(LOW), first
+                ).astype(LOW)
+                return carry
+
+            lax.fori_loop(0, 8, weigh, 0)
+
+        totals = jnp.sum(
+            weight_ref[:, :, :room].astype(LOW).astype(WIDE), axis=-1, keepdims=True
+        ).reshape(SEQS * HEADS, 1)
+        valued = dot_nn(mixture_ref[:, :width], matrix(gat_ref, kind, 2 * width, width))
+        valued = valued + totals * vector(vec_ref, kind, 3)
+        mixed = from_heads(valued, mask).astype(LOW)
+        mixed_ref[:, :width] = mixed
+        middle = (
+            at_scr[:, :width]
+            + dot_nn(mixed, matrix(gat_ref, kind, AT_OUTPUT, width))
+            + vector(vec_ref, kind, 4)
+        )
+        middle_ref[:, :width] = middle
+        hat, _ = standardise(middle)
+        second_ref[:, :width] = (
+            hat * vector(vec_ref, kind, 5) + vector(vec_ref, kind, 6)
+        ).astype(LOW)
+
+    each_tower(run)
+
+
+def expand_matrix(ref, kind):
+    return ref[:, : kind.block, : kind.part].reshape(kind.width, kind.part)
+
+
+def reduce_matrix(ref, kind):
+    return ref[:, : kind.reduce_rows, : kind.width].reshape(kind.part, kind.width)
+
+
+def hidden_bias(vec_ref, kind):
+    chip = lax.axis_index("dp") // 2
+    whole = vec_ref[...]
+    row = lax.broadcasted_iota(jnp.int32, (16, 1), 0)
+    line = jnp.sum(jnp.where(row == 10 + chip // 2, whole, 0.0), axis=0, keepdims=True)
+    return jnp.where(
+        chip % 2 == 0, line[:, : kind.part], line[:, kind.part : 2 * kind.part]
+    )
+
+
+def hidden_kernel(second_ref, raise_ref, reduce_ref, vec_ref, part_ref, raised_ref):
+    def run(kind):
+        width = kind.width
+        rows = second_ref[:, :, :width].reshape(8 * SEQS, width)
+        raised = dot_nn(rows, expand_matrix(raise_ref, kind)) + hidden_bias(vec_ref, kind)
+        raised_ref[:, : kind.part] = raised
+        active = (raised * jax.nn.sigmoid(1.702 * raised)).astype(LOW)
+        part = dot_nn(active, reduce_matrix(reduce_ref, kind))
+        part_ref[:, :, :width] = part.reshape(8, SEQS, width).astype(LOW)
+
+    each_tower(run)
+
+
+def hidden_back_kernel(
+    grad_ref,
+    second_ref,
+    raised_ref,
+    raise_ref,
+    reduce_ref,
+    back_ref,
+    raise_grad_ref,
+    reduce_keep_ref,
+    reduce_send_ref,
+    bias_ref,
+    whole,
+):
+    def run(kind):
+        width, part = kind.width, kind.part
+        grads = grad_ref[:, :, :width].reshape(8 * SEQS, width)
+        rows = second_ref[:, :, :width].reshape(8 * SEQS, width)
+        raised = raised_ref[:, :part]
+        gate = jax.nn.sigmoid(1.702 * raised)
+        active = (raised * gate).astype(LOW)
+        slope = gate + 1.702 * raised * gate * (1.0 - gate)
+        raised_grad = dot_nt(grads, reduce_matrix(reduce_ref, kind)) * slope
+        low_grad = raised_grad.astype(LOW)
+        bias_ref[0:1, :part] = jnp.sum(low_grad.astype(WIDE), axis=0, keepdims=True)
+        back = dot_nt(low_grad, expand_matrix(raise_ref, kind))
+        back_ref[:, :, :width] = back.reshape(8, SEQS, width).astype(LOW)
+        raise_grad_ref[:, : kind.block, :part] = (
+            dot_tn(rows, low_grad).reshape(16, kind.block, part).astype(LOW)
+        )
+        whole[:part, :width] = dot_tn(active, grads)
+        core = lax.axis_index("dp") % 2
+        n = kind.reduce_rows
+        keep = pl.multiple_of(core * n, 64)
+        send = pl.multiple_of((1 - core) * n, 64)
+        reduce_keep_ref[:n, :width] = whole[pl.ds(keep, n), :width]
+        reduce_send_ref[:n, :width] = whole[pl.ds(send, n), :width].astype(LOW)
+
+    each_tower(run)
+
+
+def embed_kernel(part_ref, middle_ref, gat_ref, vec_ref, emb_ref, final_ref, pooled_ref, proj_ref):
+    def run(kind):
+        width = kind.width
+        final = (
+            middle_ref[:, :width]
+            + jnp.sum(part_ref[:, :, :width].astype(WIDE), axis=0)
+            + vector(vec_ref, kind, 7)
+        )
+        final_ref[:, :width] = final
+        hat, _ = standardise(final)
+        pooled = (hat * vector(vec_ref, kind, 8) + vector(vec_ref, kind, 9)).astype(LOW)
+        pooled_ref[:, :width] = pooled
+        proj = dot_nn(pooled, matrix(gat_ref, kind, AT_EMBED, EMB))
+        proj_ref[...] = proj
+        size = jnp.sum(proj * proj, axis=-1, keepdims=True) + 1e-06
+        emb_ref[...] = (proj * lax.rsqrt(size)).astype(LOW)
+
+    each_tower(run)
+
+
+def objective_kernel(
+    scale_ref,
+    all_ref,
+    valid_ref,
+    final_ref,
+    proj_ref,
+    gat_ref,
+    vec_ref,
+    low_ref,
+    grad_ref,
+    proj_grad_ref,
+    final_vec_ref,
+    sums_ref,
+    own_scr,
+):
+    def ordered(which):
+        blocks = []
+        for half in range(2):
+            for j in range(16):
+                rows = all_ref[j % 2, which * 8 + j // 2].astype(WIDE)
+                blocks.append(rows[half * 8 : half * 8 + 8])
+        return jnp.concatenate(blocks, axis=0).astype(LOW)
+
+    img, txt = ordered(0), ordered(1)
+    total = img.shape[0]
+    scale = jnp.exp(jnp.full((1, 1), scale_ref[0], WIDE))
+    allowed = valid_ref[...].reshape(total, total) > 0
+    same = lax.broadcasted_iota(jnp.int32, (total, total), 0) == lax.broadcasted_iota(
+        jnp.int32, (total, total), 1
+    )
+    same = same.astype(WIDE)
+
+    def side(left, right):
+        logits = scale * dot_nt(left, right)
+        masked = jnp.where(allowed, logits, -1e30)
+        top = jnp.max(masked, axis=1, keepdims=True)
+        lse = jnp.log(jnp.sum(jnp.exp(masked - top), axis=1, keepdims=True)) + top
+        terms = 0.5 * (jnp.where(allowed, jnp.exp(logits - lse), 0.0) - same)
+        loss = 0.5 * (
+            jnp.sum(lse, axis=0, keepdims=True)
+            - jnp.sum(jnp.sum(logits * same, axis=1, keepdims=True), axis=0, keepdims=True)
+        )
+        rate = jnp.sum(jnp.sum(terms * logits, axis=1, keepdims=True), axis=0, keepdims=True)
+        return (scale * terms).astype(LOW), loss, rate
+
+    row_back, row_loss, row_rate = side(img, txt)
+    col_back, col_loss, col_rate = side(txt, img)
+    row = lax.broadcasted_iota(jnp.int32, sums_ref.shape, 0)
+    sums_ref[...] = jnp.where(row == 0, row_loss + col_loss, row_rate + col_rate)
+
+    def run(kind):
+        width = kind.width
+        if kind.index == 0:
+            emb_grad = dot_nn(row_back, txt) + dot_tn(col_back, txt)
+        else:
+            emb_grad = dot_nn(col_back, img) + dot_tn(row_back, img)
+        own_scr[...] = emb_grad
+        at = lax.axis_index("dp")
+        mine = jnp.concatenate(
+            [
+                own_scr[pl.ds(pl.multiple_of(half * 128 + at * 8, 8), 8), :]
+                for half in range(2)
+            ],
+            axis=0,
+        )
+        proj = proj_ref[...]
+        size = jnp.sum(proj * proj, axis=-1, keepdims=True) + 1e-06
+        along = jnp.sum(proj * mine, axis=-1, keepdims=True)
+        proj_grad = ((mine - proj * along / size) * lax.rsqrt(size)).astype(LOW)
+        proj_grad_ref[...] = proj_grad
+        pooled_grad = dot_nt(proj_grad, matrix(gat_ref, kind, AT_EMBED, EMB))
+        hat, rate = standardise(final_ref[:, :width])
+        final_vec_ref[0:1, :width] = jnp.sum(pooled_grad * hat, axis=0, keepdims=True)
+        final_vec_ref[1:2, :width] = jnp.sum(pooled_grad, axis=0, keepdims=True)
+        final_grad = norm_back(pooled_grad, vector(vec_ref, kind, 8), hat, rate)
+        grad_ref[:, :width] = final_grad
+        low = final_grad.astype(LOW)
+        low_ref[:, :width] = low
+        final_vec_ref[2:3, :width] = jnp.sum(low.astype(WIDE), axis=0, keepdims=True)
+
+    each_tower(run)
+
+
+def attend_back_kernel(
+    ends_ref,
+    img_own,
+    img_in,
+    txt_own,
+    txt_in,
+    gat_ref,
+    vec_ref,
+    back_ref,
+    grad_ref,
+    middle_ref,
+    query_ref,
+    keyed_ref,
+    mixture_ref,
+    weight_ref,
+    mixed_ref,
+    first_ref,
+    pooled_ref,
+    proj_grad_ref,
+    final_vec_ref,
+    bias_ref,
+    img_keep,
+    txt_keep,
+    img_send,
+    txt_send,
+    factor_ref,
+    outer_ref,
+    rows_grad,
+    middle_scr,
+    query_back,
+    valued_scr,
+    shared_scr,
+    turned,
+    gains,
+):
+    def run(kind):
+        width, room, length = kind.width, kind.room, kind.length
+        gain, shift = vector(vec_ref, kind, 0), vector(vec_ref, kind, 1)
+        refs = (img_own, img_in) if kind.index == 0 else (txt_own, txt_in)
+        halves = sequence(kind, refs, 0)
+        keep, send = (img_keep, img_send) if kind.index == 0 else (txt_keep, txt_send)
+        mask = head_mask(kind)
+        positions = lax.broadcasted_iota(jnp.int32, (room, 1), 0)
+        at = lax.axis_index("dp")
+
+        second_grad = jnp.sum(back_ref[:, :, :width].astype(WIDE), axis=0)
+        hat, rate = standardise(middle_ref[:, :width])
+        middle_grad = grad_ref[:, :width] + norm_back(
+            second_grad, vector(vec_ref, kind, 5), hat, rate
+        )
+        middle_scr[:, :width] = middle_grad
+        output_grad = middle_grad.astype(LOW)
+        mixed_grad = dot_nt(output_grad, matrix(gat_ref, kind, AT_OUTPUT, width)).astype(LOW)
+        spread_grad = by_head(mixed_grad.astype(WIDE), mask)
+        constant = jnp.sum(spread_grad * vector(vec_ref, kind, 3), axis=-1, keepdims=True)
+        valued = dot_nt(
+            spread_grad.astype(LOW), matrix(gat_ref, kind, 2 * width, width)
+        ).astype(LOW)
+        valued_scr[:, :width] = valued
+        shared_scr[...] = jnp.broadcast_to(constant, (256, LANES))
+
+        def normal(half, i):
+            rows = halves[half][i].astype(WIDE)
+            hat, rate = standardise(rows)
+            return hat, rate
+
+        for half in range(2):
+
+            def through(i, carry):
+                s = half * 8 + i
+                start = pl.multiple_of(s * HEADS, HEADS)
+                span = pl.ds(start, HEADS)
+                hat, _ = normal(half, i)
+                first = (hat * gain + shift).astype(LOW)
+                weights = weight_ref[s, :, :room]
+                slope = dot_nt(valued_scr[span, :width], first) + shared_scr[span, 0:1]
+                slope = weights * (
+                    slope - jnp.sum(weights * slope, axis=-1, keepdims=True)
+                )
+                slope = slope.astype(LOW)
+                query_back[span, :width] = dot_nn(slope, first)
+                rows_grad[s, :room, :width] = dot_tn(slope, keyed_ref[span, :width]) + dot_tn(
+                    weights.astype(LOW), valued_scr[span, :width]
+                )
+                return carry
+
+            lax.fori_loop(0, 8, through, 0)
+
+        turns = query_back[:, :width].astype(LOW)
+        query_grad = from_heads(
+            dot_nn(turns, matrix(gat_ref, kind, width, width)) * 0.125, mask
+        ).astype(LOW)
+        top_grad = dot_nt(query_grad, matrix(gat_ref, kind, 0, width))
+        gains[...] = jnp.zeros_like(gains)
+        turned[:, :width] = top_grad
+
+        for half in range(2):
+            mine = half == kind.index
+
+            def finish(i, carry):
+                s = half * 8 + i
+                hat, rate = normal(half, i)
+                grad = rows_grad[s, :room, :width]
+                top = turned[pl.ds(s, 1), :width]
+                low = middle_scr[pl.ds(s, 1), :width]
+                if kind.causal:
+                    chosen = (positions == ends_ref[(half * 16 + at) * 8 + i]).astype(WIDE)
+                else:
+                    chosen = (positions == 0).astype(WIDE)
+                grad = grad + chosen * top
+                gains[0:1, :width] += jnp.sum(grad * hat, axis=0, keepdims=True)
+                gains[1:2, :width] += jnp.sum(grad, axis=0, keepdims=True)
+                result = norm_back(grad, gain, hat, rate) + chosen * low
+                if mine:
+                    keep[i] = result[:length]
+                else:
+                    send[i] = result.astype(LOW)
+                return carry
+
+            lax.fori_loop(0, 8, finish, 0)
+
+        factor_ref[:, 0:width] = query_ref[:, :width]
+        factor_ref[:, WIDTH : WIDTH + width] = mixed_grad
+        factor_ref[:, 2 * WIDTH : 2 * WIDTH + width] = query_grad
+        factor_ref[:, 3 * WIDTH : 3 * WIDTH + width] = output_grad
+        factor_ref[:, 4 * WIDTH : 4 * WIDTH + EMB] = proj_grad_ref[...]
+        start = 4 * WIDTH + EMB
+
+        def column_sum(value):
+            return jnp.sum(value.astype(WIDE), axis=0, keepdims=True)
+
+        totals = jnp.sum(
+            weight_ref[:, :, :room].astype(LOW).astype(WIDE), axis=-1, keepdims=True
+        ).reshape(SEQS * HEADS, 1)
+        lines = [
+            gains[0:1, :width],
+            gains[1:2, :width],
+            column_sum(query_grad),
+            column_sum(spread_grad * totals),
+            column_sum(output_grad),
+            column_sum(second_grad * hat),
+            column_sum(second_grad),
+            final_vec_ref[2:3, :width],
+            final_vec_ref[0:1, :width],
+            final_vec_ref[1:2, :width],
+            jnp.pad(bias_ref[0:1, : kind.part], ((0, 0), (0, width - kind.part))),
+            jnp.zeros((5, width), WIDE),
+        ]
+        factor_ref[:, start : start + width] = jnp.concatenate(lines, axis=0).astype(LOW)
+
+        slot = lax.broadcasted_iota(jnp.int32, (HEADS, 1), 0)
+
+        def in_slot(index, value):
+            chosen = (slot == index).astype(WIDE)
+            return (value.astype(WIDE)[:, None, :] * chosen[None]).reshape(SEQS * HEADS, width)
+
+        left = (
+            mixture_ref[:, :width].astype(WIDE)
+            + in_slot(12, first_ref[:, :width])
+            + in_slot(13, mixed_ref[:, :width])
+            + in_slot(14, pooled_ref[:, :width])
+        )
+        block = kind.block
+        outer_ref[:, :block, 0:256] = left.T.reshape(16, block, 256).astype(LOW)
+        outer_ref[:, :block, 256:512] = query_back[:, :width].T.reshape(16, block, 256).astype(LOW)
+
+    each_tower(run)
+
+
+def weigh_kernel(
+    outer_ref, factor_ref, raise_ref, keep_ref, sent_ref, img_ref, txt_ref, flat, acc, lines
+):
+    def run(kind):
+        width, block = kind.width, kind.block
+        mask = head_mask(kind)
+        slot = lax.broadcasted_iota(jnp.int32, (HEADS, 1), 0)
+        acc[...] = jnp.zeros_like(acc)
+        lines[...] = jnp.zeros_like(lines)
+
+        def in_slot(index, value):
+            chosen = (slot == index).astype(WIDE)
+            return (
+                (value.astype(WIDE)[:, None, :] * chosen[None])
+                .reshape(SEQS * HEADS, value.shape[1])
+                .astype(LOW)
+            )
+
+        def add(source, carry):
+            left = outer_ref[source, :block, 0:256]
+            turned = outer_ref[source, :block, 256:512]
+
+            def factor(k, wide):
+                return factor_ref[source, :, k * WIDTH : k * WIDTH + wide]
+
+            query = by_head(factor(0, width).astype(WIDE), mask).astype(LOW)
+            value = by_head(factor(1, width).astype(WIDE), mask).astype(LOW)
+            acc[:block, 0:width] += dot_nn(left, in_slot(12, factor(2, width)))
+            acc[:block, width : 2 * width] += dot_nn(turned, query) * 0.125
+            acc[:block, 2 * width : 3 * width] += dot_nn(left, value)
+            acc[:block, AT_OUTPUT : AT_OUTPUT + width] += dot_nn(left, in_slot(13, factor(3, width)))
+            acc[:block, AT_EMBED : AT_EMBED + EMB] += dot_nn(left, in_slot(14, factor(4, EMB)))
+            start = 4 * WIDTH + EMB
+            part = factor_ref[source, :, start : start + width].astype(WIDE)
+            lines[0:10, :width] += part[0:10]
+            chip = source // 2
+            piece = part[10:11, : kind.part]
+            other = jnp.zeros_like(piece)
+            both = jnp.where(
+                chip % 2 == 0,
+                jnp.concatenate([piece, other], axis=1),
+                jnp.concatenate([other, piece], axis=1),
+            )
+            rows = 2 * kind.part // width
+            lines[pl.ds(10 + chip // 2, 1), :width] += both
+            return carry
+
+        lax.fori_loop(0, 16, add, 0)
+
+        def drop(base, height, pitch, c, value):
+            flat[pl.ds(base + c, height, stride=pitch), :] = value
+
+        base = 0
+        for start, wide in ((0, 3 * width), (AT_OUTPUT, width)):
+            pitch = wide // LANES
+            for c in range(pitch):
+                lane = start + c * LANES
+                drop(base, block, pitch, c, acc[:block, lane : lane + LANES])
+            base += block * pitch
+        pitch = kind.hidden // LANES
+        per = kind.part // LANES
+        for c in range(pitch):
+            chip, lane = c // per, c % per * LANES
+            value = raise_ref[2 * chip, :block, lane : lane + LANES].astype(WIDE) + raise_ref[
+                2 * chip + 1, :block, lane : lane + LANES
+            ].astype(WIDE)
+            drop(base, block, pitch, c, value)
+        base += block * pitch
+        pitch = width // LANES
+        n = kind.reduce_rows
+        other_core = 1 - lax.axis_index("dp") % 2
+        for c in range(pitch):
+            lane = c * LANES
+            value = keep_ref[:n, lane : lane + LANES] + sent_ref[
+                other_core, :n, lane : lane + LANES
+            ].astype(WIDE)
+            drop(base, n, pitch, c, value)
+        base += n * pitch
+        pitch = EMB // LANES
+        for c in range(pitch):
+            lane = AT_EMBED + c * LANES
+            drop(base, block, pitch, c, acc[:block, lane : lane + LANES])
+        base += block * pitch
+        pitch = width // LANES
+        for c in range(pitch):
+            drop(base, 16, pitch, c, lines[:, c * LANES : (c + 1) * LANES])
+        ref = img_ref if kind.index == 0 else txt_ref
+        n, rows, lanes = ref.shape
+        ref[...] = flat[: n * rows, :].reshape(n, rows, lanes).astype(LOW)
+
+    each_tower(run)
+
+
+def compute(kernel, outs, scratch, scalars, *args):
+    like = jax.ShapeDtypeStruct
+    vmem = pl.BlockSpec(memory_space=pltpu.VMEM)
+    smem = pl.BlockSpec(memory_space=pltpu.SMEM)
+    return pl.pallas_call(
+        kernel,
+        out_shape=[like(shape, dtype) for shape, dtype in outs],
+        in_specs=[smem] * scalars + [vmem] * (len(args) - scalars),
+        out_specs=[vmem] * len(outs),
+        scratch_shapes=[pltpu.VMEM(shape, dtype) for shape, dtype in scratch],
+        compiler_params=pltpu.CompilerParams(vmem_limit_bytes=GRANT),
+    )(*args)
+
+
+def plans_for(img_share, txt_share):
+    return (
+        Plan(0, img_share, 96, (9, 3, 12, 12, 2)),
+        Plan(1, txt_share, 64, (6, 2, 8, 8, 2)),
+    )
+
+
+def to_chunks(flat, plan, me):
+    start = me * plan.share % plan.chunk
+    padded = jnp.pad(flat, (plan.chunk, plan.local * plan.chunk - plan.share))
+    piece = lax.dynamic_slice(padded, (plan.chunk - start,), (plan.local * plan.chunk,))
+    return piece.astype(LOW).reshape(plan.local, plan.rows, LANES)
+
+
+def from_chunks(chunks, plan, me):
+    start = me * plan.share % plan.chunk
+    return lax.dynamic_slice(chunks.reshape(-1), (start,), (plan.share,)).astype(WIDE)
+
+
+def step(
+    img_tokens,
+    txt_tokens,
+    txt_ends,
+    valid,
+    img_master,
+    img_moment,
+    img_average,
+    txt_master,
+    txt_moment,
+    txt_average,
+    scale_state,
+):
+    me = lax.axis_index(("tower", "dp"))
+    tower_at = lax.axis_index("tower")
+    is_image = tower_at == 0
+    plans = plans_for(img_master.shape[0], txt_master.shape[0])
+    img_rows = jnp.pad(img_tokens, ((0, 0), (0, TOWERS[0].room - TOWERS[0].length), (0, 0)))
+    txt_rows = jnp.pad(txt_tokens, ((0, 0), (0, TOWERS[1].room - TOWERS[1].length), (0, 0)))
+    img_slots, txt_slots, pairs = deal(
+        to_chunks(img_master, plans[0], me), to_chunks(txt_master, plans[1], me), valid, plans, 0
+    )
+    att, rise, fall, vec = compute(
+        place_kernel,
+        [
+            ((48, ATTENTION), LOW),
+            ((8, 48, PART), LOW),
+            ((192, WIDTH), LOW),
+            ((16, WIDTH), WIDE),
+        ],
+        [((39 * 96, LANES), WIDE)],
+        0,
+        img_slots,
+        txt_slots,
+    )
+    rise = jnp.repeat(rise, 2, axis=0)
+    gat, fall, img_in, txt_in, rise = exchange(att, fall, img_rows, txt_rows, [rise], 1)
+    second, middle, query, keyed, mixture, weights, mixed, tops = compute(
+        attend_kernel,
+        [
+            ((SEQS, WIDTH), LOW),
+            ((SEQS, WIDTH), WIDE),
+            ((SEQS, WIDTH), LOW),
+            ((256, WIDTH), LOW),
+            ((256, WIDTH), LOW),
+            ((SEQS, HEADS, LANES), WIDE),
+            ((SEQS, WIDTH), LOW),
+            ((SEQS, WIDTH), LOW),
+        ],
+        [((SEQS, ROOM, WIDTH), LOW), ((SEQS, WIDTH), WIDE), ((SEQS, WIDTH), WIDE)],
+        1,
+        txt_ends,
+        img_rows,
+        img_in,
+        txt_rows,
+        txt_in,
+        gat,
+        vec,
+    )
+    seconds = group_exchange(second, False, 2)
+    part, raised = compute(
+        hidden_kernel,
+        [((8, SEQS, WIDTH), LOW), ((128, PART), WIDE)],
+        [],
+        0,
+        seconds,
+        rise,
+        fall,
+        vec,
+    )
+    parts = group_exchange(part, True, 3)
+    emb, final, pooled, proj = compute(
+        embed_kernel,
+        [
+            ((SEQS, EMB), LOW),
+            ((SEQS, WIDTH), WIDE),
+            ((SEQS, WIDTH), LOW),
+            ((SEQS, EMB), WIDE),
+        ],
+        [],
+        0,
+        parts,
+        middle,
+        gat,
+        vec,
+    )
+    embs = spread(emb, 4)
+    low, final_grad, proj_grad, final_vec, sums = compute(
+        objective_kernel,
+        [
+            ((SEQS, WIDTH), LOW),
+            ((SEQS, WIDTH), WIDE),
+            ((SEQS, EMB), LOW),
+            ((8, WIDTH), WIDE),
+            ((8, LANES), WIDE),
+        ],
+        [((256, EMB), WIDE)],
+        1,
+        scale_state,
+        embs.reshape(2, 16, SEQS, EMB),
+        pairs,
+        final,
+        proj,
+        gat,
+        vec,
+    )
+    lows = group_exchange(low, False, 5)
+    back, rise_grad, fall_keep, fall_send, bias_grad = compute(
+        hidden_back_kernel,
+        [
+            ((8, SEQS, WIDTH), LOW),
+            ((16, 48, PART), LOW),
+            ((192, WIDTH), WIDE),
+            ((192, WIDTH), LOW),
+            ((8, PART), WIDE),
+        ],
+        [((PART, WIDTH), WIDE)],
+        0,
+        lows,
+        seconds,
+        raised,
+        rise,
+        fall,
+    )
+    backs = group_exchange(back, True, 6)
+    img_keep, txt_keep, img_send, txt_send, factor, outer = compute(
+        attend_back_kernel,
+        [
+            ((8, TOWERS[0].length, D_IMG), WIDE),
+            ((8, TOWERS[1].length, D_TXT), WIDE),
+            (img_rows.shape, LOW),
+            (txt_rows.shape, LOW),
+            ((SEQS, 5 * WIDTH + EMB), LOW),
+            ((16, 48, 512), LOW),
+        ],
+        [
+            ((SEQS, ROOM, WIDTH), WIDE),
+            ((SEQS, WIDTH), WIDE),
+            ((256, WIDTH), WIDE),
+            ((256, WIDTH), LOW),
+            ((256, LANES), WIDE),
+            ((SEQS, WIDTH), WIDE),
+            ((8, WIDTH), WIDE),
+        ],
+        1,
+        txt_ends,
+        img_rows,
+        img_in,
+        txt_rows,
+        txt_in,
+        gat,
+        vec,
+        backs,
+        final_grad,
+        middle,
+        query,
+        keyed,
+        mixture,
+        weights,
+        mixed,
+        tops,
+        pooled,
+        proj_grad,
+        final_vec,
+        bias_grad,
+    )
+    factors, falls, txt_home, img_home, outers, rises = exchange(
+        factor, fall_send, txt_send, img_send, [outer, rise_grad], 7
+    )
+    img_slots, txt_slots = compute(
+        weigh_kernel,
+        [(img_slots.shape, LOW), (txt_slots.shape, LOW)],
+        [((39 * 96, LANES), WIDE), ((48, ATTENTION), WIDE), ((16, WIDTH), WIDE)],
+        0,
+        outers,
+        factors,
+        rises,
+        fall_keep,
+        falls,
+    )
+    img_chunks, txt_chunks = collect(img_slots, txt_slots, plans, 8)
+    img_grad = jnp.where(is_image, img_keep, img_home[:, : TOWERS[0].length].astype(WIDE))
+    txt_grad = jnp.where(is_image, txt_home[:, : TOWERS[1].length].astype(WIDE), txt_keep)
+    img_new = advance(
+        img_master, img_moment, img_average, from_chunks(img_chunks, plans[0], me), step_rate
+    )
+    txt_new = advance(
+        txt_master, txt_moment, txt_average, from_chunks(txt_chunks, plans[1], me), step_rate
+    )
+    scale_parts = advance(
+        scale_state[0], scale_state[1], scale_state[2], sums[1, 0], scale_rate
+    )
+    return (
+        sums[0, 0] / 256,
+        img_grad,
+        txt_grad,
+        img_new[0],
+        img_new[1],
+        img_new[2],
+        img_new[0].astype(LOW),
+        txt_new[0],
+        txt_new[1],
+        txt_new[2],
+        txt_new[0].astype(LOW),
+        jnp.stack(scale_parts),
+    )
 
 
 def from_partner(value, axis, stride):
@@ -386,4 +1914,5 @@
         P(("tower", "dp")),
         P(),
     )
-    return jax.shard_map(body, mesh=mesh, in_specs=in_specs, out_specs=out_specs, check_vma=False)
+    run = step if (mesh.shape["tower"], mesh.shape["dp"]) == (2, 16) else body
+    return jax.shard_map(run, mesh=mesh, in_specs=in_specs, out_specs=out_specs, check_vma=False)

time: 1940 us -> 312 us (0.16); the launches traced: 1920 us -> 311 us
  waiting for transfers between devices: 839 us -> 0 us
  local copies, waits for them, and re-layouts: 533 us -> 14.5 us
  Pallas kernels: 0 us -> 283 us
  matrix products: 125 us -> 0 us
  blocking collectives: 124 us -> 0 us
  other arithmetic: 124 us -> 7.89 us
  starting transfers between devices: 114 us -> 0 us
  loops' own time: 35.6 us -> 0 us
    unnamed x5 -> x0, waiting for transfers between devices: 457 us -> none
    pallas_call x0 -> x17, Pallas kernels: none -> 283 us  [the longest x2 99.1 us: exchange(): pl.pallas_call(functools.partial(exchange_kernel, count), out_shape=[like...]
    reduce_scatter x2 -> x0, waiting for transfers between devices: 257 us -> none  [the longest x1 132 us: body(): lax.psum_scatter(across(row_back, img_local), ('tower', 'dp'), scatter_di...]
    reshape x23 -> x0, local copies, waits for them, and re-layouts: 155 us -> none  [the longest x2 63.8 us: text_weights(): whole.reshape(2, tower_count, shard_room)[:, :, :txt_share].reshape(-1)]
    cond x101 -> x0, local copies, waits for them, and re-layouts: 155 us -> none
    dot_general x34 -> x0, matrix products: 125 us -> none  [the longest x20 89.4 us: product(): return jnp.matmul(left, right)]
    all_gather x1 -> x0, waiting for transfers between devices: 116 us -> none  [body(): gathered = lax.all_gather(stacked, 'dp', axis=1, tiled=True)]
    ppermute x6 -> x0, starting transfers between devices: 113 us -> none  [from_partner(): return lax.ppermute(value, axis, pairs)]
  transfers between devices with their start and end apart: 10 -> 0, of which waited for: 7 -> 0; matrix products, arithmetic and copies ran while one was open for 7% -> 0% of each run, Pallas kernels for 0% -> 0%
where the time goes in v1:
time: 312 us; the launch traced here: 311 us
  Pallas kernels  283 us (91%)
  local copies, waits for them, and re-layouts  14.5 us (5%)
  other arithmetic  7.89 us (3%)
  between operations  5.95 us (2%)
    pallas_call x2, Pallas kernels, exchange(): pl.pallas_call(functools.partial(exchange_kernel, count), out_shape=[like...  99.1 us
    pallas_call x8, Pallas kernels, compute(): pl.pallas_call(kernel, out_shape=[like(shape, dtype) for shape, dtype in...  65.6 us
    pallas_call x1, Pallas kernels, collect(): pl.pallas_call(functools.partial(collect_kernel, plans), out_shape=[like(...  38.9 us
    pallas_call x1, Pallas kernels, deal(): pl.pallas_call(functools.partial(deal_kernel, plans), out_shape=[like((pl...  35.6 us
    pallas_call x4, Pallas kernels, group_exchange(): pl.pallas_call(functools.partial(group_kernel, scattered), out_shape=jax....  29.1 us
    pallas_call x1, Pallas kernels, spread(): pl.pallas_call(spread_kernel, out_shape=jax.ShapeDtypeStruct((2, 16, *val...  14.7 us

profile of v1, /device:TPU:3, one launch (start us, length us, event | category | flops | bytes accessed | tf_op | source)
XLA Modules:
  0.0 311.3 jit_solution(9130927860900276847)
XLA Ops:
  0.7 1.4 fusion.11
  2.8 1.9 fusion.3
  4.7 2.4 fusion
  7.3 0.9 pad.19.refs_3_.txt_own
  8.3 0.9 pad.16.refs_2_.img_own
  9.2 35.6 %shard_map.202 = (bf16[39,96,128]{2,1,0:T(8,128)(2,1)}, bf16[27,64,128]{2,1,0:T(8,128)(2,1)}, s32[32,8,256]{2,1,0:T(8,128)}) custom-call(bf16[20,96,128]{2,1,0:T(8,128)(2,1)} %bitcast.14, bf16[14,64,128]{2,1,0:T(8,128)(2,1)} %bitcast.15, s32[8,256]{1,0:T(8,128)} %refs_2_.1), custom_call_target="tpu_custom_call" | custom-call | tf_op jit(solution)/shard_map/pallas_call | solution.py:515
  44.8 2.4 shard_map.203
  47.3 1.8 broadcast_in_dim.3
  49.1 52.4 %shard_map.204 = (bf16[16,48,3584]{2,1,0:T(8,128)(2,1)}, bf16[2,192,768]{2,1,0:T(8,128)(2,1)}, bf16[8,64,768]{2,1,0:T(8,128)(2,1)}, bf16[8,80,512]{2,1,0:T(8,128)(2,1)}, bf16[16,48,384]{2,1,0:T(8,128)(2,1)}) custom-call(bf16[48,3584]{1,0:T(8,128)(2,1)} %get-tuple-element.66.refs_0_, bf16[192,768]{1,0:T(8,128)(2,1)} %get-tuple-element.67.refs_1_, ...), custom_call_target="tpu_custom_call" | custom-call | tf_op jit(solution)/shard_map/pallas_call | solution.py:308
  101.5 16.3 %shard_map.205 = (bf16[16,768]{1,0:T(8,128)(2,1)}, f32[16,768]{1,0:T(8,128)}, bf16[16,768]{1,0:T(8,128)(2,1)}, bf16[256,768]{1,0:T(8,128)(2,1)}, bf16[256,768]{1...) custom-call(s32[256]{0:T(256)} %ends_ref.3, ...), custom_call_target="tpu_custom_call" | custom-call | tf_op jit(solution)/shard_map/pallas_call | solution.py:1313
  117.8 7.6 %shard_map.206.second_ref = bf16[8,16,768]{2,1,0:T(8,128)(2,1)} custom-call(bf16[16,768]{1,0:T(8,128)(2,1)} %get-tuple-element.73.x_ref), custom_call_target="tpu_custom_call" | custom-call | tf_op jit(solution)/shard_map/pallas_call | solution.py:93
  125.4 2.4 shard_map.207
  127.8 6.4 %shard_map.208.part_ref = bf16[8,16,768]{2,1,0:T(8,128)(2,1)} custom-call(bf16[8,16,768]{2,1,0:T(8,128)(2,1)} %get-tuple-element.76.x_ref), custom_call_target="tpu_custom_call" | custom-call | tf_op jit(solution)/shard_map/pallas_call | solution.py:93
  134.2 3.8 %shard_map.209 = (bf16[16,512]{1,0:T(8,128)(2,1)}, f32[16,768]{1,0:T(8,128)}, bf16[16,768]{1,0:T(8,128)(2,1)}, f32[16,512]{1,0:T(8,128)}) custom-call(bf16[8,16,768]{2,1,0:T(8,128)(2,1)} %shard_map.208.part_ref, f32[16,768]{1,0:T(8,128)} %get-tuple-element.77.middle_ref, bf16[16,48,3584]{2,1,0:T(8,128)(2,1)} %get-tuple-element.71.gat_ref, ...), custom_call_target="tpu_custom_call" | custom-call | tf_op jit(solution)/shard_map/pallas_call | solution.py:1313
  138.0 14.7 %shard_map.210.all_ref = bf16[2,16,16,512]{3,2,1,0:T(8,128)(2,1)} custom-call(bf16[16,512]{1,0:T(8,128)(2,1)} %get-tuple-element.78.x_ref), custom_call_target="tpu_custom_call" | custom-call | tf_op jit(solution)/shard_map/pallas_call | solution.py:142
  152.7 5.0 %shard_map.211 = (bf16[16,768]{1,0:T(8,128)(2,1)}, f32[16,768]{1,0:T(8,128)}, bf16[16,512]{1,0:T(8,128)(2,1)}, f32[8,768]{1,0:T(8,128)}, f32[8,128]{1,0:T(8,128)}) custom-call(f32[3]{0:T(128)} %scale_ref.1, bf16[2,16,16,512]{3,2,1,0:T(8,128)(2,1)} %shard_map.210.all_ref, s32[32,8,256]{2,1,0:T(8,128)} %get-tuple-element.79.valid_ref, ...), custom_call_target="tpu_custom_call" | custom-call | tf_op jit(solution)/shard_map/pallas_call | solution.py:1313
  157.7 1.3 fusion.10
  162.3 0.6 pad_maximum_fusion
  162.8 7.5 %shard_map.212.grad_ref = bf16[8,16,768]{2,1,0:T(8,128)(2,1)} custom-call(bf16[16,768]{1,0:T(8,128)(2,1)} %get-tuple-element.83.x_ref), custom_call_target="tpu_custom_call" | custom-call | tf_op jit(solution)/shard_map/pallas_call | solution.py:93
  170.3 3.3 %shard_map.213 = (bf16[8,16,768]{2,1,0:T(8,128)(2,1)}, bf16[16,48,384]{2,1,0:T(8,128)(2,1)}, f32[192,768]{1,0:T(8,128)}, bf16[192,768]{1,0:T(8,128)(2,1)}, f32[8,384]{1,0:T(8,128)}) custom-call(bf16[8,16,768]{2,1,0:T(8,128)(2,1)} %shard_map.212.grad_ref, bf16[8,16,768]{2,1,0:T(8,128)(2,1)} %shard_map.206.second_ref, ...), custom_call_target="tpu_custom_call" | custom-call | tf_op jit(solution)/shard_map/pallas_call | solution.py:1313
  173.7 7.6 %shard_map.214.back_ref = bf16[8,16,768]{2,1,0:T(8,128)(2,1)} custom-call(bf16[8,16,768]{2,1,0:T(8,128)(2,1)} %get-tuple-element.85.x_ref), custom_call_target="tpu_custom_call" | custom-call | tf_op jit(solution)/shard_map/pallas_call | solution.py:93
  181.3 22.5 %shard_map.215 = (f32[8,50,768]{2,1,0:T(8,128)}, f32[8,77,512]{2,1,0:T(8,128)}, bf16[8,64,768]{2,1,0:T(8,128)(2,1)}, bf16[8,80,512]{2,1,0:T(8,128)(2,1)}, bf16[1...) custom-call(s32[256]{0:T(256)} %ends_ref.3, bf16[8,64,768]{2,1,0:T(8,128)(2,1)} %pad.16.refs_2_.img_own, ...), custom_call_target="tpu_custom_call" | custom-call | tf_op jit(solution)/shard_map/pallas_call | solution.py:1313
  203.8 46.7 %shard_map.216 = (bf16[16,16,4352]{2,1,0:T(8,128)(2,1)}, bf16[2,192,768]{2,1,0:T(8,128)(2,1)}, bf16[8,80,512]{2,1,0:T(8,128)(2,1)}, bf16[8,64,768]{2,1,0:T(8,128...) custom-call(bf16[16,4352]{1,0:T(8,128)(2,1)} %get-tuple-element.98.refs_0_, ...), custom_call_target="tpu_custom_call" | custom-call | tf_op jit(solution)/shard_map/pallas_call | solution.py:308
  250.6 1.4 convert_select_fusion
  252.5 1.4 copy.25
  253.9 1.8 copy.26
  255.7 9.7 %shard_map.217 = (bf16[39,96,128]{2,1,0:T(8,128)(2,1)}, bf16[27,64,128]{2,1,0:T(8,128)(2,1)}) custom-call(bf16[16,48,512]{2,1,0:T(8,128)(2,1)} %get-tuple-element.107.outer_ref, bf16[16,16,4352]{2,1,0:T(8,128)(2,1)} %get-tuple-element.108.factor_ref, bf16[16,48,384]{2,1,0:T(8,128)(2,1)} %get-tuple-element.109.raise_ref, ...), custom_call_target="tpu_custom_call" | custom-call | tf_op jit(solution)/shard_map/pallas_call | solution.py:1313
  265.4 38.9 %shard_map.218 = (bf16[20,96,128]{2,1,0:T(8,128)(2,1)}, bf16[14,64,128]{2,1,0:T(8,128)(2,1)}) custom-call(bf16[39,96,128]{2,1,0:T(8,128)(2,1)} %get-tuple-element.112.refs_0_, bf16[27,64,128]{2,1,0:T(8,128)(2,1)} %get-tuple-element.113.refs_1_), custom_call_target="tpu_custom_call" | custom-call | tf_op jit(solution)/shard_map/pallas_call | solution.py:616
  304.4 2.1 fusion.6
  306.5 0.9 add_multiply_fusion.1
  307.4 1.5 fusion.8
  308.9 1.2 add_multiply_fusion
  (31 shorter events, 0.9 us)
Async XLA Ops:
  0.6 6.4 %copy-start.9 = (bf16[8,77,512]{2,0,1:T(8,128)(2,1)S(1)}, bf16[8,77,512]{2,0,1:T(8,128)(2,1)}, u32[]{:S(2)}) copy-start(bf16[8,77,512]{2,0,1:T(8,128)(2,1)} %param.12) | copy-start | bytes 1892356
  7.1 1.1 copy-start.10
  203.8 46.7 %copy-start.4 = (f32[8,50,768]{2,1,0:T(8,128)S(1)}, f32[8,50,768]{2,1,0:T(8,128)}, u32[]{:S(2)}) copy-start(f32[8,50,768]{2,1,0:T(8,128)} %get-tuple-element.97) | copy-start | bytes 3686404
  250.6 1.5 copy-start.5
  250.6 1.7 copy-start.8
  265.4 38.9 %copy-start.3 = (f32[106720]{0:T(1024)S(1)}, f32[106720]{0:T(1024)}, u32[]{:S(2)}) copy-start(f32[106720]{0:T(1024)} %param.18) | copy-start | bytes 1280644
  265.4 38.9 %copy-start.13 = (f32[106720]{0:T(1024)S(1)}, f32[106720]{0:T(1024)}, u32[]{:S(2)}) copy-start(f32[106720]{0:T(1024)} %param.19) | copy-start | bytes 1280644
  304.3 2.2 copy-start.12
  304.3 3.1 copy-start
  304.3 3.0 copy-start.6
  304.3 3.0 copy-start.11
  306.5 2.4 copy-start.2
  307.4 1.5 copy-start.7
  308.9 1.2 copy-start.1

commit v2 on v1

--- a/solution.py
+++ b/solution.py
@@ -56,102 +56,69 @@
     )
 
 
-def group_kernel(scattered, x_ref, o_ref, send_sem, recv_sem, own_sem):
+def same_core(tower, at):
+    chip, core = at // 2, at % 2
+    return [(tower, (chip + k) % 8 * 2 + core) for k in range(1, 8)]
+
+
+def both_towers(tower, at):
+    place, core = tower * 8 + at // 2, at % 2
+    others = [(place + k) % 16 for k in range(1, 16)]
+    return [(other // 8, other % 8 * 2 + core) for other in others]
+
+
+def group_exchange(scattered, x_ref, o_ref, send_sem, recv_sem):
     tower, at = here()
-    chip, core = at // 2, at % 2
-    others = [(chip + k) % 8 for k in range(1, 8)]
-    greet([(tower, other * 2 + core) for other in others])
-    own = pltpu.make_async_copy(x_ref.at[chip] if scattered else x_ref, o_ref.at[chip], own_sem)
-    own.start()
+    chip = at // 2
+
+    def source(k):
+        return x_ref.at[k] if scattered else x_ref
+
+    own = pltpu.make_async_copy(source(chip), o_ref.at[chip], send_sem.at[7])
     sent = []
-    for k, other in enumerate(others):
+    for k, device in enumerate(same_core(tower, at)):
         copy = remote(
-            x_ref.at[other] if scattered else x_ref,
-            o_ref.at[chip],
-            send_sem.at[k],
-            recv_sem.at[k],
-            (tower, other * 2 + core),
+            source((chip + 1 + k) % 8), o_ref.at[chip], send_sem.at[k], recv_sem.at[k], device
         )
         copy.start()
         sent.append(copy)
+    own.start()
     own.wait()
-    for k, copy in enumerate(sent):
-        copy.wait_send()
-        source = (chip + 7 - k) % 8
+    for k in range(7):
         remote(
-            x_ref.at[chip] if scattered else x_ref,
-            o_ref.at[source],
+            source(chip),
+            o_ref.at[(chip + 7 - k) % 8],
             send_sem.at[k],
             recv_sem.at[k],
             (tower, at),
         ).wait_recv()
-
-
-def group_exchange(value, scattered, number, space=pl.ANY):
-    block = value.shape[1:] if scattered else value.shape
-    spec = pl.BlockSpec(memory_space=space)
-    return pl.pallas_call(
-        functools.partial(group_kernel, scattered),
-        out_shape=jax.ShapeDtypeStruct((8, *block), value.dtype),
-        in_specs=[spec],
-        out_specs=spec,
-        scratch_shapes=[
-            pltpu.SemaphoreType.DMA((7,)),
-            pltpu.SemaphoreType.DMA((7,)),
-            pltpu.SemaphoreType.DMA,
-        ],
-        compiler_params=comm_params(number),
-    )(value)
-
-
-def spread_kernel(x_ref, o_ref, send_sem, recv_sem, own_sem, core_sems):
+    return sent
+
+
+def spread(x_ref, o_ref, send_sem, recv_sem, core_sems):
     tower, at = here()
     chip, core = at // 2, at % 2
     place = tower * 8 + chip
-    others = [(place + k) % 16 for k in range(1, 16)]
-    homes = [(other // 8, (other % 8) * 2 + core) for other in others]
     sibling = (tower, chip * 2 + 1 - core)
-    greet([*homes, sibling])
-    own = pltpu.make_async_copy(x_ref, o_ref.at[core, place], own_sem)
-    own.start()
     sent = []
-    for k, home in enumerate(homes):
-        copy = remote(
-            x_ref, o_ref.at[core, place], send_sem.at[k], recv_sem.at[k], home
-        )
+    for k, device in enumerate(both_towers(tower, at)):
+        copy = remote(x_ref, o_ref.at[core, place], send_sem.at[k], recv_sem.at[k], device)
         copy.start()
         sent.append(copy)
+    own = pltpu.make_async_copy(x_ref, o_ref.at[core, place], send_sem.at[15])
+    own.start()
     own.wait()
-    for k, copy in enumerate(sent):
-        source = (place + 15 - k) % 16
+    for k in range(15):
         remote(
-            x_ref, o_ref.at[core, source], send_sem.at[k], recv_sem.at[k], sibling
+            x_ref, o_ref.at[core, (place + 15 - k) % 16], send_sem.at[k], recv_sem.at[k], sibling
         ).wait_recv()
     across = remote(o_ref.at[core], o_ref.at[core], core_sems.at[0], core_sems.at[1], sibling)
     across.start()
-    for copy in sent:
-        copy.wait_send()
-    across.wait_send()
+    sent.append(across)
     remote(
         o_ref.at[1 - core], o_ref.at[1 - core], core_sems.at[0], core_sems.at[1], sibling
     ).wait_recv()
-
-
-def spread(value, number, space=pl.ANY):
-    spec = pl.BlockSpec(memory_space=space)
-    return pl.pallas_call(
-        spread_kernel,
-        out_shape=jax.ShapeDtypeStruct((2, 16, *value.shape), value.dtype),
-        in_specs=[spec],
-        out_specs=spec,
-        scratch_shapes=[
-            pltpu.SemaphoreType.DMA((15,)),
-            pltpu.SemaphoreType.DMA((15,)),
-            pltpu.SemaphoreType.DMA,
-            pltpu.SemaphoreType.DMA((2,)),
-        ],
-        compiler_params=comm_params(number),
-    )(value)
+    return sent
 
 
 def exchange_kernel(count, *refs):
@@ -953,7 +920,7 @@
         hat, _ = standardise(final)
         pooled = (hat * vector(vec_ref, kind, 8) + vector(vec_ref, kind, 9)).astype(LOW)
         pooled_ref[:, :width] = pooled
-        proj = dot_nn(pooled, matrix(gat_ref, kind, AT_EMBED, EMB))
+        proj = dot_nn(pooled, matrix(gat_ref, kind, 0, EMB))
         proj_ref[...] = proj
         size = jnp.sum(proj * proj, axis=-1, keepdims=True) + 1e-06
         emb_ref[...] = (proj * lax.rsqrt(size)).astype(LOW)
@@ -973,7 +940,8 @@
     grad_ref,
     proj_grad_ref,
     final_vec_ref,
-    sums_ref,
+    loss_ref,
+    scale_new_ref,
     own_scr,
 ):
     def ordered(which):
@@ -1008,8 +976,12 @@
 
     row_back, row_loss, row_rate = side(img, txt)
     col_back, col_loss, col_rate = side(txt, img)
-    row = lax.broadcasted_iota(jnp.int32, sums_ref.shape, 0)
-    sums_ref[...] = jnp.where(row == 0, row_loss + col_loss, row_rate + col_rate)
+    loss_ref[0] = jnp.sum(row_loss + col_loss) / total
+    parts = advance(
+        scale_ref[0], scale_ref[1], scale_ref[2], jnp.sum(row_rate + col_rate), scale_rate
+    )
+    for k in range(3):
+        scale_new_ref[k] = parts[k]
 
     def run(kind):
         width = kind.width
@@ -1031,7 +1003,7 @@
         along = jnp.sum(proj * mine, axis=-1, keepdims=True)
         proj_grad = ((mine - proj * along / size) * lax.rsqrt(size)).astype(LOW)
         proj_grad_ref[...] = proj_grad
-        pooled_grad = dot_nt(proj_grad, matrix(gat_ref, kind, AT_EMBED, EMB))
+        pooled_grad = dot_nt(proj_grad, matrix(gat_ref, kind, 0, EMB))
         hat, rate = standardise(final_ref[:, :width])
         final_vec_ref[0:1, :width] = jnp.sum(pooled_grad * hat, axis=0, keepdims=True)
         final_vec_ref[1:2, :width] = jnp.sum(pooled_grad, axis=0, keepdims=True)
@@ -1042,6 +1014,95 @@
         final_vec_ref[2:3, :width] = jnp.sum(low.astype(WIDE), axis=0, keepdims=True)
 
     each_tower(run)
+
+
+def centre_kernel(
+    scale_ref,
+    second_ref,
+    middle_ref,
+    gat_ref,
+    vec_ref,
+    raise_ref,
+    reduce_ref,
+    valid_ref,
+    loss_ref,
+    scale_new_ref,
+    final_grad_ref,
+    pooled_ref,
+    proj_grad_ref,
+    final_vec_ref,
+    raise_grad_ref,
+    reduce_keep_ref,
+    reduce_send_ref,
+    bias_ref,
+    backs_ref,
+    emb_weight_ref,
+    seconds,
+    part,
+    parts,
+    raised,
+    emb,
+    embs,
+    final,
+    proj,
+    low,
+    lows,
+    back,
+    own_scr,
+    whole,
+    send_sems,
+    recv_sems,
+    spread_send,
+    spread_recv,
+    core_sems,
+    fetch_sem,
+):
+    tower, at = here()
+    fetch = pltpu.make_async_copy(
+        gat_ref.at[:, :, pl.ds(AT_EMBED, EMB)], emb_weight_ref, fetch_sem
+    )
+    fetch.start()
+    greet([*both_towers(tower, at), (tower, at + 1 - at % 2 * 2)])
+    sent = []
+    sent += group_exchange(False, second_ref, seconds, send_sems.at[0], recv_sems.at[0])
+    hidden_kernel(seconds, raise_ref, reduce_ref, vec_ref, part, raised)
+    sent += group_exchange(True, part, parts, send_sems.at[1], recv_sems.at[1])
+    fetch.wait()
+    embed_kernel(parts, middle_ref, emb_weight_ref, vec_ref, emb, final, pooled_ref, proj)
+    sent += spread(emb, embs, spread_send, spread_recv, core_sems)
+    objective_kernel(
+        scale_ref,
+        embs,
+        valid_ref,
+        final,
+        proj,
+        emb_weight_ref,
+        vec_ref,
+        low,
+        final_grad_ref,
+        proj_grad_ref,
+        final_vec_ref,
+        loss_ref,
+        scale_new_ref,
+        own_scr,
+    )
+    sent += group_exchange(False, low, lows, send_sems.at[2], recv_sems.at[2])
+    hidden_back_kernel(
+        lows,
+        seconds,
+        raised,
+        raise_ref,
+        reduce_ref,
+        back,
+        raise_grad_ref,
+        reduce_keep_ref,
+        reduce_send_ref,
+        bias_ref,
+        whole,
+    )
+    sent += group_exchange(True, back, backs_ref, send_sems.at[3], recv_sems.at[3])
+    for copy in sent:
+        copy.wait_send()
 
 
 def attend_back_kernel(
@@ -1320,6 +1381,57 @@
     )(*args)
 
 
+def centre(scale_state, second, middle, gat, vec, rise, fall, pairs, number):
+    like = jax.ShapeDtypeStruct
+    vmem = pl.BlockSpec(memory_space=pltpu.VMEM)
+    smem = pl.BlockSpec(memory_space=pltpu.SMEM)
+    group = ((8, SEQS, WIDTH), LOW)
+    rows_low, rows_wide = ((SEQS, WIDTH), LOW), ((SEQS, WIDTH), WIDE)
+    outs = [
+        rows_wide,
+        rows_low,
+        ((SEQS, EMB), LOW),
+        ((8, WIDTH), WIDE),
+        ((16, 48, PART), LOW),
+        ((192, WIDTH), WIDE),
+        ((192, WIDTH), LOW),
+        ((8, PART), WIDE),
+        group,
+    ]
+    scratch = [
+        ((16, 48, EMB), LOW),
+        group,
+        group,
+        group,
+        ((128, PART), WIDE),
+        ((SEQS, EMB), LOW),
+        ((2, 16, SEQS, EMB), LOW),
+        rows_wide,
+        ((SEQS, EMB), WIDE),
+        rows_low,
+        group,
+        group,
+        ((256, EMB), WIDE),
+        ((PART, WIDTH), WIDE),
+    ]
+    return pl.pallas_call(
+        centre_kernel,
+        out_shape=[like((1,), WIDE), like((3,), WIDE)] + [like(*out) for out in outs],
+        in_specs=[smem, vmem, vmem, ANY] + [vmem] * 4,
+        out_specs=[smem, smem] + [vmem] * len(outs),
+        scratch_shapes=[pltpu.VMEM(*each) for each in scratch]
+        + [
+            pltpu.SemaphoreType.DMA((4, 8)),
+            pltpu.SemaphoreType.DMA((4, 7)),
+            pltpu.SemaphoreType.DMA((16,)),
+            pltpu.SemaphoreType.DMA((15,)),
+            pltpu.SemaphoreType.DMA((2,)),
+            pltpu.SemaphoreType.DMA,
+        ],
+        compiler_params=comm_params(number),
+    )(scale_state, second, middle, gat, vec, rise, fall, pairs)
+
+
 def plans_for(img_share, txt_share):
     return (
         Plan(0, img_share, 96, (9, 3, 12, 12, 2)),
@@ -1398,72 +1510,19 @@
         gat,
         vec,
     )
-    seconds = group_exchange(second, False, 2)
-    part, raised = compute(
-        hidden_kernel,
-        [((8, SEQS, WIDTH), LOW), ((128, PART), WIDE)],
-        [],
-        0,
-        seconds,
-        rise,
-        fall,
-        vec,
-    )
-    parts = group_exchange(part, True, 3)
-    emb, final, pooled, proj = compute(
-        embed_kernel,
-        [
-            ((SEQS, EMB), LOW),
-            ((SEQS, WIDTH), WIDE),
-            ((SEQS, WIDTH), LOW),
-            ((SEQS, EMB), WIDE),
-        ],
-        [],
-        0,
-        parts,
-        middle,
-        gat,
-        vec,
-    )
-    embs = spread(emb, 4)
-    low, final_grad, proj_grad, final_vec, sums = compute(
-        objective_kernel,
-        [
-            ((SEQS, WIDTH), LOW),
-            ((SEQS, WIDTH), WIDE),
-            ((SEQS, EMB), LOW),
-            ((8, WIDTH), WIDE),
-            ((8, LANES), WIDE),
-        ],
-        [((256, EMB), WIDE)],
-        1,
-        scale_state,
-        embs.reshape(2, 16, SEQS, EMB),
-        pairs,
-        final,
-        proj,
-        gat,
-        vec,
-    )
-    lows = group_exchange(low, False, 5)
-    back, rise_grad, fall_keep, fall_send, bias_grad = compute(
-        hidden_back_kernel,
-        [
-            ((8, SEQS, WIDTH), LOW),
-            ((16, 48, PART), LOW),
-            ((192, WIDTH), WIDE),
-            ((192, WIDTH), LOW),
-            ((8, PART), WIDE),
-        ],
-        [((PART, WIDTH), WIDE)],
-        0,
-        lows,
-        seconds,
-        raised,
-        rise,
-        fall,
-    )
-    backs = group_exchange(back, True, 6)
+    (
+        loss,
+        scale_new,
+        final_grad,
+        pooled,
+        proj_grad,
+        final_vec,
+        rise_grad,
+        fall_keep,
+        fall_send,
+        bias_grad,
+        backs,
+    ) = centre(scale_state, second, middle, gat, vec, rise, fall, pairs, 2)
     img_keep, txt_keep, img_send, txt_send, factor, outer = compute(
         attend_back_kernel,
         [
@@ -1506,7 +1565,7 @@
         bias_grad,
     )
     factors, falls, txt_home, img_home, outers, rises = exchange(
-        factor, fall_send, txt_send, img_send, [outer, rise_grad], 7
+        factor, fall_send, txt_send, img_send, [outer, rise_grad], 3
     )
     img_slots, txt_slots = compute(
         weigh_kernel,
@@ -1519,7 +1578,7 @@
         fall_keep,
         falls,
     )
-    img_chunks, txt_chunks = collect(img_slots, txt_slots, plans, 8)
+    img_chunks, txt_chunks = collect(img_slots, txt_slots, plans, 4)
     img_grad = jnp.where(is_image, img_keep, img_home[:, : TOWERS[0].length].astype(WIDE))
     txt_grad = jnp.where(is_image, txt_home[:, : TOWERS[1].length].astype(WIDE), txt_keep)
     img_new = advance(
@@ -1528,11 +1587,8 @@
     txt_new = advance(
         txt_master, txt_moment, txt_average, from_chunks(txt_chunks, plans[1], me), step_rate
     )
-    scale_parts = advance(
-        scale_state[0], scale_state[1], scale_state[2], sums[1, 0], scale_rate
-    )
     return (
-        sums[0, 0] / 256,
+        loss[0],
         img_grad,
         txt_grad,
         img_new[0],
@@ -1543,7 +1599,7 @@
         txt_new[1],
         txt_new[2],
         txt_new[0].astype(LOW),
-        jnp.stack(scale_parts),
+        scale_new,
     )
 
 

time: 312 us -> 283 us (0.907)
  Pallas kernels: 283 us -> 260 us
  between operations: 5.95 us -> 2.69 us
    pallas_call x8 -> x4, Pallas kernels: 65.6 us -> 51 us  [compute(): pl.pallas_call(kernel, out_shape=[like(shape, dtype) for shape, dtype in...]
    pallas_call x5 -> x1, Pallas kernels: 43.8 us -> 38.7 us  [centre(): pl.pallas_call(centre_kernel, out_shape=[like((1,), WIDE), like((3,), WID...]
where the time goes in v2:
time: 283 us
  Pallas kernels  260 us (92%)
  local copies, waits for them, and re-layouts  12.4 us (4%)
  other arithmetic  7.25 us (3%)
    pallas_call x2, Pallas kernels, exchange(): pl.pallas_call(functools.partial(exchange_kernel, count), out_shape=[like...  98.3 us
    pallas_call x4, Pallas kernels, compute(): pl.pallas_call(kernel, out_shape=[like(shape, dtype) for shape, dtype in...  51 us
    pallas_call x1, Pallas kernels, centre(): pl.pallas_call(centre_kernel, out_shape=[like((1,), WIDE), like((3,), WID...  38.7 us
    pallas_call x1, Pallas kernels, collect(): pl.pallas_call(functools.partial(collect_kernel, plans), out_shape=[like(...  36.7 us
    pallas_call x1, Pallas kernels, deal(): pl.pallas_call(functools.partial(deal_kernel, plans), out_shape=[like((pl...  35.6 us

profile of v2, /device:TPU:3, one launch (start us, length us, event | category | flops | bytes accessed | tf_op | source)
XLA Modules:
  0.0 282.7 jit_solution(9256438299119470783)
XLA Ops:
  0.6 0.0 copy-start.9
  0.7 2.0 fusion.3
  2.7 2.4 fusion
  5.0 0.2 copy.24
  5.2 0.9 pad.19.refs_3_.txt_own
  6.1 0.1 copy.23
  6.3 0.9 pad.16.refs_2_.img_own
  7.2 35.6 %shard_map.202 = (bf16[39,96,128]{2,1,0:T(8,128)(2,1)}, bf16[27,64,128]{2,1,0:T(8,128)(2,1)}, s32[32,8,256]{2,1,0:T(8,128)}) custom-call(bf16[20,96,128]{2,1,0:T(8,128)(2,1)} %bitcast.7, bf16[14,64,128]{2,1,0:T(8,128)(2,1)} %bitcast.8, s32[8,256]{1,0:T(8,128)} %refs_2_.1), custom_call_target="tpu_custom_call" | custom-call | tf_op jit(solution)/shard_map/pallas_call | solution.py:482
  42.8 2.4 shard_map.203
  45.2 1.8 broadcast_in_dim.3
  47.1 52.4 %shard_map.204 = (bf16[16,48,3584]{2,1,0:T(8,128)(2,1)}, bf16[2,192,768]{2,1,0:T(8,128)(2,1)}, bf16[8,64,768]{2,1,0:T(8,128)(2,1)}, bf16[8,80,512]{2,1,0:T(8,128)(2,1)}, bf16[16,48,384]{2,1,0:T(8,128)(2,1)}) custom-call(bf16[48,3584]{1,0:T(8,128)(2,1)} %get-tuple-element.61.refs_0_, bf16[192,768]{1,0:T(8,128)(2,1)} %get-tuple-element.62.refs_1_, ...), custom_call_target="tpu_custom_call" | custom-call | tf_op jit(solution)/shard_map/pallas_call | solution.py:275
  99.4 16.3 %shard_map.205 = (bf16[16,768]{1,0:T(8,128)(2,1)}, f32[16,768]{1,0:T(8,128)}, bf16[16,768]{1,0:T(8,128)(2,1)}, bf16[256,768]{1,0:T(8,128)(2,1)}, bf16[256,768]{1...) custom-call(s32[256]{0:T(256)} %ends_ref.3, ...), custom_call_target="tpu_custom_call" | custom-call | tf_op jit(solution)/shard_map/pallas_call | solution.py:1374
  115.8 38.7 %shard_map.206 = (f32[1]{0:T(128)}, f32[3]{0:T(128)}, f32[16,768]{1,0:T(8,128)}, bf16[16,768]{1,0:T(8,128)(2,1)}, bf16[16,512]{1,0:T(8,128)(2,1)}, /*index=5*/f3...) custom-call(f32[3]{0:T(128)} %scale_ref.1, ...), custom_call_target="tpu_custom_call" | custom-call | tf_op jit(solution)/shard_map/pallas_call | solution.py:1417
  154.5 22.5 %shard_map.207 = (f32[8,50,768]{2,1,0:T(8,128)}, f32[8,77,512]{2,1,0:T(8,128)}, bf16[8,64,768]{2,1,0:T(8,128)(2,1)}, bf16[8,80,512]{2,1,0:T(8,128)(2,1)}, bf16[1...) custom-call(s32[256]{0:T(256)} %ends_ref.3, bf16[8,64,768]{2,1,0:T(8,128)(2,1)} %pad.16.refs_2_.img_own, ...), custom_call_target="tpu_custom_call" | custom-call | tf_op jit(solution)/shard_map/pallas_call | solution.py:1374
  177.1 46.0 %shard_map.208 = (bf16[16,16,4352]{2,1,0:T(8,128)(2,1)}, bf16[2,192,768]{2,1,0:T(8,128)(2,1)}, bf16[8,80,512]{2,1,0:T(8,128)(2,1)}, bf16[8,64,768]{2,1,0:T(8,128...) custom-call(bf16[16,4352]{1,0:T(8,128)(2,1)} %get-tuple-element.87.refs_0_, ...), custom_call_target="tpu_custom_call" | custom-call | tf_op jit(solution)/shard_map/pallas_call | solution.py:275
  223.1 1.4 convert_select_fusion
  224.4 0.1 copy-done.5
  224.6 0.2 copy-done.8
  224.7 0.2 convert_select_fusion.1
  224.9 1.4 copy.25
  226.4 1.8 copy.26
  228.1 9.7 %shard_map.209 = (bf16[39,96,128]{2,1,0:T(8,128)(2,1)}, bf16[27,64,128]{2,1,0:T(8,128)(2,1)}) custom-call(bf16[16,48,512]{2,1,0:T(8,128)(2,1)} %get-tuple-element.96.outer_ref, bf16[16,16,4352]{2,1,0:T(8,128)(2,1)} %get-tuple-element.97.factor_ref, bf16[16,48,384]{2,1,0:T(8,128)(2,1)} %get-tuple-element.98.raise_ref, f32[192,768]{1,0:T(8,128)} %get-tuple-element.99.keep_ref, ...), custom_call_target="tpu_custom_call" | custom-call | tf_op jit(solution)/shard_map/pallas_call | solution.py:1374
  237.9 36.7 %shard_map.210 = (bf16[20,96,128]{2,1,0:T(8,128)(2,1)}, bf16[14,64,128]{2,1,0:T(8,128)(2,1)}) custom-call(bf16[39,96,128]{2,1,0:T(8,128)(2,1)} %get-tuple-element.101.refs_0_, bf16[27,64,128]{2,1,0:T(8,128)(2,1)} %get-tuple-element.102.refs_1_), custom_call_target="tpu_custom_call" | custom-call | tf_op jit(solution)/shard_map/pallas_call | solution.py:583
  274.5 0.0 copy-start.12
  274.6 0.0 copy-start
  274.6 0.0 copy-start.6
  274.6 2.1 fusion.6
  276.7 0.8 add_multiply_fusion.1
  277.6 1.5 fusion.8
  279.1 1.2 add_multiply_fusion
  280.3 0.1 copy-done.1
  281.1 0.5 copy.30
  (23 shorter events, 0.0 us)
Async XLA Ops:
  0.6 4.4 %copy-start.9 = (bf16[8,77,512]{2,0,1:T(8,128)(2,1)S(1)}, bf16[8,77,512]{2,0,1:T(8,128)(2,1)}, u32[]{:S(2)}) copy-start(bf16[8,77,512]{2,0,1:T(8,128)(2,1)} %param.12) | copy-start | bytes 1892356
  5.0 1.1 copy-start.10
  177.1 46.0 %copy-start.4 = (f32[8,50,768]{2,1,0:T(8,128)S(1)}, f32[8,50,768]{2,1,0:T(8,128)}, u32[]{:S(2)}) copy-start(f32[8,50,768]{2,1,0:T(8,128)} %get-tuple-element.86) | copy-start | bytes 3686404
  223.0 1.5 copy-start.5
  223.0 1.7 copy-start.8
  237.8 36.7 %copy-start.3 = (f32[106720]{0:T(1024)S(1)}, f32[106720]{0:T(1024)}, u32[]{:S(2)}) copy-start(f32[106720]{0:T(1024)} %param.18) | copy-start | bytes 1280644
  237.8 36.7 %copy-start.13 = (f32[106720]{0:T(1024)S(1)}, f32[106720]{0:T(1024)}, u32[]{:S(2)}) copy-start(f32[106720]{0:T(1024)} %param.19) | copy-start | bytes 1280644
  274.5 2.2 copy-start.12
  274.6 3.0 %copy-start = (f32[233808]{0:T(1024)S(1)}, f32[233808]{0:T(1024)}, u32[]{:S(2)}) copy-start(f32[233808]{0:T(1024)} %param.15) | copy-start | bytes 2805700
  274.6 3.0 %copy-start.6 = (f32[233808]{0:T(1024)S(1)}, f32[233808]{0:T(1024)}, u32[]{:S(2)}) copy-start(f32[233808]{0:T(1024)} %param.16) | copy-start | bytes 2805700
  274.6 3.0 %copy-start.11 = (bf16[20,96,128]{2,1,0:T(8,128)(2,1)S(1)}, bf16[20,96,128]{2,1,0:T(8,128)(2,1)}, u32[]{:S(2)}) copy-start(bf16[20,96,128]{2,1,0:T(8,128)(2,1)} %get-tuple-element.103) | copy-start | bytes 1474564
  276.7 2.4 copy-start.2
  277.6 1.5 copy-start.7
  279.1 1.2 copy-start.1
  279.1 1.9 copy-start.14

commit v3 on v0

--- a/solution.py
+++ b/solution.py
@@ -1,8 +1,11 @@
+import functools
 import math
 
 import jax
 import jax.numpy as jnp
 from jax import lax
+from jax.experimental import pallas as pl
+from jax.experimental.pallas import tpu as pltpu
 from jax.sharding import PartitionSpec as P
 
 D_IMG = 768
@@ -17,6 +20,1857 @@
 average_rate = 0.5
 step_rate = 0.08
 scale_rate = 0.0001
+
+
+MESH = pl.DeviceIdType.MESH
+ANY = pl.BlockSpec(memory_space=pl.ANY)
+GRANT = 58 * 1024 * 1024
+LANES = 128
+LOW = jnp.bfloat16
+WIDE = jnp.float32
+
+
+def here():
+    return lax.axis_index("tower"), lax.axis_index("dp")
+
+
+def greet(devices):
+    barrier = pltpu.get_barrier_semaphore()
+    for device in devices:
+        pl.semaphore_signal(barrier, inc=1, device_id=device, device_id_type=MESH)
+    pl.semaphore_wait(barrier, len(devices))
+
+
+def remote(src, dst, send_sem, recv_sem, device):
+    return pltpu.make_async_remote_copy(
+        src_ref=src,
+        dst_ref=dst,
+        send_sem=send_sem,
+        recv_sem=recv_sem,
+        device_id=device,
+        device_id_type=MESH,
+    )
+
+
+def comm_params(number):
+    return pltpu.CompilerParams(
+        collective_id=number, has_side_effects=True, vmem_limit_bytes=GRANT
+    )
+
+
+def same_core(tower, at):
+    chip, core = at // 2, at % 2
+    return [(tower, (chip + k) % 8 * 2 + core) for k in range(1, 8)]
+
+
+def both_towers(tower, at):
+    place, core = tower * 8 + at // 2, at % 2
+    others = [(place + k) % 16 for k in range(1, 16)]
+    return [(other // 8, other % 8 * 2 + core) for other in others]
+
+
+def everyone(tower, at):
+    me = tower * 16 + at
+    others = [(me + k) % 32 for k in range(1, 32)]
+    return [(other // 16, other % 16) for other in others]
+
+
+def group_exchange(scattered, x_ref, o_ref, send_sem, recv_sem):
+    tower, at = here()
+    chip = at // 2
+
+    def source(k):
+        return x_ref.at[k] if scattered else x_ref
+
+    own = pltpu.make_async_copy(source(chip), o_ref.at[chip], send_sem.at[7])
+    sent = []
+    for k, device in enumerate(same_core(tower, at)):
+        copy = remote(
+            source((chip + 1 + k) % 8), o_ref.at[chip], send_sem.at[k], recv_sem.at[k], device
+        )
+        copy.start()
+        sent.append(copy)
+    own.start()
+    own.wait()
+    for k in range(7):
+        remote(
+            source(chip),
+            o_ref.at[(chip + 7 - k) % 8],
+            send_sem.at[k],
+            recv_sem.at[k],
+            (tower, at),
+        ).wait_recv()
+    return sent
+
+
+def spread(x_ref, o_ref, send_sem, recv_sem, core_sems):
+    tower, at = here()
+    chip, core = at // 2, at % 2
+    place = tower * 8 + chip
+    sibling = (tower, chip * 2 + 1 - core)
+    sent = []
+    for k, device in enumerate(both_towers(tower, at)):
+        copy = remote(x_ref, o_ref.at[core, place], send_sem.at[k], recv_sem.at[k], device)
+        copy.start()
+        sent.append(copy)
+    own = pltpu.make_async_copy(x_ref, o_ref.at[core, place], send_sem.at[15])
+    own.start()
+    own.wait()
+    for k in range(15):
+        remote(
+            x_ref, o_ref.at[core, (place + 15 - k) % 16], send_sem.at[k], recv_sem.at[k], sibling
+        ).wait_recv()
+    across = remote(o_ref.at[core], o_ref.at[core], core_sems.at[0], core_sems.at[1], sibling)
+    across.start()
+    sent.append(across)
+    remote(
+        o_ref.at[1 - core], o_ref.at[1 - core], core_sems.at[0], core_sems.at[1], sibling
+    ).wait_recv()
+    return sent
+
+
+class Ring:
+    def __init__(self, src, dst, send, recv):
+        self.src, self.dst, self.send, self.recv = src, dst, send, recv
+        self.tower, self.at = here()
+        self.deep, self.row, self.core = self.at // 4, self.at // 2 % 2, self.at % 2
+        self.sibling = (self.tower, self.at + 1 - 2 * self.core)
+        self.beside = (self.tower, self.spot(0, 1 - self.row))
+        self.sent = []
+
+    def spot(self, k, row):
+        return (self.deep + k) % 4 * 4 + row * 2 + self.core
+
+    def launch(self, src, slot, index, device):
+        copy = remote(src, self.dst.at[slot], self.send.at[index], self.recv.at[index], device)
+        copy.start()
+        self.sent.append(copy)
+
+    def arrived(self, slot, index):
+        remote(
+            self.src, self.dst.at[slot], self.send.at[index], self.recv.at[index], self.sibling
+        ).wait_recv()
+
+    def start(self):
+        for k in (1, 3, 2):
+            self.launch(self.src, self.at, k - 1, (self.tower, self.spot(k, self.row)))
+        self.launch(self.src, self.at, 3, self.beside)
+        self.launch(self.src, self.at, 7, self.sibling)
+        self.own = pltpu.make_async_copy(self.src, self.dst.at[self.at], self.send.at[15])
+        self.own.start()
+
+    def relay_deep(self):
+        for k in (1, 3, 2):
+            slot = self.spot(4 - k, self.row)
+            self.arrived(slot, k - 1)
+            self.launch(self.dst.at[slot], slot, 3 + k, self.beside)
+            self.launch(self.dst.at[slot], slot, 7 + k, self.sibling)
+
+    def relay_row(self):
+        for k in (0, 1, 3, 2):
+            slot = self.spot(4 - k, 1 - self.row)
+            self.arrived(slot, 3 + k)
+            self.launch(self.dst.at[slot], slot, 11 + k, self.sibling)
+
+    def finish(self):
+        for index in range(8):
+            k, row = index % 4, self.row if index < 4 else 1 - self.row
+            slot = (self.deep + 4 - k) % 4 * 4 + row * 2 + 1 - self.core
+            self.arrived(slot, 7 + index)
+        self.own.wait()
+
+    def drain(self):
+        for copy in self.sent:
+            copy.wait_send()
+
+
+class Blocks:
+    def __init__(self, src, dst, send, recv, shared=1):
+        self.src, self.dst, self.send, self.recv = src, dst, send, recv
+        self.tower, self.at = here()
+        self.shared = shared
+        self.sent = []
+
+    def start(self):
+        for k in range(1, 16):
+            to = (self.at + k) % 16
+            copy = remote(
+                self.src.at[to // self.shared],
+                self.dst.at[self.at],
+                self.send.at[k - 1],
+                self.recv.at[k - 1],
+                (self.tower, to),
+            )
+            copy.start()
+            self.sent.append(copy)
+        self.own = pltpu.make_async_copy(
+            self.src.at[self.at // self.shared], self.dst.at[self.at], self.send.at[15]
+        )
+        self.own.start()
+
+    def finish(self):
+        for k in range(1, 16):
+            remote(
+                self.src.at[0],
+                self.dst.at[(self.at + 16 - k) % 16],
+                self.send.at[k - 1],
+                self.recv.at[k - 1],
+                (self.tower, self.at),
+            ).wait_recv()
+        self.own.wait()
+
+    def drain(self):
+        for copy in self.sent:
+            copy.wait_send()
+
+
+class Pair:
+    def __init__(self, from_zero, zero_dst, from_one, one_dst, sems):
+        tower, at = here()
+        partner = (1 - tower, at)
+        self.tower = tower
+        self.up = remote(from_zero, zero_dst, sems.at[0], sems.at[1], partner)
+        self.down = remote(from_one, one_dst, sems.at[0], sems.at[1], partner)
+
+    def by_tower(self, zero, one):
+        pl.when(self.tower == 0)(zero)
+        pl.when(self.tower == 1)(one)
+
+    def start(self):
+        self.by_tower(self.up.start, self.down.start)
+
+    def finish(self):
+        self.by_tower(self.down.wait_recv, self.up.wait_recv)
+
+    def drain(self):
+        self.by_tower(self.up.wait_send, self.down.wait_send)
+
+
+VECTORS = 5
+
+
+class Plan:
+    def __init__(self, tower, share, rows, per_device):
+        self.tower = tower
+        self.share = share
+        self.rows = rows
+        self.chunk = rows * LANES
+        self.per_device = per_device
+        self.first_slot = [sum(per_device[:p]) for p in range(6)]
+        self.first_chunk = [16 * slot for slot in self.first_slot]
+        self.slots = sum(per_device) + 1
+        self.total = 16 * sum(per_device) + 1
+        spans = [self.span(device) for device in range(32)]
+        self.counts = sorted({last - first + 1 for first, last in spans})
+        self.local = self.counts[-1]
+
+    def span(self, device):
+        first = device * self.share // self.chunk
+        last = ((device + 1) * self.share - 1) // self.chunk
+        return first, min(last, self.total - 1)
+
+    def bounds(self, device):
+        first = device * self.share // self.chunk
+        last = ((device + 1) * self.share - 1) // self.chunk
+        return first, jnp.minimum(last, self.total - 1)
+
+    def pieces(self, p):
+        return self.per_device[p] if p < VECTORS else 1
+
+    def target(self, g):
+        piece, base, slot, n = (jnp.int32(0), jnp.int32(0), jnp.int32(0), jnp.int32(1))
+        for p in range(VECTORS):
+            inside = g >= self.first_chunk[p]
+            piece = jnp.where(inside, p, piece)
+            base = jnp.where(inside, self.first_chunk[p], base)
+            slot = jnp.where(inside, self.first_slot[p], slot)
+            n = jnp.where(inside, self.per_device[p], n)
+        at = (g - base) // n
+        return piece, at, slot + (g - base) - at * n
+
+
+class Deal:
+    def __init__(self, plan, s, src, dst, extra, last, sems):
+        self.plan, self.s, self.src, self.dst = plan, s, src, dst
+        self.extra, self.last = extra, last
+        self.chunk_send, self.recv, self.edge, self.fetch = sems
+        self.tower, self.at = here()
+        self.me = self.tower * 16 + self.at
+        self.first, self.last_chunk = plan.bounds(self.me)
+        before = (self.me + 31) % 32
+        self.head = remote(
+            src.at[0], extra, self.edge.at[s, 0], self.edge.at[s, 1], (before // 16, before % 16)
+        )
+
+    def send_head(self):
+        pl.when(self.me > 0)(self.head.start)
+
+    def move(self, src, i, piece, at_to, slot, wait):
+        far = jnp.logical_or(self.tower != self.plan.tower, at_to != self.at)
+        recv = self.recv.at[self.s, piece]
+        copy = remote(
+            src,
+            self.dst.at[slot],
+            self.chunk_send.at[self.s, i],
+            recv,
+            (jnp.int32(self.plan.tower), at_to),
+        )
+        pl.when(far)(copy.wait_send if wait else copy.start)
+        if not wait:
+            pl.when(jnp.logical_not(far))(
+                pltpu.make_async_copy(src, self.dst.at[slot], recv).start
+            )
+
+    def whole(self, early, wait):
+        def step(i, carry):
+            g = self.first + i
+            piece, at_to, slot = self.plan.target(g)
+            inside = jnp.logical_and(
+                jnp.logical_or(i > 0, self.me == 0),
+                jnp.logical_or(
+                    g < self.last_chunk, jnp.logical_and(self.me == 31, g < self.plan.total - 1)
+                ),
+            )
+            inside = jnp.logical_and(inside, g <= self.last_chunk)
+            inside = jnp.logical_and(inside, g < self.plan.total - 1)
+            if early is not None:
+                hidden = jnp.logical_and(piece >= 2, piece <= 3)
+                inside = jnp.logical_and(inside, jnp.logical_not(hidden) if early else hidden)
+
+            @pl.when(inside)
+            def _():
+                self.move(self.src.at[i], i, piece, at_to, slot, wait)
+
+            return carry
+
+        lax.fori_loop(0, self.plan.local, step, 0)
+
+    def vectors(self, wait):
+        @pl.when(self.me == 31)
+        def _():
+            src = self.src.at[self.last_chunk - self.first]
+
+            def each(k, carry):
+                self.move(src, self.plan.local + k, VECTORS, k, self.plan.slots - 1, wait)
+                return carry
+
+            lax.fori_loop(0, 16, each, 0)
+
+    def fetch_last(self):
+        return pltpu.make_async_copy(
+            self.src.at[self.last_chunk - self.first], self.last, self.fetch.at[self.s]
+        )
+
+    def join(self):
+        @pl.when(self.me < 31)
+        def _():
+            self.fetch_last().wait()
+            self.head.wait_recv()
+            self.last[...] = self.last[...] + self.extra[...]
+            piece, at_to, slot = self.plan.target(self.last_chunk)
+            self.move(self.last, self.plan.local + 16, piece, at_to, slot, False)
+
+    def start_fetch(self):
+        pl.when(self.me < 31)(self.fetch_last().start)
+
+    def arrived(self, p):
+        part = self.dst.at[pl.ds(self.plan.first_slot[p], self.plan.pieces(p))]
+        pltpu.make_async_copy(part, part, self.recv.at[self.s, p]).wait()
+
+    def drain(self):
+        pl.when(self.me > 0)(self.head.wait_send)
+        self.whole(None, True)
+        self.vectors(True)
+
+        @pl.when(self.me < 31)
+        def _():
+            piece, at_to, slot = self.plan.target(self.last_chunk)
+            self.move(self.last, self.plan.local + 16, piece, at_to, slot, True)
+
+
+class Collect:
+    def __init__(self, plan, s, src, dst, send, recv):
+        self.plan, self.s, self.src, self.dst = plan, s, src, dst
+        self.send, self.recv = send, recv
+        self.tower, self.at = here()
+        self.me = self.tower * 16 + self.at
+
+    def one(self, owner, slot, g, which, wait):
+        first, _ = self.plan.bounds(owner)
+        far = owner != self.me
+        recv = self.recv.at[self.s]
+        copy = remote(
+            self.src.at[slot],
+            self.dst.at[g - first],
+            self.send.at[which, slot],
+            recv,
+            (owner // 16, owner % 16),
+        )
+        pl.when(far)(copy.wait_send if wait else copy.start)
+        if not wait:
+            pl.when(jnp.logical_not(far))(
+                pltpu.make_async_copy(self.src.at[slot], self.dst.at[g - first], recv).start
+            )
+
+    def piece(self, p, wait):
+        n = self.plan.pieces(p)
+
+        def step(i, carry):
+            slot = self.plan.first_slot[p] + i
+            g = self.plan.first_chunk[p] + self.at * n + i if p < VECTORS else self.plan.total - 1
+            low = g * self.plan.chunk // self.plan.share
+            high = jnp.minimum(((g + 1) * self.plan.chunk - 1) // self.plan.share, 31)
+            self.one(low, slot, g, 0, wait)
+            pl.when(high != low)(lambda: self.one(high, slot, g, 1, wait))
+            return carry
+
+        if p == VECTORS:
+
+
+            @pl.when(self.at == 0)
+            def _():
+                step(0, 0)
+
+        else:
+            lax.fori_loop(0, n, step, 0)
+
+    def finish(self):
+        first, last = self.plan.bounds(self.me)
+        held = last - first + 1
+        for n in self.plan.counts:
+
+            @pl.when(held == n)
+            def _():
+                part = self.dst.at[pl.ds(0, n)]
+                pltpu.make_async_copy(part, part, self.recv.at[self.s]).wait()
+
+
+SEQS = 16
+HEADS = 16
+
+
+class Tower:
+    def __init__(self, index, width, hidden, length, room, causal):
+        self.index = index
+        self.width = width
+        self.hidden = hidden
+        self.length = length
+        self.room = room
+        self.causal = causal
+        self.heads = width // HEAD
+        self.block = width // 16
+        self.part = hidden // 8
+        self.reduce_rows = hidden // 16
+
+
+TOWERS = (
+    Tower(0, D_IMG, FF_IMG, 50, 64, False),
+    Tower(1, D_TXT, FF_TXT, 77, 80, True),
+)
+ROOM = 80
+WIDTH = D_IMG
+PART = FF_IMG // 8
+
+
+def each_tower(run):
+    tower = lax.axis_index("tower")
+    for kind in TOWERS:
+        pl.when(tower == kind.index)(functools.partial(run, kind))
+
+
+def dot_nn(a, b):
+    return lax.dot_general(a, b, (((1,), (0,)), ((), ())), preferred_element_type=WIDE)
+
+
+def dot_nt(a, b):
+    return lax.dot_general(a, b, (((1,), (1,)), ((), ())), preferred_element_type=WIDE)
+
+
+def dot_tn(a, b):
+    return lax.dot_general(a, b, (((0,), (0,)), ((), ())), preferred_element_type=WIDE)
+
+
+def standardise(rows):
+    centred = rows - jnp.mean(rows, axis=-1, keepdims=True)
+    spread = jnp.mean(centred * centred, axis=-1, keepdims=True)
+    rate = lax.rsqrt(spread + 1e-05)
+    return centred * rate, rate
+
+
+def norm_back(grad, gain, hat, rate):
+    scaled = grad * gain
+    return rate * (
+        scaled
+        - jnp.mean(scaled, axis=-1, keepdims=True)
+        - hat * jnp.mean(scaled * hat, axis=-1, keepdims=True)
+    )
+
+
+def spans(kind):
+    return [
+        (lo, min(lo + 512, kind.width), lo // HEAD, (min(lo + 512, kind.width) - lo) // HEAD)
+        for lo in range(0, kind.width, 512)
+    ]
+
+
+def head_rows(rows, span):
+    lo, hi, _, n = span
+    part = rows[:, lo:hi]
+    owner = lax.broadcasted_iota(jnp.int32, part.shape, 1) // HEAD
+    nothing = jnp.zeros_like(part)
+    return jnp.concatenate([jnp.where(owner == h, part, nothing) for h in range(n)], axis=0)
+
+
+def from_head_rows(rows, span):
+    _, _, _, n = span
+    owner = lax.broadcasted_iota(jnp.int32, (SEQS, rows.shape[1]), 1) // HEAD
+    total = jnp.zeros((SEQS, rows.shape[1]), rows.dtype)
+    for h in range(n):
+        total = jnp.where(owner == h, rows[h * SEQS : (h + 1) * SEQS], total)
+    return total
+
+
+def side_by_side(parts):
+    return parts[0] if len(parts) == 1 else jnp.concatenate(parts, axis=1)
+
+
+def get_rows(ref, place, width):
+    return side_by_side([ref[c, place, :] for c in range(width // LANES)])
+
+
+def put_rows(ref, place, value):
+    for c in range(value.shape[1] // LANES):
+        ref[c, place, :] = value[:, c * LANES : (c + 1) * LANES]
+
+
+def matrix(ref, kind, start, width):
+    return ref[:, : kind.block, start : start + width].reshape(kind.width, width)
+
+
+def vector(vec_ref, kind, row):
+    return vec_ref[row : row + 1, : kind.width]
+
+
+def pieces_of(kind):
+    return (
+        (kind.block, 3 * kind.width),
+        (kind.block, kind.width),
+        (kind.block, kind.hidden),
+        (kind.reduce_rows, kind.width),
+        (kind.block, EMB),
+        (16, kind.width),
+    )
+
+
+def lane_blocks(kind, plan, p):
+    height, width = pieces_of(kind)[p]
+    pitch = width // LANES
+    base = plan.first_slot[p] * plan.rows if p < VECTORS else (plan.slots - 1) * plan.rows
+    return [(c, pl.ds(base + c, height, stride=pitch)) for c in range(pitch)]
+
+
+def lift(kind, plan, p, slots, flat):
+    n = plan.pieces(p)
+    slot = plan.first_slot[p]
+    rows = slots[slot : slot + n].reshape(n * plan.rows, LANES)
+    flat[slot * plan.rows : (slot + n) * plan.rows, :] = rows.astype(WIDE)
+    return [(c, flat[place, :]) for c, place in lane_blocks(kind, plan, p)]
+
+
+def drop(kind, plan, p, value, slots, flat):
+    for c, place in lane_blocks(kind, plan, p):
+        flat[place, :] = value(c)
+    n = plan.pieces(p)
+    slot = plan.first_slot[p]
+    rows = flat[slot * plan.rows : (slot + n) * plan.rows, :]
+    slots[slot : slot + n] = rows.reshape(n, plan.rows, LANES).astype(LOW)
+
+
+def front_kernel(
+    plans,
+    ends_ref,
+    img_src,
+    txt_src,
+    valid_ref,
+    img_own,
+    txt_own,
+    second_ref,
+    middle_ref,
+    query_ref,
+    keyed_ref,
+    mixture_ref,
+    weight_ref,
+    first_ref,
+    img_in,
+    txt_in,
+    ask_ref,
+    mix_ref,
+    emb_ref,
+    vec_ref,
+    raise_ref,
+    reduce_ref,
+    pairs_ref,
+    img_slots,
+    txt_slots,
+    img_extra,
+    txt_extra,
+    img_last,
+    txt_last,
+    flat,
+    ask_block,
+    mix_block,
+    emb_block,
+    raise_block,
+    reduce_block,
+    top_scr,
+    at_scr,
+    score_scr,
+    low_scr,
+    deal_send,
+    deal_recv,
+    deal_edge,
+    deal_fetch,
+    ask_send,
+    ask_recv,
+    mix_send,
+    mix_recv,
+    emb_send,
+    emb_recv,
+    raise_send,
+    raise_recv,
+    reduce_sems,
+    pair_sems,
+    valid_send,
+    valid_recv,
+):
+    tower, at = here()
+    core = at % 2
+    me = tower * 16 + at
+    sibling = (tower, at + 1 - 2 * core)
+    homes = everyone(tower, at)
+    greet(homes)
+    deal_sems = (deal_send, deal_recv, deal_edge, deal_fetch)
+    deals = [
+        Deal(plans[0], 0, img_src, img_slots, img_extra, img_last, deal_sems),
+        Deal(plans[1], 1, txt_src, txt_slots, txt_extra, txt_last, deal_sems),
+    ]
+    pair = Pair(txt_own, txt_in, img_own, img_in, pair_sems)
+    ask = Ring(ask_block, ask_ref, ask_send, ask_recv)
+    mix = Ring(mix_block, mix_ref, mix_send, mix_recv)
+    embed = Ring(emb_block, emb_ref, emb_send, emb_recv)
+    rise = Blocks(raise_block, raise_ref, raise_send, raise_recv, 2)
+    fall = remote(
+        reduce_block, reduce_ref.at[core], reduce_sems.at[0], reduce_sems.at[1], sibling
+    )
+    fall_own = pltpu.make_async_copy(reduce_block, reduce_ref.at[core], reduce_sems.at[2])
+    masks = [
+        remote(valid_ref, pairs_ref.at[me], valid_send.at[k], valid_recv.at[k], home)
+        for k, home in enumerate(homes)
+    ]
+    mask_own = pltpu.make_async_copy(valid_ref, pairs_ref.at[me], valid_send.at[31])
+
+    for deal in deals:
+        deal.send_head()
+        deal.start_fetch()
+        deal.vectors(False)
+    for deal in deals:
+        deal.whole(True, False)
+    pair.start()
+    for deal in deals:
+        deal.join()
+
+    def lift_to(kind, p, ref, start):
+        slots = (img_slots, txt_slots)[kind.index]
+        for c, value in lift(kind, plans[kind.index], p, slots, flat):
+            lane = start + c * LANES
+            ref[: value.shape[0], lane : lane + LANES] = value.astype(ref.dtype)
+
+    def normalise(kind, half):
+        width, room = kind.width, kind.room
+        own, arrived = ((img_own, img_in), (txt_own, txt_in))[kind.index]
+        ref = own if half == kind.index else arrived
+        gain, shift = vector(vec_ref, kind, 0), vector(vec_ref, kind, 1)
+        positions = lax.broadcasted_iota(jnp.int32, (room, 1), 0)
+        for i in range(8):
+            rows = ref[i].astype(WIDE)
+            hat, _ = standardise(rows)
+            first = (hat * gain + shift).astype(LOW)
+            s = half * 8 + i
+            first_ref[s, :room, :width] = first
+            if kind.causal:
+                chosen = positions == ends_ref[(half * 16 + at) * 8 + i]
+                top = jnp.sum(jnp.where(chosen, first.astype(WIDE), 0.0), axis=0, keepdims=True)
+                raw = jnp.sum(jnp.where(chosen, rows, 0.0), axis=0, keepdims=True)
+            else:
+                top, raw = first[:1].astype(WIDE), rows[:1]
+            top_scr[s : s + 1, :width] = top
+            at_scr[s : s + 1, :width] = raw
+
+    def begin(kind):
+        deal = deals[kind.index]
+        deal.arrived(VECTORS)
+        lift_to(kind, VECTORS, vec_ref, 0)
+        normalise(kind, kind.index)
+
+    each_tower(begin)
+
+    def place_inputs(kind):
+        deals[kind.index].arrived(0)
+        slots = (img_slots, txt_slots)[kind.index]
+        per = kind.width // LANES
+        for c, value in lift(kind, plans[kind.index], 0, slots, flat):
+            lane = c // per * WIDTH + c % per * LANES
+            ref = ask_block
+            if lane >= 2 * WIDTH:
+                ref, lane = mix_block, lane - 2 * WIDTH
+            ref[: value.shape[0], lane : lane + LANES] = value.astype(LOW)
+
+    each_tower(place_inputs)
+    ask.start()
+
+    def place_rest(kind):
+        deals[kind.index].arrived(1)
+        lift_to(kind, 1, mix_block, WIDTH)
+        deals[kind.index].arrived(4)
+        lift_to(kind, 4, emb_block, 0)
+
+    each_tower(place_rest)
+    mix.start()
+    embed.start()
+    for deal in deals:
+        deal.whole(False, False)
+    pair.finish()
+    each_tower(lambda kind: normalise(kind, 1 - kind.index))
+    for copy in masks:
+        copy.start()
+    mask_own.start()
+    ask.relay_deep()
+    ask.relay_row()
+    ask.finish()
+
+    def question(kind):
+        width = kind.width
+        tops = top_scr[:, :width].astype(LOW)
+        query = dot_nn(tops, matrix(ask_ref, kind, 0, width)) + vector(vec_ref, kind, 2)
+        query = query.astype(LOW)
+        query_ref[:, :width] = query
+        for span in spans(kind):
+            lo, hi, first_head, n = span
+            put_rows(
+                keyed_ref,
+                pl.ds(first_head * SEQS, n * SEQS),
+                dot_nt(head_rows(query, span), matrix(ask_ref, kind, WIDTH + lo, hi - lo)) * 0.125,
+            )
+        dead = (HEADS - kind.heads) * SEQS
+        put_rows(keyed_ref, pl.ds(kind.heads * SEQS, dead), jnp.zeros((dead, width), WIDE))
+
+    each_tower(question)
+    mix.relay_deep()
+    embed.relay_deep()
+
+    def score(kind):
+        width, room = kind.width, kind.room
+        lane = lax.broadcasted_iota(jnp.int32, (HEADS, room), 1)
+        for s in range(SEQS):
+            keys = get_rows(keyed_ref, pl.ds(s, HEADS, stride=SEQS), width).astype(LOW)
+            scores = dot_nt(keys, first_ref[s, :room, :width])
+            if kind.causal:
+                allowed = lane <= ends_ref[(s // 8 * 16 + at) * 8 + s % 8]
+            else:
+                allowed = lane < kind.length
+            score_scr[s * HEADS : (s + 1) * HEADS, :room] = jnp.where(allowed, scores, -1e30)
+        scores = score_scr[:, :room]
+        raw = jnp.exp(scores - jnp.max(scores, axis=-1, keepdims=True))
+        weights = raw / jnp.sum(raw, axis=-1, keepdims=True)
+        head = lax.broadcasted_iota(jnp.int32, (SEQS * HEADS, 1), 0) % HEADS
+        weights = jnp.where(head < kind.heads, weights, 0.0)
+        weight_ref[:, :room] = weights
+        low_scr[:, :room] = weights.astype(LOW)
+
+    each_tower(score)
+    mix.relay_row()
+    embed.relay_row()
+
+    def mixture(kind):
+        width, room = kind.width, kind.room
+        for s in range(SEQS):
+            mixed = dot_nn(
+                low_scr[s * HEADS : (s + 1) * HEADS, :room], first_ref[s, :room, :width]
+            )
+            put_rows(mixture_ref, pl.ds(s, HEADS, stride=SEQS), mixed)
+        totals = jnp.sum(low_scr[:, :room].astype(WIDE), axis=-1, keepdims=True)
+        score_scr[...] = jnp.broadcast_to(totals, score_scr.shape)
+
+    each_tower(mixture)
+
+    def place_hidden(kind):
+        deal, plan = deals[kind.index], plans[kind.index]
+        slots = (img_slots, txt_slots)[kind.index]
+        deal.arrived(2)
+        per = kind.part // LANES
+        for c, value in lift(kind, plan, 2, slots, flat):
+            lane = c % per * LANES
+            raise_block[c // per, : kind.block, lane : lane + LANES] = value.astype(LOW)
+        deal.arrived(3)
+        lift_to(kind, 3, reduce_block, 0)
+
+    each_tower(place_hidden)
+    rise.start()
+    fall.start()
+    fall_own.start()
+    mix.finish()
+
+    def answer(kind):
+        width = kind.width
+        mixed = []
+        bias = vector(vec_ref, kind, 3)
+        for span in spans(kind):
+            lo, hi, first_head, n = span
+            z = get_rows(mixture_ref, pl.ds(first_head * SEQS, n * SEQS), width).astype(LOW)
+            valued = dot_nn(z, matrix(mix_ref, kind, lo, hi - lo))
+            totals = jnp.concatenate(
+                [score_scr[pl.ds(first_head + h, SEQS, stride=HEADS), 0:1] for h in range(n)],
+                axis=0,
+            )
+            mixed.append(from_head_rows(valued + totals * bias[:, lo:hi], span))
+        mixed = side_by_side(mixed).astype(LOW)
+        middle = (
+            at_scr[:, :width]
+            + dot_nn(mixed, matrix(mix_ref, kind, WIDTH, width))
+            + vector(vec_ref, kind, 4)
+        )
+        middle_ref[:, :width] = middle
+        hat, _ = standardise(middle)
+        second_ref[:, :width] = (
+            hat * vector(vec_ref, kind, 5) + vector(vec_ref, kind, 6)
+        ).astype(LOW)
+        put_rows(mixture_ref, pl.ds(12 * SEQS, SEQS), top_scr[:, :width])
+        put_rows(mixture_ref, pl.ds(13 * SEQS, SEQS), mixed.astype(WIDE))
+
+    each_tower(answer)
+    embed.finish()
+    rise.finish()
+    fall_own.wait()
+    remote(
+        reduce_block, reduce_ref.at[1 - core], reduce_sems.at[0], reduce_sems.at[1], sibling
+    ).wait_recv()
+    mask_own.wait()
+    for k, home in enumerate(homes):
+        source = (me + 31 - k) % 32
+        remote(
+            valid_ref, pairs_ref.at[source], valid_send.at[k], valid_recv.at[k], home
+        ).wait_recv()
+    for copy in [*masks, fall]:
+        copy.wait_send()
+    for group in (pair, ask, mix, embed, rise, *deals):
+        group.drain()
+
+
+def expand_matrix(ref, kind):
+    return ref[:, : kind.block, : kind.part].reshape(kind.width, kind.part)
+
+
+def reduce_matrix(ref, kind):
+    return ref[:, : kind.reduce_rows, : kind.width].reshape(kind.part, kind.width)
+
+
+def hidden_bias(vec_ref, kind):
+    chip = lax.axis_index("dp") // 2
+    whole = vec_ref[...]
+    row = lax.broadcasted_iota(jnp.int32, (16, 1), 0)
+    line = jnp.sum(jnp.where(row == 10 + chip // 2, whole, 0.0), axis=0, keepdims=True)
+    return jnp.where(
+        chip % 2 == 0, line[:, : kind.part], line[:, kind.part : 2 * kind.part]
+    )
+
+
+def hidden_kernel(second_ref, raise_ref, reduce_ref, vec_ref, part_ref, raised_ref):
+    def run(kind):
+        width = kind.width
+        rows = second_ref[:, :, :width].reshape(8 * SEQS, width)
+        raised = dot_nn(rows, expand_matrix(raise_ref, kind)) + hidden_bias(vec_ref, kind)
+        raised_ref[:, : kind.part] = raised
+        active = (raised * jax.nn.sigmoid(1.702 * raised)).astype(LOW)
+        part = dot_nn(active, reduce_matrix(reduce_ref, kind))
+        part_ref[:, :, :width] = part.reshape(8, SEQS, width).astype(LOW)
+
+    each_tower(run)
+
+
+def hidden_back_kernel(
+    grad_ref,
+    second_ref,
+    raised_ref,
+    raise_ref,
+    reduce_ref,
+    back_ref,
+    raise_grad_ref,
+    reduce_keep_ref,
+    reduce_send_ref,
+    bias_ref,
+    whole,
+):
+    def run(kind):
+        width, part = kind.width, kind.part
+        grads = grad_ref[:, :, :width].reshape(8 * SEQS, width)
+        rows = second_ref[:, :, :width].reshape(8 * SEQS, width)
+        raised = raised_ref[:, :part]
+        gate = jax.nn.sigmoid(1.702 * raised)
+        active = (raised * gate).astype(LOW)
+        slope = gate + 1.702 * raised * gate * (1.0 - gate)
+        raised_grad = dot_nt(grads, reduce_matrix(reduce_ref, kind)) * slope
+        low_grad = raised_grad.astype(LOW)
+        bias_ref[0:1, :part] = jnp.sum(low_grad.astype(WIDE), axis=0, keepdims=True)
+        back = dot_nt(low_grad, expand_matrix(raise_ref, kind))
+        back_ref[:, :, :width] = back.reshape(8, SEQS, width).astype(LOW)
+        raise_grad_ref[:, : kind.block, :part] = (
+            dot_tn(rows, low_grad).reshape(16, kind.block, part).astype(LOW)
+        )
+        whole[:part, :width] = dot_tn(active, grads)
+        core = lax.axis_index("dp") % 2
+        n = kind.reduce_rows
+        keep = pl.multiple_of(core * n, 64)
+        send = pl.multiple_of((1 - core) * n, 64)
+        reduce_keep_ref[:n, :width] = whole[pl.ds(keep, n), :width]
+        reduce_send_ref[:n, :width] = whole[pl.ds(send, n), :width].astype(LOW)
+
+    each_tower(run)
+
+
+def embed_kernel(part_ref, middle_ref, gat_ref, vec_ref, emb_ref, final_ref, pooled_ref, proj_ref):
+    def run(kind):
+        width = kind.width
+        final = (
+            middle_ref[:, :width]
+            + jnp.sum(part_ref[:, :, :width].astype(WIDE), axis=0)
+            + vector(vec_ref, kind, 7)
+        )
+        final_ref[:, :width] = final
+        hat, _ = standardise(final)
+        pooled = (hat * vector(vec_ref, kind, 8) + vector(vec_ref, kind, 9)).astype(LOW)
+        pooled_ref[:, :width] = pooled
+        proj = dot_nn(pooled, matrix(gat_ref, kind, 0, EMB))
+        proj_ref[...] = proj
+        size = jnp.sum(proj * proj, axis=-1, keepdims=True) + 1e-06
+        emb_ref[...] = (proj * lax.rsqrt(size)).astype(LOW)
+
+    each_tower(run)
+
+
+def objective_kernel(
+    scale_ref,
+    all_ref,
+    valid_ref,
+    final_ref,
+    proj_ref,
+    gat_ref,
+    vec_ref,
+    low_ref,
+    grad_ref,
+    proj_grad_ref,
+    final_vec_ref,
+    loss_ref,
+    scale_new_ref,
+    own_scr,
+):
+    def ordered(which):
+        blocks = []
+        for half in range(2):
+            for j in range(16):
+                rows = all_ref[j % 2, which * 8 + j // 2].astype(WIDE)
+                blocks.append(rows[half * 8 : half * 8 + 8])
+        return jnp.concatenate(blocks, axis=0).astype(LOW)
+
+    img, txt = ordered(0), ordered(1)
+    total = img.shape[0]
+    scale = jnp.exp(jnp.full((1, 1), scale_ref[0], WIDE))
+    allowed = valid_ref[...].reshape(total, total) > 0
+    same = lax.broadcasted_iota(jnp.int32, (total, total), 0) == lax.broadcasted_iota(
+        jnp.int32, (total, total), 1
+    )
+    same = same.astype(WIDE)
+
+    def side(left, right):
+        logits = scale * dot_nt(left, right)
+        masked = jnp.where(allowed, logits, -1e30)
+        top = jnp.max(masked, axis=1, keepdims=True)
+        lse = jnp.log(jnp.sum(jnp.exp(masked - top), axis=1, keepdims=True)) + top
+        terms = 0.5 * (jnp.where(allowed, jnp.exp(logits - lse), 0.0) - same)
+        loss = 0.5 * (
+            jnp.sum(lse, axis=0, keepdims=True)
+            - jnp.sum(jnp.sum(logits * same, axis=1, keepdims=True), axis=0, keepdims=True)
+        )
+        rate = jnp.sum(jnp.sum(terms * logits, axis=1, keepdims=True), axis=0, keepdims=True)
+        return (scale * terms).astype(LOW), loss, rate
+
+    row_back, row_loss, row_rate = side(img, txt)
+    col_back, col_loss, col_rate = side(txt, img)
+    loss_ref[0] = jnp.sum(row_loss + col_loss) / total
+    parts = advance(
+        scale_ref[0], scale_ref[1], scale_ref[2], jnp.sum(row_rate + col_rate), scale_rate
+    )
+    for k in range(3):
+        scale_new_ref[k] = parts[k]
+
+    def run(kind):
+        width = kind.width
+        if kind.index == 0:
+            emb_grad = dot_nn(row_back, txt) + dot_tn(col_back, txt)
+        else:
+            emb_grad = dot_nn(col_back, img) + dot_tn(row_back, img)
+        own_scr[...] = emb_grad
+        at = lax.axis_index("dp")
+        mine = jnp.concatenate(
+            [
+                own_scr[pl.ds(pl.multiple_of(half * 128 + at * 8, 8), 8), :]
+                for half in range(2)
+            ],
+            axis=0,
+        )
+        proj = proj_ref[...]
+        size = jnp.sum(proj * proj, axis=-1, keepdims=True) + 1e-06
+        along = jnp.sum(proj * mine, axis=-1, keepdims=True)
+        proj_grad = ((mine - proj * along / size) * lax.rsqrt(size)).astype(LOW)
+        proj_grad_ref[...] = proj_grad
+        pooled_grad = dot_nt(proj_grad, matrix(gat_ref, kind, 0, EMB))
+        hat, rate = standardise(final_ref[:, :width])
+        final_vec_ref[0:1, :width] = jnp.sum(pooled_grad * hat, axis=0, keepdims=True)
+        final_vec_ref[1:2, :width] = jnp.sum(pooled_grad, axis=0, keepdims=True)
+        final_grad = norm_back(pooled_grad, vector(vec_ref, kind, 8), hat, rate)
+        grad_ref[:, :width] = final_grad
+        low = final_grad.astype(LOW)
+        low_ref[:, :width] = low
+        final_vec_ref[2:3, :width] = jnp.sum(low.astype(WIDE), axis=0, keepdims=True)
+
+    each_tower(run)
+
+
+def centre_kernel(
+    scale_ref,
+    second_ref,
+    middle_ref,
+    emb_weight_ref,
+    vec_ref,
+    raise_ref,
+    reduce_ref,
+    valid_ref,
+    loss_ref,
+    scale_new_ref,
+    final_grad_ref,
+    pooled_ref,
+    proj_grad_ref,
+    final_vec_ref,
+    raise_grad_ref,
+    reduce_keep_ref,
+    reduce_send_ref,
+    bias_ref,
+    backs_ref,
+    seconds,
+    part,
+    parts,
+    raised,
+    emb,
+    embs,
+    final,
+    proj,
+    low,
+    lows,
+    back,
+    own_scr,
+    whole,
+    send_sems,
+    recv_sems,
+    spread_send,
+    spread_recv,
+    core_sems,
+):
+    tower, at = here()
+    greet([*both_towers(tower, at), (tower, at + 1 - at % 2 * 2)])
+    sent = []
+    sent += group_exchange(False, second_ref, seconds, send_sems.at[0], recv_sems.at[0])
+    hidden_kernel(seconds, raise_ref, reduce_ref, vec_ref, part, raised)
+    sent += group_exchange(True, part, parts, send_sems.at[1], recv_sems.at[1])
+    embed_kernel(parts, middle_ref, emb_weight_ref, vec_ref, emb, final, pooled_ref, proj)
+    sent += spread(emb, embs, spread_send, spread_recv, core_sems)
+    objective_kernel(
+        scale_ref,
+        embs,
+        valid_ref,
+        final,
+        proj,
+        emb_weight_ref,
+        vec_ref,
+        low,
+        final_grad_ref,
+        proj_grad_ref,
+        final_vec_ref,
+        loss_ref,
+        scale_new_ref,
+        own_scr,
+    )
+    sent += group_exchange(False, low, lows, send_sems.at[2], recv_sems.at[2])
+    hidden_back_kernel(
+        lows,
+        seconds,
+        raised,
+        raise_ref,
+        reduce_ref,
+        back,
+        raise_grad_ref,
+        reduce_keep_ref,
+        reduce_send_ref,
+        bias_ref,
+        whole,
+    )
+    sent += group_exchange(True, back, backs_ref, send_sems.at[3], recv_sems.at[3])
+    for copy in sent:
+        copy.wait_send()
+
+
+def back_kernel(
+    plans,
+    ends_ref,
+    img_own,
+    img_in,
+    txt_own,
+    txt_in,
+    first_ref,
+    ask_ref,
+    mix_ref,
+    vec_ref,
+    backs_ref,
+    grad_ref,
+    middle_ref,
+    query_ref,
+    keyed_ref,
+    mixture_ref,
+    weight_ref,
+    pooled_ref,
+    proj_grad_ref,
+    final_vec_ref,
+    bias_ref,
+    raise_grad_ref,
+    reduce_keep_ref,
+    reduce_send_ref,
+    img_keep,
+    txt_keep,
+    img_chunks,
+    txt_chunks,
+    img_send,
+    txt_send,
+    img_home,
+    txt_home,
+    rows_grad,
+    middle_scr,
+    second_scr,
+    valued_scr,
+    turn_scr,
+    shared_scr,
+    slope_scr,
+    low_scr,
+    left_scr,
+    left_block,
+    turn_block,
+    left_all,
+    turn_all,
+    early_block,
+    early_all,
+    late_block,
+    late_all,
+    lines_block,
+    lines_all,
+    raise_all,
+    reduce_in,
+    flat,
+    img_slots,
+    txt_slots,
+    gains,
+    top_grad_scr,
+    raise_send,
+    raise_recv,
+    reduce_sems,
+    left_send,
+    left_recv,
+    turn_send,
+    turn_recv,
+    early_send,
+    early_recv,
+    late_send,
+    late_recv,
+    lines_send,
+    lines_recv,
+    pair_sems,
+    collect_send,
+    collect_recv,
+):
+    tower, at = here()
+    core = at % 2
+    sibling = (tower, at + 1 - 2 * core)
+    greet(everyone(tower, at))
+    rise = Blocks(raise_grad_ref, raise_all, raise_send, raise_recv)
+    fall = remote(reduce_send_ref, reduce_in, reduce_sems.at[0], reduce_sems.at[1], sibling)
+    lefts = Blocks(left_block, left_all, left_send, left_recv)
+    turns = Blocks(turn_block, turn_all, turn_send, turn_recv)
+    early = Ring(early_block, early_all, early_send, early_recv)
+    late = Ring(late_block, late_all, late_send, late_recv)
+    pair = Pair(img_send, img_home, txt_send, txt_home, pair_sems)
+    collects = [
+        Collect(plans[0], 0, img_slots, img_chunks, collect_send.at[0], collect_recv),
+        Collect(plans[1], 1, txt_slots, txt_chunks, collect_send.at[1], collect_recv),
+    ]
+    rise.start()
+    fall.start()
+
+    def outputs(kind):
+        width = kind.width
+        second_grad = jnp.sum(backs_ref[:, :, :width].astype(WIDE), axis=0)
+        second_scr[:, :width] = second_grad
+        hat, rate = standardise(middle_ref[:, :width])
+        middle_grad = grad_ref[:, :width] + norm_back(
+            second_grad, vector(vec_ref, kind, 5), hat, rate
+        )
+        middle_scr[:, :width] = middle_grad
+        output_grad = middle_grad.astype(LOW)
+        mixed_grad = dot_nt(output_grad, matrix(mix_ref, kind, WIDTH, width)).astype(LOW)
+        early_block[:, 0:width] = query_ref[:, :width]
+        early_block[:, WIDTH : WIDTH + width] = mixed_grad
+        early_block[:, 2 * WIDTH : 2 * WIDTH + width] = output_grad
+        early_block[:, 3 * WIDTH : 3 * WIDTH + EMB] = proj_grad_ref[...]
+        left_scr[:, :width] = get_rows(mixture_ref, slice(None), width)
+        left_scr[14 * SEQS : 15 * SEQS, :width] = pooled_ref[:, :width].astype(WIDE)
+        left_scr[15 * SEQS :, :width] = jnp.zeros((SEQS, width), WIDE)
+
+    each_tower(outputs)
+    early.start()
+
+    def turned(kind):
+        width, block = kind.width, kind.block
+        left_block[:, :block, :] = left_scr[:, :width].T.reshape(16, block, 256).astype(LOW)
+
+    each_tower(turned)
+    lefts.start()
+
+    def values(kind):
+        width = kind.width
+        mixed_grad = early_block[:, WIDTH : WIDTH + width]
+        bias = vector(vec_ref, kind, 3)
+        dead = kind.heads * SEQS
+        put_rows(valued_scr, pl.ds(dead, 256 - dead), jnp.zeros((256 - dead, width), WIDE))
+        shared_scr[dead:, :] = jnp.zeros((256 - dead, LANES), WIDE)
+        for span in spans(kind):
+            lo, hi, first_head, n = span
+            rows = head_rows(mixed_grad, span)
+            place = pl.ds(first_head * SEQS, n * SEQS)
+            put_rows(valued_scr, place, dot_nt(rows, matrix(mix_ref, kind, lo, hi - lo)))
+            constant = jnp.sum(rows.astype(WIDE) * bias[:, lo:hi], axis=-1, keepdims=True)
+            shared_scr[place, :] = jnp.broadcast_to(constant, (n * SEQS, LANES))
+
+    each_tower(values)
+
+    def slopes(kind):
+        width, room = kind.width, kind.room
+        for s in range(SEQS):
+            line = pl.ds(s, HEADS, stride=SEQS)
+            slope = dot_nt(
+                get_rows(valued_scr, line, width).astype(LOW), first_ref[s, :room, :width]
+            )
+            slope_scr[s * HEADS : (s + 1) * HEADS, :room] = slope + shared_scr[line, 0:1]
+        weights = weight_ref[:, :room]
+        slope = slope_scr[:, :room]
+        slope = weights * (slope - jnp.sum(weights * slope, axis=-1, keepdims=True))
+        both = jnp.concatenate(
+            [slope.reshape(SEQS, HEADS, room), weights.reshape(SEQS, HEADS, room)], axis=1
+        )
+        low_scr[:, :room] = both.reshape(2 * SEQS * HEADS, room).astype(LOW)
+
+    each_tower(slopes)
+    early.relay_deep()
+
+    def tokens(kind):
+        width, room = kind.width, kind.room
+        for s in range(SEQS):
+            line = pl.ds(s, HEADS, stride=SEQS)
+            both = low_scr[2 * s * HEADS : 2 * (s + 1) * HEADS, :room]
+            first = first_ref[s, :room, :width]
+            put_rows(turn_scr, line, dot_nn(both[:HEADS], first))
+            right = jnp.concatenate(
+                [get_rows(keyed_ref, line, width), get_rows(valued_scr, line, width)], axis=0
+            )
+            rows_grad[s, :room, :width] = dot_tn(both, right.astype(LOW))
+
+    each_tower(tokens)
+    early.relay_row()
+
+    def queries(kind):
+        width, block = kind.width, kind.block
+        grads = []
+        for span in spans(kind):
+            lo, hi, first_head, n = span
+            rows = get_rows(turn_scr, pl.ds(first_head * SEQS, n * SEQS), width).astype(LOW)
+            back = dot_nn(rows, matrix(ask_ref, kind, WIDTH + lo, hi - lo)) * 0.125
+            grads.append(from_head_rows(back, span))
+        query_grad = side_by_side(grads).astype(LOW)
+        late_block[:, :width] = query_grad
+        top_grad_scr[:, :width] = dot_nt(query_grad, matrix(ask_ref, kind, 0, width))
+        turn_block[:, :block, :] = (
+            get_rows(turn_scr, slice(None), width).T.reshape(16, block, 256).astype(LOW)
+        )
+
+    each_tower(queries)
+    late.start()
+    turns.start()
+    gains[...] = jnp.zeros_like(gains)
+
+    def finish(kind, half):
+        width, room, length = kind.width, kind.room, kind.length
+        own, arrived = ((img_own, img_in), (txt_own, txt_in))[kind.index]
+        ref = own if half == kind.index else arrived
+        keep, send = ((img_keep, img_send), (txt_keep, txt_send))[kind.index]
+        gain = vector(vec_ref, kind, 0)
+        positions = lax.broadcasted_iota(jnp.int32, (room, 1), 0)
+        gain_sum = jnp.zeros((1, width), WIDE)
+        shift_sum = jnp.zeros((1, width), WIDE)
+        for i in range(8):
+            s = half * 8 + i
+            hat, rate = standardise(ref[i].astype(WIDE))
+            if kind.causal:
+                chosen = positions == ends_ref[(half * 16 + at) * 8 + i]
+            else:
+                chosen = positions == 0
+            chosen = chosen.astype(WIDE)
+            grad = rows_grad[s, :room, :width] + chosen * top_grad_scr[s : s + 1, :width]
+            gain_sum += jnp.sum(grad * hat, axis=0, keepdims=True)
+            shift_sum += jnp.sum(grad, axis=0, keepdims=True)
+            result = norm_back(grad, gain, hat, rate) + chosen * middle_scr[s : s + 1, :width]
+            if half == kind.index:
+                keep[i] = result[:length]
+            else:
+                send[i] = result.astype(LOW)
+        gains[0:1, :width] += gain_sum
+        gains[1:2, :width] += shift_sum
+
+    each_tower(lambda kind: finish(kind, 1 - kind.index))
+    pair.start()
+    rise.finish()
+    remote(
+        reduce_send_ref, reduce_in, reduce_sems.at[0], reduce_sems.at[1], sibling
+    ).wait_recv()
+
+    def slots_of(kind):
+        return (img_slots, txt_slots)[kind.index]
+
+    def hidden_grads(kind):
+        plan, collect = plans[kind.index], collects[kind.index]
+        block, n, per = kind.block, kind.reduce_rows, kind.part // LANES
+
+        def risen(c):
+            chip, lane = c // per, c % per * LANES
+            return raise_all[2 * chip, :block, lane : lane + LANES].astype(WIDE) + raise_all[
+                2 * chip + 1, :block, lane : lane + LANES
+            ].astype(WIDE)
+
+        def fallen(c):
+            lane = c * LANES
+            return reduce_keep_ref[:n, lane : lane + LANES] + reduce_in[
+                :n, lane : lane + LANES
+            ].astype(WIDE)
+
+        drop(kind, plan, 2, risen, slots_of(kind), flat)
+        collect.piece(2, False)
+        drop(kind, plan, 3, fallen, slots_of(kind), flat)
+        collect.piece(3, False)
+
+    each_tower(hidden_grads)
+    late.relay_deep()
+    each_tower(lambda kind: finish(kind, kind.index))
+    late.relay_row()
+
+    def lines(kind):
+        width = kind.width
+        hat, _ = standardise(middle_ref[:, :width])
+        second_grad = second_scr[:, :width]
+
+        def column_sum(value):
+            return jnp.sum(value.astype(WIDE), axis=0, keepdims=True)
+
+        mixed_grad = early_block[:, WIDTH : WIDTH + width].astype(WIDE)
+        weights = low_scr[:, : kind.room].astype(WIDE).reshape(SEQS, 2 * HEADS, kind.room)
+        totals = jnp.sum(weights[:, HEADS:], axis=-1, keepdims=True).reshape(SEQS * HEADS, 1)
+        shared_scr[...] = jnp.broadcast_to(totals, shared_scr.shape)
+        value_bias = []
+        for lo, hi, first_head, n in spans(kind):
+            owner = lax.broadcasted_iota(jnp.int32, (SEQS, hi - lo), 1) // HEAD
+            scaled = jnp.zeros((SEQS, hi - lo), WIDE)
+            for h in range(n):
+                total = shared_scr[pl.ds(first_head + h, SEQS, stride=HEADS), 0:1]
+                scaled = jnp.where(owner == h, mixed_grad[:, lo:hi] * total, scaled)
+            value_bias.append(column_sum(scaled))
+        hidden = bias_ref[0:1, : kind.part]
+        parts = [
+            gains[0:1, :width],
+            gains[1:2, :width],
+            column_sum(late_block[:, :width]),
+            side_by_side(value_bias),
+            column_sum(early_block[:, 2 * WIDTH : 2 * WIDTH + width]),
+            column_sum(second_grad * hat),
+            column_sum(second_grad),
+            final_vec_ref[2:3, :width],
+            final_vec_ref[0:1, :width],
+            final_vec_ref[1:2, :width],
+            jnp.concatenate([hidden, jnp.zeros((1, width - kind.part), WIDE)], axis=1),
+            jnp.zeros((5, width), WIDE),
+        ]
+        lines_block[:, :width] = jnp.concatenate(parts, axis=0)
+
+    each_tower(lines)
+    line_copy = remote(
+        lines_block, lines_all.at[at], lines_send.at[0], lines_recv.at[at], (tower, jnp.int32(0))
+    )
+    line_own = pltpu.make_async_copy(lines_block, lines_all.at[at], lines_recv.at[at])
+    pl.when(at > 0)(line_copy.start)
+    pl.when(at == 0)(line_own.start)
+
+    early.finish()
+    lefts.finish()
+
+    def from_early(kind):
+        plan, collect = plans[kind.index], collects[kind.index]
+        width, block = kind.width, kind.block
+
+        def gathered(k):
+            lane = lax.broadcasted_iota(jnp.int32, (block, LANES), 1) // SEQS
+            halves = []
+            for side in range(2):
+                total = jnp.zeros((block, LANES), WIDE)
+                for j in range(8):
+                    part = left_all[side * 8 + j, :block, LANES:].astype(WIDE)
+                    shift = (j * SEQS - (k - 8) * SEQS) % LANES
+                    turned_part = pltpu.roll(part, shift, 1) if shift else part
+                    total = jnp.where(lane == j, turned_part, total)
+                halves.append(total)
+            return jnp.concatenate(halves, axis=1).astype(LOW)
+
+        def right(start, wide):
+            return early_all[:, :, start : start + wide].reshape(256, wide)
+
+        output = dot_nn(gathered(13), right(2 * WIDTH, width))
+        drop(
+            kind, plan, 1, lambda c: output[:, c * LANES : (c + 1) * LANES], slots_of(kind), flat
+        )
+        collect.piece(1, False)
+        embed = dot_nn(gathered(14), right(3 * WIDTH, EMB))
+        drop(kind, plan, 4, lambda c: embed[:, c * LANES : (c + 1) * LANES], slots_of(kind), flat)
+        collect.piece(4, False)
+        left_scr[:block, :256] = gathered(12).astype(WIDE)
+
+    each_tower(from_early)
+    late.finish()
+    turns.finish()
+
+    def from_late(kind):
+        plan, collect = plans[kind.index], collects[kind.index]
+        width, block = kind.width, kind.block
+        ask = dot_nn(left_scr[:block, :256].astype(LOW), late_all[:, :, :width].reshape(256, width))
+
+        def outer(side_ref, start, span):
+            lo, hi, first_head, n = span
+            lane = first_head * SEQS
+            total = jnp.zeros((block, hi - lo), WIDE)
+            for j in range(8):
+                left, rows = [], []
+                for source in (2 * j, 2 * j + 1):
+                    left.append(side_ref[source, :block, lane : lane + LANES])
+                    rows.append(
+                        head_rows(early_all[source, :, start : start + width], span)
+                    )
+                    if n < 8:
+                        rows.append(jnp.zeros(((8 - n) * SEQS, hi - lo), LOW))
+                total += dot_nn(
+                    jnp.concatenate(left, axis=1), jnp.concatenate(rows, axis=0)
+                )
+            return total
+
+        keys = side_by_side([outer(turn_all, 0, span) for span in spans(kind)]) * 0.125
+        worth = side_by_side([outer(left_all, WIDTH, span) for span in spans(kind)])
+        per = width // LANES
+
+        def inputs(c):
+            value = (ask, keys, worth)[c // per]
+            return value[:, c % per * LANES : (c % per + 1) * LANES]
+
+        drop(kind, plan, 0, inputs, slots_of(kind), flat)
+        collect.piece(0, False)
+
+    each_tower(from_late)
+
+    @pl.when(at == 0)
+    def _():
+        for k in range(1, 16):
+            remote(
+                lines_block, lines_all.at[k], lines_send.at[0], lines_recv.at[k], sibling
+            ).wait_recv()
+        line_own.wait()
+
+        def vectors(kind):
+            width, part = kind.width, kind.part
+            whole = [jnp.sum(lines_all[:, :10, :width], axis=0)]
+            for row in range(4):
+                pair_of = []
+                for chip in (2 * row, 2 * row + 1):
+                    pair_of.append(
+                        lines_all[2 * chip, 10:11, :part] + lines_all[2 * chip + 1, 10:11, :part]
+                    )
+                whole.append(jnp.concatenate(pair_of, axis=1))
+            whole.append(jnp.zeros((2, width), WIDE))
+            result = jnp.concatenate(whole, axis=0)
+            drop(
+                kind,
+                plans[kind.index],
+                VECTORS,
+                lambda c: result[:, c * LANES : (c + 1) * LANES],
+                slots_of(kind),
+                flat,
+            )
+
+        each_tower(vectors)
+
+    each_tower(lambda kind: collects[kind.index].piece(VECTORS, False))
+    pair.finish()
+
+    @pl.when(tower == 1)
+    def _():
+        img_keep[...] = img_home[:, : TOWERS[0].length].astype(WIDE)
+
+    @pl.when(tower == 0)
+    def _():
+        txt_keep[...] = txt_home[:, : TOWERS[1].length].astype(WIDE)
+
+    for collect in collects:
+        collect.finish()
+    fall.wait_send()
+    pl.when(at > 0)(line_copy.wait_send)
+    for group in (rise, lefts, turns, early, late, pair):
+        group.drain()
+
+    def drain(kind):
+        for p in range(VECTORS + 1):
+            collects[kind.index].piece(p, True)
+
+    each_tower(drain)
+
+
+def dma(*shape):
+    return pltpu.SemaphoreType.DMA(shape)
+
+
+def call(kernel, number, operands, outs, scratch, semaphores):
+    spec = {"vmem": pltpu.VMEM, "smem": pltpu.SMEM, "any": pl.ANY}
+    return pl.pallas_call(
+        kernel,
+        out_shape=[jax.ShapeDtypeStruct(shape, dtype) for _, shape, dtype in outs],
+        in_specs=[pl.BlockSpec(memory_space=spec[place]) for place, _ in operands],
+        out_specs=[pl.BlockSpec(memory_space=spec[place]) for place, _, _ in outs],
+        scratch_shapes=[pltpu.VMEM(shape, dtype) for shape, dtype in scratch] + semaphores,
+        compiler_params=comm_params(number),
+    )(*[value for _, value in operands])
+
+
+ROWS_LOW = ((SEQS, WIDTH), LOW)
+ROWS_WIDE = ((SEQS, WIDTH), WIDE)
+HEAD_ROWS = ((WIDTH // LANES, SEQS * HEADS, LANES), WIDE)
+LANE_ROWS = ((SEQS * HEADS, LANES), WIDE)
+GROUP = ((8, SEQS, WIDTH), LOW)
+
+
+def chunk_shapes(plan, n):
+    return ((n, plan.rows, LANES), LOW)
+
+
+def front(txt_ends, img_chunks, txt_chunks, valid, img_rows, txt_rows, plans, number):
+    operands = [
+        ("smem", txt_ends),
+        ("any", img_chunks),
+        ("any", txt_chunks),
+        ("vmem", valid),
+        ("vmem", img_rows),
+        ("vmem", txt_rows),
+    ]
+    outs = [
+        ROWS_LOW,
+        ROWS_WIDE,
+        ROWS_LOW,
+        HEAD_ROWS,
+        HEAD_ROWS,
+        LANE_ROWS,
+        ((SEQS, ROOM, WIDTH), LOW),
+        (img_rows.shape, LOW),
+        (txt_rows.shape, LOW),
+        ((16, 48, 2 * WIDTH), LOW),
+        ((16, 48, 2 * WIDTH), LOW),
+        ((16, 48, EMB), LOW),
+        ROWS_WIDE,
+        ((16, 48, PART), LOW),
+        ((2, 192, WIDTH), LOW),
+        ((32, *valid.shape), valid.dtype),
+    ]
+    chunks = [chunk_shapes(plan, 1) for plan in plans]
+    edges = [(shape[1:], dtype) for shape, dtype in chunks]
+    scratch = [
+        *[chunk_shapes(plan, plan.slots) for plan in plans],
+        *edges,
+        *edges,
+        ((plans[0].slots * plans[0].rows, LANES), WIDE),
+        ((48, 2 * WIDTH), LOW),
+        ((48, 2 * WIDTH), LOW),
+        ((48, EMB), LOW),
+        ((8, 48, PART), LOW),
+        ((192, WIDTH), LOW),
+        ROWS_WIDE,
+        ROWS_WIDE,
+        LANE_ROWS,
+        ((SEQS * HEADS, LANES), LOW),
+    ]
+    most = max(plan.local for plan in plans) + 17
+    semaphores = [
+        dma(2, most),
+        dma(2, 6),
+        dma(2, 2),
+        dma(2),
+        *[dma(16), dma(15)] * 4,
+        dma(3),
+        dma(2),
+        dma(32),
+        dma(31),
+    ]
+    return call(
+        functools.partial(front_kernel, plans),
+        number,
+        operands,
+        [("vmem", *out) for out in outs],
+        scratch,
+        semaphores,
+    )
+
+
+def centre(scale_state, second, middle, emb_weight, vec, rise, fall, pairs, number):
+    operands = [("smem", scale_state)] + [
+        ("vmem", value) for value in (second, middle, emb_weight, vec, rise, fall, pairs)
+    ]
+    outs = [
+        ROWS_WIDE,
+        ROWS_LOW,
+        ((SEQS, EMB), LOW),
+        ((8, WIDTH), WIDE),
+        ((16, 48, PART), LOW),
+        ((192, WIDTH), WIDE),
+        ((192, WIDTH), LOW),
+        ((8, PART), WIDE),
+        GROUP,
+    ]
+    scratch = [
+        GROUP,
+        GROUP,
+        GROUP,
+        ((128, PART), WIDE),
+        ((SEQS, EMB), LOW),
+        ((2, 16, SEQS, EMB), LOW),
+        ROWS_WIDE,
+        ((SEQS, EMB), WIDE),
+        ROWS_LOW,
+        GROUP,
+        GROUP,
+        ((256, EMB), WIDE),
+        ((PART, WIDTH), WIDE),
+    ]
+    return call(
+        centre_kernel,
+        number,
+        operands,
+        [("smem", (1,), WIDE), ("smem", (3,), WIDE)] + [("vmem", *out) for out in outs],
+        scratch,
+        [dma(4, 8), dma(4, 7), dma(16), dma(15), dma(2)],
+    )
+
+
+def back(txt_ends, values, plans, number):
+    operands = [("smem", txt_ends)] + [("vmem", value) for value in values]
+    rooms = [((8, kind.room, kind.width), LOW) for kind in TOWERS]
+    outs = [((8, kind.length, kind.width), WIDE) for kind in TOWERS] + [
+        chunk_shapes(plan, plan.local) for plan in plans
+    ]
+    blocks = ((16, 48, 256), LOW)
+    scratch = [
+        *rooms,
+        *rooms,
+        ((SEQS, ROOM, WIDTH), WIDE),
+        ROWS_WIDE,
+        ROWS_WIDE,
+        HEAD_ROWS,
+        HEAD_ROWS,
+        LANE_ROWS,
+        LANE_ROWS,
+        ((2 * SEQS * HEADS, LANES), LOW),
+        ((SEQS * HEADS, WIDTH), WIDE),
+        blocks,
+        blocks,
+        blocks,
+        blocks,
+        ((SEQS, 3 * WIDTH + EMB), LOW),
+        ((16, SEQS, 3 * WIDTH + EMB), LOW),
+        ROWS_LOW,
+        ((16, SEQS, WIDTH), LOW),
+        ROWS_WIDE,
+        ((16, SEQS, WIDTH), WIDE),
+        ((16, 48, PART), LOW),
+        ((192, WIDTH), LOW),
+        ((plans[0].slots * plans[0].rows, LANES), WIDE),
+        *[chunk_shapes(plan, plan.slots) for plan in plans],
+        ((8, WIDTH), WIDE),
+        ROWS_WIDE,
+    ]
+    most = max(plan.slots for plan in plans)
+    semaphores = [
+        dma(16),
+        dma(15),
+        dma(2),
+        *[dma(16), dma(15)] * 4,
+        dma(1),
+        dma(16),
+        dma(2),
+        dma(2, 2, most),
+        dma(2),
+    ]
+    return call(
+        functools.partial(back_kernel, plans),
+        number,
+        operands,
+        [("vmem", *out) for out in outs],
+        scratch,
+        semaphores,
+    )
+
+
+def to_chunks(flat, plan, me):
+    start = me * plan.share % plan.chunk
+    padded = jnp.pad(flat, (plan.chunk, plan.local * plan.chunk - plan.share))
+    piece = lax.dynamic_slice(padded, (plan.chunk - start,), (plan.local * plan.chunk,))
+    return piece.astype(LOW).reshape(plan.local, plan.rows, LANES)
+
+
+def from_chunks(chunks, plan, me):
+    start = me * plan.share % plan.chunk
+    return lax.dynamic_slice(chunks.reshape(-1), (start,), (plan.share,)).astype(WIDE)
+
+
+def step(
+    img_tokens,
+    txt_tokens,
+    txt_ends,
+    valid,
+    img_master,
+    img_moment,
+    img_average,
+    txt_master,
+    txt_moment,
+    txt_average,
+    scale_state,
+):
+    me = lax.axis_index(("tower", "dp"))
+    plans = (
+        Plan(0, img_master.shape[0], 96, (9, 3, 12, 12, 2)),
+        Plan(1, txt_master.shape[0], 64, (6, 2, 8, 8, 2)),
+    )
+    img_rows = jnp.pad(img_tokens, ((0, 0), (0, TOWERS[0].room - TOWERS[0].length), (0, 0)))
+    txt_rows = jnp.pad(txt_tokens, ((0, 0), (0, TOWERS[1].room - TOWERS[1].length), (0, 0)))
+    (
+        second,
+        middle,
+        query,
+        keyed,
+        mixture,
+        weights,
+        first,
+        img_in,
+        txt_in,
+        ask,
+        mix,
+        emb_weight,
+        vec,
+        rise,
+        fall,
+        pairs,
+    ) = front(
+        txt_ends,
+        to_chunks(img_master, plans[0], me),
+        to_chunks(txt_master, plans[1], me),
+        valid,
+        img_rows,
+        txt_rows,
+        plans,
+        0,
+    )
+    (
+        loss,
+        scale_new,
+        final_grad,
+        pooled,
+        proj_grad,
+        final_vec,
+        rise_grad,
+        fall_keep,
+        fall_send,
+        bias_grad,
+        backs,
+    ) = centre(scale_state, second, middle, emb_weight, vec, rise, fall, pairs, 1)
+    img_grad, txt_grad, img_chunks, txt_chunks = back(
+        txt_ends,
+        [
+            img_rows,
+            img_in,
+            txt_rows,
+            txt_in,
+            first,
+            ask,
+            mix,
+            vec,
+            backs,
+            final_grad,
+            middle,
+            query,
+            keyed,
+            mixture,
+            weights,
+            pooled,
+            proj_grad,
+            final_vec,
+            bias_grad,
+            rise_grad,
+            fall_keep,
+            fall_send,
+        ],
+        plans,
+        2,
+    )
+    img_new = advance(
+        img_master, img_moment, img_average, from_chunks(img_chunks, plans[0], me), step_rate
+    )
+    txt_new = advance(
+        txt_master, txt_moment, txt_average, from_chunks(txt_chunks, plans[1], me), step_rate
+    )
+    return (
+        loss[0],
+        img_grad,
+        txt_grad,
+        img_new[0],
+        img_new[1],
+        img_new[2],
+        img_new[0].astype(LOW),
+        txt_new[0],
+        txt_new[1],
+        txt_new[2],
+        txt_new[0].astype(LOW),
+        scale_new,
+    )
 
 
 def from_partner(value, axis, stride):
@@ -386,4 +2240,5 @@
         P(("tower", "dp")),
         P(),
     )
-    return jax.shard_map(body, mesh=mesh, in_specs=in_specs, out_specs=out_specs, check_vma=False)
+    run = step if (mesh.shape["tower"], mesh.shape["dp"]) == (2, 16) else body
+    return jax.shard_map(run, mesh=mesh, in_specs=in_specs, out_specs=out_specs, check_vma=False)

time: 1940 us -> 248 us (0.13)
  waiting for transfers between devices: 839 us -> 0 us
  local copies, waits for them, and re-layouts: 533 us -> 11.8 us
  Pallas kernels: 0 us -> 225 us
  matrix products: 125 us -> 0 us
  blocking collectives: 124 us -> 0 us
  other arithmetic: 124 us -> 4.56 us
  starting transfers between devices: 114 us -> 0 us
  loops' own time: 35.6 us -> 0 us
  between operations: 24.2 us -> 2.62 us
    unnamed x5 -> x0, waiting for transfers between devices: 457 us -> none
    reduce_scatter x2 -> x0, waiting for transfers between devices: 257 us -> none  [the longest x1 132 us: body(): lax.psum_scatter(across(row_back, img_local), ('tower', 'dp'), scatter_di...]
    pallas_call x0 -> x3, Pallas kernels: none -> 225 us  [call(): pl.pallas_call(kernel, out_shape=[jax.ShapeDtypeStruct(shape, dtype) for...]
    reshape x23 -> x0, local copies, waits for them, and re-layouts: 155 us -> none  [the longest x2 63.8 us: text_weights(): whole.reshape(2, tower_count, shard_room)[:, :, :txt_share].reshape(-1)]
    cond x101 -> x0, local copies, waits for them, and re-layouts: 155 us -> none
    dot_general x34 -> x0, matrix products: 125 us -> none  [the longest x20 89.4 us: product(): return jnp.matmul(left, right)]
    all_gather x1 -> x0, waiting for transfers between devices: 116 us -> none  [body(): gathered = lax.all_gather(stacked, 'dp', axis=1, tiled=True)]
    ppermute x6 -> x0, starting transfers between devices: 113 us -> none  [from_partner(): return lax.ppermute(value, axis, pairs)]
  transfers between devices with their start and end apart: 10 -> 0, of which waited for: 7 -> 0; matrix products, arithmetic and copies ran while one was open for 7% -> 0% of each run, Pallas kernels for 0% -> 0%
where the time goes in v3:
time: 248 us; the launch traced here: 244 us
  Pallas kernels  225 us (91%)
  local copies, waits for them, and re-layouts  11.8 us (5%)
  other arithmetic  4.56 us (2%)
  between operations  2.62 us (1%)
    pallas_call x3, Pallas kernels, call(): pl.pallas_call(kernel, out_shape=[jax.ShapeDtypeStruct(shape, dtype) for...  225 us
    unnamed x33, local copies, waits for them, and re-layouts  5.63 us

profile of v3, /device:TPU:3, one launch (start us, length us, event | category | flops | bytes accessed | tf_op | source)
XLA Modules:
  0.0 244.3 jit_solution(16512451811380143164)
XLA Ops:
  0.6 0.0 copy-start.7
  0.7 2.0 fusion.3
  2.7 2.4 fusion
  5.0 0.0 copy-done.7
  5.0 0.2 copy.24
  5.2 0.9 pad.19.txt_own
  6.1 0.0 copy-done.8
  6.1 0.1 copy.23
  6.3 0.9 pad.18.img_own
  7.2 98.4 %shard_map.202 = (bf16[16,768]{1,0:T(8,128)(2,1)}, f32[16,768]{1,0:T(8,128)}, bf16[16,768]{1,0:T(8,128)(2,1)}, f32[6,256,128]{2,1,0:T(8,128)}, f32[6,256,128]{2,...) custom-call(s32[256]{0:T(256)} %ends_ref.3, ...), custom_call_target="tpu_custom_call" | custom-call | tf_op jit(solution)/shard_map/pallas_call | solution.py:1568
  105.6 47.4 %shard_map.203 = (f32[1]{0:T(128)}, f32[3]{0:T(128)}, f32[16,768]{1,0:T(8,128)}, bf16[16,768]{1,0:T(8,128)(2,1)}, bf16[16,512]{1,0:T(8,128)(2,1)}, /*index=5*/f3...) custom-call(f32[3]{0:T(128)} %scale_ref.1, ...), custom_call_target="tpu_custom_call" | custom-call | tf_op jit(solution)/shard_map/pallas_call | solution.py:1568
  153.0 79.5 %shard_map.204 = (f32[8,50,768]{2,1,0:T(8,128)}, f32[8,77,512]{2,1,0:T(8,128)}, bf16[20,96,128]{2,1,0:T(8,128)(2,1)}, bf16[14,64,128]{2,1,0:T(8,128)(2,1)}) custom-call(s32[256]{0:T(256)} %ends_ref.3, bf16[8,64,768]{2,1,0:T(8,128)(2,1)} %pad.18.img_own, bf16[8,64,768]{2,1,0:T(8,128)(2,1)} %get-tuple-element.51.img_in, bf16[8,80,512]{2,1,0:T(8,128)(2,1)} %pad.19.txt_own, ...), custom_call_target="tpu_custom_call" | custom-call | tf_op jit(solution)/shard_map/pallas_call | solution.py:1568
  232.6 0.0 copy-start.3
  232.6 0.0 copy-start.11
  232.6 0.0 copy-start.12
  232.6 2.9 %copy.25 = f32[8,50,768]{2,0,1:T(8,128)} copy(f32[8,50,768]{2,1,0:T(8,128)} %get-tuple-element.75) | data formatting | bytes 2457600
  235.4 0.0 copy-done.3
  235.4 0.0 copy-done.11
  235.4 0.0 copy-done.12
  235.5 0.0 copy-start.10
  235.5 0.0 copy-start.4
  235.5 1.0 fusion.6
  236.5 0.0 copy-done.10
  236.5 0.9 add_multiply_fusion.1
  237.4 1.8 copy.26
  239.2 0.0 copy-done.2
  239.2 0.0 copy-done.5
  239.2 0.0 copy-start.6
  239.2 1.5 fusion.8
  240.8 1.1 add_multiply_fusion
  241.9 0.1 copy-done.1
  242.7 0.5 copy.30
  (12 shorter events, 0.0 us)
Async XLA Ops:
  0.6 4.4 %copy-start.7 = (bf16[8,77,512]{2,0,1:T(8,128)(2,1)S(1)}, bf16[8,77,512]{2,0,1:T(8,128)(2,1)}, u32[]{:S(2)}) copy-start(bf16[8,77,512]{2,0,1:T(8,128)(2,1)} %param.12) | copy-start | bytes 1892356
  5.0 1.1 copy-start.8
  232.6 2.9 %copy-start.3 = (f32[106720]{0:T(1024)S(1)}, f32[106720]{0:T(1024)}, u32[]{:S(2)}) copy-start(f32[106720]{0:T(1024)} %param.18) | copy-start | bytes 1280644
  232.6 2.9 %copy-start.11 = (f32[106720]{0:T(1024)S(1)}, f32[106720]{0:T(1024)}, u32[]{:S(2)}) copy-start(f32[106720]{0:T(1024)} %param.19) | copy-start | bytes 1280644
  232.6 2.9 %copy-start.12 = (bf16[14,64,128]{2,1,0:T(8,128)(2,1)S(1)}, bf16[14,64,128]{2,1,0:T(8,128)(2,1)}, u32[]{:S(2)}) copy-start(bf16[14,64,128]{2,1,0:T(8,128)(2,1)} %get-tuple-element.72) | copy-start | bytes 688132
  235.5 1.1 copy-start.10
  235.5 1.9 copy-start.4
  236.5 2.7 %copy-start.2 = (f32[106720]{0:T(1024)}, f32[106720]{0:T(1024)S(1)}, u32[]{:S(2)}) copy-start(f32[106720]{0:T(1024)S(1)} %get-tuple-element.111) | copy-start | bytes 1280644
  237.4 1.8 copy-start
  237.4 1.8 copy-start.5
  237.4 1.8 copy-start.9
  239.2 1.5 copy-start.6
  240.8 1.2 copy-start.1
  240.8 1.9 copy-start.13

commit v4 on v3

--- a/solution.py
+++ b/solution.py
@@ -103,30 +103,93 @@
     return sent
 
 
-def spread(x_ref, o_ref, send_sem, recv_sem, core_sems):
-    tower, at = here()
-    chip, core = at // 2, at % 2
-    place = tower * 8 + chip
-    sibling = (tower, chip * 2 + 1 - core)
-    sent = []
-    for k, device in enumerate(both_towers(tower, at)):
-        copy = remote(x_ref, o_ref.at[core, place], send_sem.at[k], recv_sem.at[k], device)
+class Spread:
+    def __init__(self, src, dst, send, recv):
+        self.src, self.dst, self.send, self.recv = src, dst, send, recv
+        tower, at = here()
+        self.core = at % 2
+        self.sibling = (tower, at + 1 - 2 * self.core)
+        self.devices = self.peers(tower, at)
+        self.n = len(self.devices) + 1
+        self.place = self.spot(tower, at)
+        self.sent = []
+
+    def peers(self, tower, at):
+        return both_towers(tower, at)
+
+    def spot(self, tower, at):
+        return tower * 8 + at // 2
+
+    def block(self, place):
+        return self.src
+
+    def side(self, core):
+        return self.dst.at[core]
+
+    def launch(self, src, dst, k, device):
+        copy = remote(src, dst, self.send.at[k], self.recv.at[k], device)
         copy.start()
-        sent.append(copy)
-    own = pltpu.make_async_copy(x_ref, o_ref.at[core, place], send_sem.at[15])
-    own.start()
-    own.wait()
-    for k in range(15):
+        self.sent.append(copy)
+
+    def start(self):
+        for k, device in enumerate(self.devices):
+            to = (self.place + 1 + k) % self.n
+            self.launch(self.block(to), self.side(self.core).at[self.place], k, device)
+        self.own = pltpu.make_async_copy(
+            self.block(self.place), self.side(self.core).at[self.place], self.send.at[self.n]
+        )
+        self.own.start()
+
+    def arrived(self):
+        for k in range(self.n - 1):
+            source = (self.place + self.n - 1 - k) % self.n
+            remote(
+                self.block(0),
+                self.side(self.core).at[source],
+                self.send.at[k],
+                self.recv.at[k],
+                self.sibling,
+            ).wait_recv()
+        self.own.wait()
+
+    def relay(self):
+        self.arrived()
+        side = self.side(self.core)
+        self.launch(side, side, self.n - 1, self.sibling)
+
+    def finish(self):
+        side = self.side(1 - self.core)
         remote(
-            x_ref, o_ref.at[core, (place + 15 - k) % 16], send_sem.at[k], recv_sem.at[k], sibling
+            side, side, self.send.at[self.n - 1], self.recv.at[self.n - 1], self.sibling
         ).wait_recv()
-    across = remote(o_ref.at[core], o_ref.at[core], core_sems.at[0], core_sems.at[1], sibling)
-    across.start()
-    sent.append(across)
-    remote(
-        o_ref.at[1 - core], o_ref.at[1 - core], core_sems.at[0], core_sems.at[1], sibling
-    ).wait_recv()
-    return sent
+
+    def drain(self):
+        for copy in self.sent:
+            copy.wait_send()
+
+
+class Group(Spread):
+    def __init__(self, src, dst, send, recv, both=True):
+        self.both = both
+        super().__init__(src, dst, send, recv)
+
+    def peers(self, tower, at):
+        return same_core(tower, at)
+
+    def spot(self, tower, at):
+        return at // 2
+
+    def block(self, place):
+        return self.src.at[place]
+
+    def side(self, core):
+        return self.dst.at[core] if self.both else self.dst
+
+    def finish(self):
+        if self.both:
+            super().finish()
+        else:
+            self.arrived()
 
 
 class Ring:
@@ -586,288 +649,10 @@
     slots[slot : slot + n] = rows.reshape(n, plan.rows, LANES).astype(LOW)
 
 
-def front_kernel(
-    plans,
-    ends_ref,
-    img_src,
-    txt_src,
-    valid_ref,
-    img_own,
-    txt_own,
-    second_ref,
-    middle_ref,
-    query_ref,
-    keyed_ref,
-    mixture_ref,
-    weight_ref,
-    first_ref,
-    img_in,
-    txt_in,
-    ask_ref,
-    mix_ref,
-    emb_ref,
-    vec_ref,
-    raise_ref,
-    reduce_ref,
-    pairs_ref,
-    img_slots,
-    txt_slots,
-    img_extra,
-    txt_extra,
-    img_last,
-    txt_last,
-    flat,
-    ask_block,
-    mix_block,
-    emb_block,
-    raise_block,
-    reduce_block,
-    top_scr,
-    at_scr,
-    score_scr,
-    low_scr,
-    deal_send,
-    deal_recv,
-    deal_edge,
-    deal_fetch,
-    ask_send,
-    ask_recv,
-    mix_send,
-    mix_recv,
-    emb_send,
-    emb_recv,
-    raise_send,
-    raise_recv,
-    reduce_sems,
-    pair_sems,
-    valid_send,
-    valid_recv,
-):
-    tower, at = here()
-    core = at % 2
-    me = tower * 16 + at
-    sibling = (tower, at + 1 - 2 * core)
-    homes = everyone(tower, at)
-    greet(homes)
-    deal_sems = (deal_send, deal_recv, deal_edge, deal_fetch)
-    deals = [
-        Deal(plans[0], 0, img_src, img_slots, img_extra, img_last, deal_sems),
-        Deal(plans[1], 1, txt_src, txt_slots, txt_extra, txt_last, deal_sems),
-    ]
-    pair = Pair(txt_own, txt_in, img_own, img_in, pair_sems)
-    ask = Ring(ask_block, ask_ref, ask_send, ask_recv)
-    mix = Ring(mix_block, mix_ref, mix_send, mix_recv)
-    embed = Ring(emb_block, emb_ref, emb_send, emb_recv)
-    rise = Blocks(raise_block, raise_ref, raise_send, raise_recv, 2)
-    fall = remote(
-        reduce_block, reduce_ref.at[core], reduce_sems.at[0], reduce_sems.at[1], sibling
-    )
-    fall_own = pltpu.make_async_copy(reduce_block, reduce_ref.at[core], reduce_sems.at[2])
-    masks = [
-        remote(valid_ref, pairs_ref.at[me], valid_send.at[k], valid_recv.at[k], home)
-        for k, home in enumerate(homes)
-    ]
-    mask_own = pltpu.make_async_copy(valid_ref, pairs_ref.at[me], valid_send.at[31])
-
-    for deal in deals:
-        deal.send_head()
-        deal.start_fetch()
-        deal.vectors(False)
-    for deal in deals:
-        deal.whole(True, False)
-    pair.start()
-    for deal in deals:
-        deal.join()
-
-    def lift_to(kind, p, ref, start):
-        slots = (img_slots, txt_slots)[kind.index]
-        for c, value in lift(kind, plans[kind.index], p, slots, flat):
-            lane = start + c * LANES
-            ref[: value.shape[0], lane : lane + LANES] = value.astype(ref.dtype)
-
-    def normalise(kind, half):
-        width, room = kind.width, kind.room
-        own, arrived = ((img_own, img_in), (txt_own, txt_in))[kind.index]
-        ref = own if half == kind.index else arrived
-        gain, shift = vector(vec_ref, kind, 0), vector(vec_ref, kind, 1)
-        positions = lax.broadcasted_iota(jnp.int32, (room, 1), 0)
-        for i in range(8):
-            rows = ref[i].astype(WIDE)
-            hat, _ = standardise(rows)
-            first = (hat * gain + shift).astype(LOW)
-            s = half * 8 + i
-            first_ref[s, :room, :width] = first
-            if kind.causal:
-                chosen = positions == ends_ref[(half * 16 + at) * 8 + i]
-                top = jnp.sum(jnp.where(chosen, first.astype(WIDE), 0.0), axis=0, keepdims=True)
-                raw = jnp.sum(jnp.where(chosen, rows, 0.0), axis=0, keepdims=True)
-            else:
-                top, raw = first[:1].astype(WIDE), rows[:1]
-            top_scr[s : s + 1, :width] = top
-            at_scr[s : s + 1, :width] = raw
-
-    def begin(kind):
-        deal = deals[kind.index]
-        deal.arrived(VECTORS)
-        lift_to(kind, VECTORS, vec_ref, 0)
-        normalise(kind, kind.index)
-
-    each_tower(begin)
-
-    def place_inputs(kind):
-        deals[kind.index].arrived(0)
-        slots = (img_slots, txt_slots)[kind.index]
-        per = kind.width // LANES
-        for c, value in lift(kind, plans[kind.index], 0, slots, flat):
-            lane = c // per * WIDTH + c % per * LANES
-            ref = ask_block
-            if lane >= 2 * WIDTH:
-                ref, lane = mix_block, lane - 2 * WIDTH
-            ref[: value.shape[0], lane : lane + LANES] = value.astype(LOW)
-
-    each_tower(place_inputs)
-    ask.start()
-
-    def place_rest(kind):
-        deals[kind.index].arrived(1)
-        lift_to(kind, 1, mix_block, WIDTH)
-        deals[kind.index].arrived(4)
-        lift_to(kind, 4, emb_block, 0)
-
-    each_tower(place_rest)
-    mix.start()
-    embed.start()
-    for deal in deals:
-        deal.whole(False, False)
-    pair.finish()
-    each_tower(lambda kind: normalise(kind, 1 - kind.index))
-    for copy in masks:
-        copy.start()
-    mask_own.start()
-    ask.relay_deep()
-    ask.relay_row()
-    ask.finish()
-
-    def question(kind):
-        width = kind.width
-        tops = top_scr[:, :width].astype(LOW)
-        query = dot_nn(tops, matrix(ask_ref, kind, 0, width)) + vector(vec_ref, kind, 2)
-        query = query.astype(LOW)
-        query_ref[:, :width] = query
-        for span in spans(kind):
-            lo, hi, first_head, n = span
-            put_rows(
-                keyed_ref,
-                pl.ds(first_head * SEQS, n * SEQS),
-                dot_nt(head_rows(query, span), matrix(ask_ref, kind, WIDTH + lo, hi - lo)) * 0.125,
-            )
-        dead = (HEADS - kind.heads) * SEQS
-        put_rows(keyed_ref, pl.ds(kind.heads * SEQS, dead), jnp.zeros((dead, width), WIDE))
-
-    each_tower(question)
-    mix.relay_deep()
-    embed.relay_deep()
-
-    def score(kind):
-        width, room = kind.width, kind.room
-        lane = lax.broadcasted_iota(jnp.int32, (HEADS, room), 1)
-        for s in range(SEQS):
-            keys = get_rows(keyed_ref, pl.ds(s, HEADS, stride=SEQS), width).astype(LOW)
-            scores = dot_nt(keys, first_ref[s, :room, :width])
-            if kind.causal:
-                allowed = lane <= ends_ref[(s // 8 * 16 + at) * 8 + s % 8]
-            else:
-                allowed = lane < kind.length
-            score_scr[s * HEADS : (s + 1) * HEADS, :room] = jnp.where(allowed, scores, -1e30)
-        scores = score_scr[:, :room]
-        raw = jnp.exp(scores - jnp.max(scores, axis=-1, keepdims=True))
-        weights = raw / jnp.sum(raw, axis=-1, keepdims=True)
-        head = lax.broadcasted_iota(jnp.int32, (SEQS * HEADS, 1), 0) % HEADS
-        weights = jnp.where(head < kind.heads, weights, 0.0)
-        weight_ref[:, :room] = weights
-        low_scr[:, :room] = weights.astype(LOW)
-
-    each_tower(score)
-    mix.relay_row()
-    embed.relay_row()
-
-    def mixture(kind):
-        width, room = kind.width, kind.room
-        for s in range(SEQS):
-            mixed = dot_nn(
-                low_scr[s * HEADS : (s + 1) * HEADS, :room], first_ref[s, :room, :width]
-            )
-            put_rows(mixture_ref, pl.ds(s, HEADS, stride=SEQS), mixed)
-        totals = jnp.sum(low_scr[:, :room].astype(WIDE), axis=-1, keepdims=True)
-        score_scr[...] = jnp.broadcast_to(totals, score_scr.shape)
-
-    each_tower(mixture)
-
-    def place_hidden(kind):
-        deal, plan = deals[kind.index], plans[kind.index]
-        slots = (img_slots, txt_slots)[kind.index]
-        deal.arrived(2)
-        per = kind.part // LANES
-        for c, value in lift(kind, plan, 2, slots, flat):
-            lane = c % per * LANES
-            raise_block[c // per, : kind.block, lane : lane + LANES] = value.astype(LOW)
-        deal.arrived(3)
-        lift_to(kind, 3, reduce_block, 0)
-
-    each_tower(place_hidden)
-    rise.start()
-    fall.start()
-    fall_own.start()
-    mix.finish()
-
-    def answer(kind):
-        width = kind.width
-        mixed = []
-        bias = vector(vec_ref, kind, 3)
-        for span in spans(kind):
-            lo, hi, first_head, n = span
-            z = get_rows(mixture_ref, pl.ds(first_head * SEQS, n * SEQS), width).astype(LOW)
-            valued = dot_nn(z, matrix(mix_ref, kind, lo, hi - lo))
-            totals = jnp.concatenate(
-                [score_scr[pl.ds(first_head + h, SEQS, stride=HEADS), 0:1] for h in range(n)],
-                axis=0,
-            )
-            mixed.append(from_head_rows(valued + totals * bias[:, lo:hi], span))
-        mixed = side_by_side(mixed).astype(LOW)
-        middle = (
-            at_scr[:, :width]
-            + dot_nn(mixed, matrix(mix_ref, kind, WIDTH, width))
-            + vector(vec_ref, kind, 4)
-        )
-        middle_ref[:, :width] = middle
-        hat, _ = standardise(middle)
-        second_ref[:, :width] = (
-            hat * vector(vec_ref, kind, 5) + vector(vec_ref, kind, 6)
-        ).astype(LOW)
-        put_rows(mixture_ref, pl.ds(12 * SEQS, SEQS), top_scr[:, :width])
-        put_rows(mixture_ref, pl.ds(13 * SEQS, SEQS), mixed.astype(WIDE))
-
-    each_tower(answer)
-    embed.finish()
-    rise.finish()
-    fall_own.wait()
-    remote(
-        reduce_block, reduce_ref.at[1 - core], reduce_sems.at[0], reduce_sems.at[1], sibling
-    ).wait_recv()
-    mask_own.wait()
-    for k, home in enumerate(homes):
-        source = (me + 31 - k) % 32
-        remote(
-            valid_ref, pairs_ref.at[source], valid_send.at[k], valid_recv.at[k], home
-        ).wait_recv()
-    for copy in [*masks, fall]:
-        copy.wait_send()
-    for group in (pair, ask, mix, embed, rise, *deals):
-        group.drain()
-
-
 def expand_matrix(ref, kind):
-    return ref[:, : kind.block, : kind.part].reshape(kind.width, kind.part)
+    return jnp.concatenate(
+        [ref[at % 2, at // 2, : kind.block, : kind.part] for at in range(16)], axis=0
+    )
 
 
 def reduce_matrix(ref, kind):
@@ -923,9 +708,9 @@
         bias_ref[0:1, :part] = jnp.sum(low_grad.astype(WIDE), axis=0, keepdims=True)
         back = dot_nt(low_grad, expand_matrix(raise_ref, kind))
         back_ref[:, :, :width] = back.reshape(8, SEQS, width).astype(LOW)
-        raise_grad_ref[:, : kind.block, :part] = (
-            dot_tn(rows, low_grad).reshape(16, kind.block, part).astype(LOW)
-        )
+        raise_grad = dot_tn(rows, low_grad).reshape(16, kind.block, part).astype(LOW)
+        for at in range(16):
+            raise_grad_ref[at % 2, at // 2, : kind.block, :part] = raise_grad[at]
         whole[:part, :width] = dot_tn(active, grads)
         core = lax.axis_index("dp") % 2
         n = kind.reduce_rows
@@ -984,7 +769,11 @@
     img, txt = ordered(0), ordered(1)
     total = img.shape[0]
     scale = jnp.exp(jnp.full((1, 1), scale_ref[0], WIDE))
-    allowed = valid_ref[...].reshape(total, total) > 0
+    lines = []
+    for d in range(32):
+        rows = valid_ref[d % 2, d // 2].astype(WIDE)
+        lines.append(jnp.concatenate([rows[:8], rows[8:]], axis=1))
+    allowed = jnp.concatenate(lines, axis=0) > 0
     same = lax.broadcasted_iota(jnp.int32, (total, total), 0) == lax.broadcasted_iota(
         jnp.int32, (total, total), 1
     )
@@ -1045,18 +834,55 @@
     each_tower(run)
 
 
-def centre_kernel(
+def step_kernel(
+    plans,
+    ends_ref,
     scale_ref,
+    img_src,
+    txt_src,
+    valid_ref,
+    img_own,
+    txt_own,
+    loss_ref,
+    scale_new_ref,
+    img_keep,
+    txt_keep,
+    img_chunks,
+    txt_chunks,
     second_ref,
     middle_ref,
-    emb_weight_ref,
+    query_ref,
+    keyed_ref,
+    mixture_ref,
+    weight_ref,
+    first_ref,
+    img_in,
+    txt_in,
+    ask_ref,
+    mix_ref,
+    emb_ref,
     vec_ref,
     raise_ref,
     reduce_ref,
-    valid_ref,
-    loss_ref,
-    scale_new_ref,
-    final_grad_ref,
+    pairs_ref,
+    img_slots,
+    txt_slots,
+    img_extra,
+    txt_extra,
+    img_last,
+    txt_last,
+    flat,
+    ask_block,
+    mix_block,
+    emb_block,
+    raise_block,
+    reduce_block,
+    mask_block,
+    top_scr,
+    at_scr,
+    score_scr,
+    low_scr,
+    grad_ref,
     pooled_ref,
     proj_grad_ref,
     final_vec_ref,
@@ -1070,7 +896,7 @@
     parts,
     raised,
     emb,
-    embs,
+    all_embs,
     final,
     proj,
     low,
@@ -1078,37 +904,310 @@
     back,
     own_scr,
     whole,
-    send_sems,
-    recv_sems,
-    spread_send,
-    spread_recv,
-    core_sems,
+    img_send,
+    txt_send,
+    img_home,
+    txt_home,
+    rows_grad,
+    middle_scr,
+    second_scr,
+    valued_scr,
+    turn_scr,
+    shared_scr,
+    slope_scr,
+    left_scr,
+    left_block,
+    turn_block,
+    left_all,
+    turn_all,
+    early_block,
+    early_all,
+    late_block,
+    late_all,
+    lines_block,
+    lines_all,
+    raise_half,
+    risen_block,
+    raise_all,
+    reduce_in,
+    img_home_slots,
+    txt_home_slots,
+    gains,
+    top_grad_scr,
+    deal_send,
+    deal_recv,
+    deal_edge,
+    deal_fetch,
+    ask_send,
+    ask_recv,
+    mix_send,
+    mix_recv,
+    emb_send,
+    emb_recv,
+    raise_send,
+    raise_recv,
+    reduce_sems,
+    pair_sems,
+    mask_send,
+    mask_recv,
+    group_send,
+    group_recv,
+    embs_send,
+    embs_recv,
+    home_sems,
+    risen_send,
+    risen_recv,
+    left_send,
+    left_recv,
+    turn_send,
+    turn_recv,
+    early_send,
+    early_recv,
+    late_send,
+    late_recv,
+    lines_send,
+    lines_recv,
+    home_pair_sems,
+    collect_send,
+    collect_recv,
 ):
     tower, at = here()
-    greet([*both_towers(tower, at), (tower, at + 1 - at % 2 * 2)])
-    sent = []
-    sent += group_exchange(False, second_ref, seconds, send_sems.at[0], recv_sems.at[0])
+    core = at % 2
+    me = tower * 16 + at
+    sibling = (tower, at + 1 - 2 * core)
+    greet(everyone(tower, at))
+    deal_sems = (deal_send, deal_recv, deal_edge, deal_fetch)
+    deals = [
+        Deal(plans[0], 0, img_src, img_slots, img_extra, img_last, deal_sems),
+        Deal(plans[1], 1, txt_src, txt_slots, txt_extra, txt_last, deal_sems),
+    ]
+    pair = Pair(txt_own, txt_in, img_own, img_in, pair_sems)
+    ask = Ring(ask_block, ask_ref, ask_send, ask_recv)
+    mix = Ring(mix_block, mix_ref, mix_send, mix_recv)
+    embed = Ring(emb_block, emb_ref, emb_send, emb_recv)
+    rise = Group(raise_block, raise_ref, raise_send, raise_recv)
+    fall = remote(
+        reduce_block, reduce_ref.at[core], reduce_sems.at[0], reduce_sems.at[1], sibling
+    )
+    fall_own = pltpu.make_async_copy(reduce_block, reduce_ref.at[core], reduce_sems.at[2])
+    masks = Spread(mask_block, pairs_ref, mask_send, mask_recv)
+    rows = valid_ref[...].astype(WIDE)
+    mask_block[...] = jnp.concatenate([rows[:, :LANES], rows[:, LANES:]], axis=0).astype(LOW)
+
+    for deal in deals:
+        deal.send_head()
+        deal.start_fetch()
+        deal.vectors(False)
+    for deal in deals:
+        deal.whole(True, False)
+    pair.start()
+    for deal in deals:
+        deal.join()
+
+    def lift_to(kind, p, ref, start):
+        slots = (img_slots, txt_slots)[kind.index]
+        for c, value in lift(kind, plans[kind.index], p, slots, flat):
+            lane = start + c * LANES
+            ref[: value.shape[0], lane : lane + LANES] = value.astype(ref.dtype)
+
+    def normalise(kind, half):
+        width, room = kind.width, kind.room
+        own, arrived = ((img_own, img_in), (txt_own, txt_in))[kind.index]
+        ref = own if half == kind.index else arrived
+        gain, shift = vector(vec_ref, kind, 0), vector(vec_ref, kind, 1)
+        positions = lax.broadcasted_iota(jnp.int32, (room, 1), 0)
+        for i in range(8):
+            rows = ref[i].astype(WIDE)
+            hat, _ = standardise(rows)
+            first = (hat * gain + shift).astype(LOW)
+            s = half * 8 + i
+            first_ref[s, :room, :width] = first
+            if kind.causal:
+                chosen = positions == ends_ref[(half * 16 + at) * 8 + i]
+                top = jnp.sum(jnp.where(chosen, first.astype(WIDE), 0.0), axis=0, keepdims=True)
+                raw = jnp.sum(jnp.where(chosen, rows, 0.0), axis=0, keepdims=True)
+            else:
+                top, raw = first[:1].astype(WIDE), rows[:1]
+            top_scr[s : s + 1, :width] = top
+            at_scr[s : s + 1, :width] = raw
+
+    def begin(kind):
+        deal = deals[kind.index]
+        deal.arrived(VECTORS)
+        lift_to(kind, VECTORS, vec_ref, 0)
+        normalise(kind, kind.index)
+
+    each_tower(begin)
+
+    def place_inputs(kind):
+        deals[kind.index].arrived(0)
+        slots = (img_slots, txt_slots)[kind.index]
+        per = kind.width // LANES
+        for c, value in lift(kind, plans[kind.index], 0, slots, flat):
+            lane = c // per * WIDTH + c % per * LANES
+            ref = ask_block
+            if lane >= 2 * WIDTH:
+                ref, lane = mix_block, lane - 2 * WIDTH
+            ref[: value.shape[0], lane : lane + LANES] = value.astype(LOW)
+
+    each_tower(place_inputs)
+    ask.start()
+
+    def place_rest(kind):
+        deals[kind.index].arrived(1)
+        lift_to(kind, 1, mix_block, WIDTH)
+        deals[kind.index].arrived(4)
+        lift_to(kind, 4, emb_block, 0)
+
+    each_tower(place_rest)
+    mix.start()
+    embed.start()
+    for deal in deals:
+        deal.whole(False, False)
+    pair.finish()
+    each_tower(lambda kind: normalise(kind, 1 - kind.index))
+    masks.start()
+    ask.relay_deep()
+    ask.relay_row()
+    ask.finish()
+
+    def question(kind):
+        width = kind.width
+        tops = top_scr[:, :width].astype(LOW)
+        query = dot_nn(tops, matrix(ask_ref, kind, 0, width)) + vector(vec_ref, kind, 2)
+        query = query.astype(LOW)
+        query_ref[:, :width] = query
+        for span in spans(kind):
+            lo, hi, first_head, n = span
+            put_rows(
+                keyed_ref,
+                pl.ds(first_head * SEQS, n * SEQS),
+                dot_nt(head_rows(query, span), matrix(ask_ref, kind, WIDTH + lo, hi - lo)) * 0.125,
+            )
+        dead = (HEADS - kind.heads) * SEQS
+        put_rows(keyed_ref, pl.ds(kind.heads * SEQS, dead), jnp.zeros((dead, width), WIDE))
+
+    each_tower(question)
+    mix.relay_deep()
+    embed.relay_deep()
+
+    def score(kind):
+        width, room = kind.width, kind.room
+        lane = lax.broadcasted_iota(jnp.int32, (HEADS, room), 1)
+        for s in range(SEQS):
+            keys = get_rows(keyed_ref, pl.ds(s, HEADS, stride=SEQS), width).astype(LOW)
+            scores = dot_nt(keys, first_ref[s, :room, :width])
+            if kind.causal:
+                allowed = lane <= ends_ref[(s // 8 * 16 + at) * 8 + s % 8]
+            else:
+                allowed = lane < kind.length
+            score_scr[s * HEADS : (s + 1) * HEADS, :room] = jnp.where(allowed, scores, -1e30)
+        scores = score_scr[:, :room]
+        raw = jnp.exp(scores - jnp.max(scores, axis=-1, keepdims=True))
+        weights = raw / jnp.sum(raw, axis=-1, keepdims=True)
+        head = lax.broadcasted_iota(jnp.int32, (SEQS * HEADS, 1), 0) % HEADS
+        weights = jnp.where(head < kind.heads, weights, 0.0)
+        weight_ref[:, :room] = weights
+        low_scr[: SEQS * HEADS, :room] = weights.astype(LOW)
+
+    each_tower(score)
+    mix.relay_row()
+    embed.relay_row()
+
+    def mixture(kind):
+        width, room = kind.width, kind.room
+        for s in range(SEQS):
+            mixed = dot_nn(
+                low_scr[s * HEADS : (s + 1) * HEADS, :room], first_ref[s, :room, :width]
+            )
+            put_rows(mixture_ref, pl.ds(s, HEADS, stride=SEQS), mixed)
+        totals = jnp.sum(
+            low_scr[: SEQS * HEADS, :room].astype(WIDE), axis=-1, keepdims=True
+        )
+        score_scr[...] = jnp.broadcast_to(totals, score_scr.shape)
+
+    each_tower(mixture)
+
+    def place_hidden(kind):
+        deal, plan = deals[kind.index], plans[kind.index]
+        slots = (img_slots, txt_slots)[kind.index]
+        deal.arrived(2)
+        per = kind.part // LANES
+        for c, value in lift(kind, plan, 2, slots, flat):
+            lane = c % per * LANES
+            raise_block[c // per, : kind.block, lane : lane + LANES] = value.astype(LOW)
+        deal.arrived(3)
+        lift_to(kind, 3, reduce_block, 0)
+
+    each_tower(place_hidden)
+    rise.start()
+    fall.start()
+    fall_own.start()
+    mix.finish()
+
+    def answer(kind):
+        width = kind.width
+        mixed = []
+        bias = vector(vec_ref, kind, 3)
+        for span in spans(kind):
+            lo, hi, first_head, n = span
+            z = get_rows(mixture_ref, pl.ds(first_head * SEQS, n * SEQS), width).astype(LOW)
+            valued = dot_nn(z, matrix(mix_ref, kind, lo, hi - lo))
+            totals = jnp.concatenate(
+                [score_scr[pl.ds(first_head + h, SEQS, stride=HEADS), 0:1] for h in range(n)],
+                axis=0,
+            )
+            mixed.append(from_head_rows(valued + totals * bias[:, lo:hi], span))
+        mixed = side_by_side(mixed).astype(LOW)
+        middle = (
+            at_scr[:, :width]
+            + dot_nn(mixed, matrix(mix_ref, kind, WIDTH, width))
+            + vector(vec_ref, kind, 4)
+        )
+        middle_ref[:, :width] = middle
+        hat, _ = standardise(middle)
+        second_ref[:, :width] = (
+            hat * vector(vec_ref, kind, 5) + vector(vec_ref, kind, 6)
+        ).astype(LOW)
+        put_rows(mixture_ref, pl.ds(12 * SEQS, SEQS), top_scr[:, :width])
+        put_rows(mixture_ref, pl.ds(13 * SEQS, SEQS), mixed.astype(WIDE))
+
+    each_tower(answer)
+    rise.relay()
+    masks.relay()
+    embed.finish()
+    rise.finish()
+    fall_own.wait()
+    remote(
+        reduce_block, reduce_ref.at[1 - core], reduce_sems.at[0], reduce_sems.at[1], sibling
+    ).wait_recv()
+
+    sent = group_exchange(False, second_ref, seconds, group_send.at[0], group_recv.at[0])
     hidden_kernel(seconds, raise_ref, reduce_ref, vec_ref, part, raised)
-    sent += group_exchange(True, part, parts, send_sems.at[1], recv_sems.at[1])
-    embed_kernel(parts, middle_ref, emb_weight_ref, vec_ref, emb, final, pooled_ref, proj)
-    sent += spread(emb, embs, spread_send, spread_recv, core_sems)
+    sent += group_exchange(True, part, parts, group_send.at[1], group_recv.at[1])
+    embed_kernel(parts, middle_ref, emb_ref, vec_ref, emb, final, pooled_ref, proj)
+    embs = Spread(emb, all_embs, embs_send, embs_recv)
+    embs.start()
+    masks.finish()
+    embs.relay()
+    embs.finish()
     objective_kernel(
         scale_ref,
-        embs,
-        valid_ref,
+        all_embs,
+        pairs_ref,
         final,
         proj,
-        emb_weight_ref,
+        emb_ref,
         vec_ref,
         low,
-        final_grad_ref,
+        grad_ref,
         proj_grad_ref,
         final_vec_ref,
         loss_ref,
         scale_new_ref,
         own_scr,
     )
-    sent += group_exchange(False, low, lows, send_sems.at[2], recv_sems.at[2])
+    sent += group_exchange(False, low, lows, group_send.at[2], group_recv.at[2])
     hidden_back_kernel(
         lows,
         seconds,
@@ -1122,104 +1221,24 @@
         bias_ref,
         whole,
     )
-    sent += group_exchange(True, back, backs_ref, send_sems.at[3], recv_sems.at[3])
-    for copy in sent:
-        copy.wait_send()
-
-
-def back_kernel(
-    plans,
-    ends_ref,
-    img_own,
-    img_in,
-    txt_own,
-    txt_in,
-    first_ref,
-    ask_ref,
-    mix_ref,
-    vec_ref,
-    backs_ref,
-    grad_ref,
-    middle_ref,
-    query_ref,
-    keyed_ref,
-    mixture_ref,
-    weight_ref,
-    pooled_ref,
-    proj_grad_ref,
-    final_vec_ref,
-    bias_ref,
-    raise_grad_ref,
-    reduce_keep_ref,
-    reduce_send_ref,
-    img_keep,
-    txt_keep,
-    img_chunks,
-    txt_chunks,
-    img_send,
-    txt_send,
-    img_home,
-    txt_home,
-    rows_grad,
-    middle_scr,
-    second_scr,
-    valued_scr,
-    turn_scr,
-    shared_scr,
-    slope_scr,
-    low_scr,
-    left_scr,
-    left_block,
-    turn_block,
-    left_all,
-    turn_all,
-    early_block,
-    early_all,
-    late_block,
-    late_all,
-    lines_block,
-    lines_all,
-    raise_all,
-    reduce_in,
-    flat,
-    img_slots,
-    txt_slots,
-    gains,
-    top_grad_scr,
-    raise_send,
-    raise_recv,
-    reduce_sems,
-    left_send,
-    left_recv,
-    turn_send,
-    turn_recv,
-    early_send,
-    early_recv,
-    late_send,
-    late_recv,
-    lines_send,
-    lines_recv,
-    pair_sems,
-    collect_send,
-    collect_recv,
-):
-    tower, at = here()
-    core = at % 2
-    sibling = (tower, at + 1 - 2 * core)
-    greet(everyone(tower, at))
-    rise = Blocks(raise_grad_ref, raise_all, raise_send, raise_recv)
-    fall = remote(reduce_send_ref, reduce_in, reduce_sems.at[0], reduce_sems.at[1], sibling)
+    sent += group_exchange(True, back, backs_ref, group_send.at[3], group_recv.at[3])
+    halves = remote(
+        raise_grad_ref.at[1 - core], raise_half, home_sems.at[0], home_sems.at[1], sibling
+    )
+    fallen = remote(reduce_send_ref, reduce_in, home_sems.at[2], home_sems.at[3], sibling)
+    halves.start()
+    fallen.start()
+    risen_group = Group(risen_block, raise_all, risen_send, risen_recv, False)
+
     lefts = Blocks(left_block, left_all, left_send, left_recv)
     turns = Blocks(turn_block, turn_all, turn_send, turn_recv)
     early = Ring(early_block, early_all, early_send, early_recv)
     late = Ring(late_block, late_all, late_send, late_recv)
-    pair = Pair(img_send, img_home, txt_send, txt_home, pair_sems)
+    home_pair = Pair(img_send, img_home, txt_send, txt_home, home_pair_sems)
     collects = [
-        Collect(plans[0], 0, img_slots, img_chunks, collect_send.at[0], collect_recv),
-        Collect(plans[1], 1, txt_slots, txt_chunks, collect_send.at[1], collect_recv),
+        Collect(plans[0], 0, img_home_slots, img_chunks, collect_send.at[0], collect_recv),
+        Collect(plans[1], 1, txt_home_slots, txt_chunks, collect_send.at[1], collect_recv),
     ]
-    rise.start()
-    fall.start()
 
     def outputs(kind):
         width = kind.width
@@ -1266,6 +1285,11 @@
             shared_scr[place, :] = jnp.broadcast_to(constant, (n * SEQS, LANES))
 
     each_tower(values)
+    halves.wait_recv()
+    risen_block[...] = (
+        raise_grad_ref[core].astype(WIDE) + raise_half[...].astype(WIDE)
+    ).astype(LOW)
+    risen_group.start()
 
     def slopes(kind):
         width, room = kind.width, kind.room
@@ -1350,14 +1374,12 @@
         gains[1:2, :width] += shift_sum
 
     each_tower(lambda kind: finish(kind, 1 - kind.index))
-    pair.start()
-    rise.finish()
-    remote(
-        reduce_send_ref, reduce_in, reduce_sems.at[0], reduce_sems.at[1], sibling
-    ).wait_recv()
+    home_pair.start()
+    risen_group.finish()
+    fallen.wait_recv()
 
     def slots_of(kind):
-        return (img_slots, txt_slots)[kind.index]
+        return (img_home_slots, txt_home_slots)[kind.index]
 
     def hidden_grads(kind):
         plan, collect = plans[kind.index], collects[kind.index]
@@ -1365,9 +1387,7 @@
 
         def risen(c):
             chip, lane = c // per, c % per * LANES
-            return raise_all[2 * chip, :block, lane : lane + LANES].astype(WIDE) + raise_all[
-                2 * chip + 1, :block, lane : lane + LANES
-            ].astype(WIDE)
+            return raise_all[chip, :block, lane : lane + LANES].astype(WIDE)
 
         def fallen(c):
             lane = c * LANES
@@ -1535,7 +1555,7 @@
         each_tower(vectors)
 
     each_tower(lambda kind: collects[kind.index].piece(VECTORS, False))
-    pair.finish()
+    home_pair.finish()
 
     @pl.when(tower == 1)
     def _():
@@ -1547,9 +1567,12 @@
 
     for collect in collects:
         collect.finish()
-    fall.wait_send()
+    for copy in (*sent, fall, fallen, halves):
+        copy.wait_send()
     pl.when(at > 0)(line_copy.wait_send)
-    for group in (rise, lefts, turns, early, late, pair):
+    for group in (pair, ask, mix, embed, rise, masks, embs, *deals):
+        group.drain()
+    for group in (risen_group, lefts, turns, early, late, home_pair):
         group.drain()
 
     def drain(kind):
@@ -1557,22 +1580,6 @@
             collects[kind.index].piece(p, True)
 
     each_tower(drain)
-
-
-def dma(*shape):
-    return pltpu.SemaphoreType.DMA(shape)
-
-
-def call(kernel, number, operands, outs, scratch, semaphores):
-    spec = {"vmem": pltpu.VMEM, "smem": pltpu.SMEM, "any": pl.ANY}
-    return pl.pallas_call(
-        kernel,
-        out_shape=[jax.ShapeDtypeStruct(shape, dtype) for _, shape, dtype in outs],
-        in_specs=[pl.BlockSpec(memory_space=spec[place]) for place, _ in operands],
-        out_specs=[pl.BlockSpec(memory_space=spec[place]) for place, _, _ in outs],
-        scratch_shapes=[pltpu.VMEM(shape, dtype) for shape, dtype in scratch] + semaphores,
-        compiler_params=comm_params(number),
-    )(*[value for _, value in operands])
 
 
 ROWS_LOW = ((SEQS, WIDTH), LOW)
@@ -1580,22 +1587,23 @@
 HEAD_ROWS = ((WIDTH // LANES, SEQS * HEADS, LANES), WIDE)
 LANE_ROWS = ((SEQS * HEADS, LANES), WIDE)
 GROUP = ((8, SEQS, WIDTH), LOW)
+HIDDEN_BLOCKS = ((2, 8, 48, PART), LOW)
+OUTER = ((16, 48, SEQS * HEADS), LOW)
 
 
 def chunk_shapes(plan, n):
     return ((n, plan.rows, LANES), LOW)
 
 
-def front(txt_ends, img_chunks, txt_chunks, valid, img_rows, txt_rows, plans, number):
-    operands = [
-        ("smem", txt_ends),
-        ("any", img_chunks),
-        ("any", txt_chunks),
-        ("vmem", valid),
-        ("vmem", img_rows),
-        ("vmem", txt_rows),
+def run_step(scalars, chunks, valid, tokens, plans):
+    most = max(plan.local for plan in plans) + 17
+    slots = max(plan.slots for plan in plans)
+    edges = [((plan.rows, LANES), LOW) for plan in plans]
+    rooms = [((8, kind.room, kind.width), LOW) for kind in TOWERS]
+    outs = [((8, kind.length, kind.width), WIDE) for kind in TOWERS] + [
+        chunk_shapes(plan, plan.local) for plan in plans
     ]
-    outs = [
+    scratch = [
         ROWS_LOW,
         ROWS_WIDE,
         ROWS_LOW,
@@ -1603,71 +1611,41 @@
         HEAD_ROWS,
         LANE_ROWS,
         ((SEQS, ROOM, WIDTH), LOW),
-        (img_rows.shape, LOW),
-        (txt_rows.shape, LOW),
+        rooms[0],
+        rooms[1],
         ((16, 48, 2 * WIDTH), LOW),
         ((16, 48, 2 * WIDTH), LOW),
         ((16, 48, EMB), LOW),
         ROWS_WIDE,
-        ((16, 48, PART), LOW),
+        HIDDEN_BLOCKS,
         ((2, 192, WIDTH), LOW),
-        ((32, *valid.shape), valid.dtype),
-    ]
-    chunks = [chunk_shapes(plan, 1) for plan in plans]
-    edges = [(shape[1:], dtype) for shape, dtype in chunks]
-    scratch = [
-        *[chunk_shapes(plan, plan.slots) for plan in plans],
-        *edges,
-        *edges,
+        ((2, 16, 16, LANES), LOW),
+        chunk_shapes(plans[0], plans[0].slots),
+        chunk_shapes(plans[1], plans[1].slots),
+        edges[0],
+        edges[1],
+        edges[0],
+        edges[1],
         ((plans[0].slots * plans[0].rows, LANES), WIDE),
         ((48, 2 * WIDTH), LOW),
         ((48, 2 * WIDTH), LOW),
         ((48, EMB), LOW),
         ((8, 48, PART), LOW),
         ((192, WIDTH), LOW),
+        ((16, LANES), LOW),
         ROWS_WIDE,
         ROWS_WIDE,
         LANE_ROWS,
-        ((SEQS * HEADS, LANES), LOW),
-    ]
-    most = max(plan.local for plan in plans) + 17
-    semaphores = [
-        dma(2, most),
-        dma(2, 6),
-        dma(2, 2),
-        dma(2),
-        *[dma(16), dma(15)] * 4,
-        dma(3),
-        dma(2),
-        dma(32),
-        dma(31),
-    ]
-    return call(
-        functools.partial(front_kernel, plans),
-        number,
-        operands,
-        [("vmem", *out) for out in outs],
-        scratch,
-        semaphores,
-    )
-
-
-def centre(scale_state, second, middle, emb_weight, vec, rise, fall, pairs, number):
-    operands = [("smem", scale_state)] + [
-        ("vmem", value) for value in (second, middle, emb_weight, vec, rise, fall, pairs)
-    ]
-    outs = [
+        ((2 * SEQS * HEADS, LANES), LOW),
         ROWS_WIDE,
         ROWS_LOW,
         ((SEQS, EMB), LOW),
         ((8, WIDTH), WIDE),
-        ((16, 48, PART), LOW),
+        HIDDEN_BLOCKS,
         ((192, WIDTH), WIDE),
         ((192, WIDTH), LOW),
         ((8, PART), WIDE),
         GROUP,
-    ]
-    scratch = [
         GROUP,
         GROUP,
         GROUP,
@@ -1681,27 +1659,10 @@
         GROUP,
         ((256, EMB), WIDE),
         ((PART, WIDTH), WIDE),
-    ]
-    return call(
-        centre_kernel,
-        number,
-        operands,
-        [("smem", (1,), WIDE), ("smem", (3,), WIDE)] + [("vmem", *out) for out in outs],
-        scratch,
-        [dma(4, 8), dma(4, 7), dma(16), dma(15), dma(2)],
-    )
-
-
-def back(txt_ends, values, plans, number):
-    operands = [("smem", txt_ends)] + [("vmem", value) for value in values]
-    rooms = [((8, kind.room, kind.width), LOW) for kind in TOWERS]
-    outs = [((8, kind.length, kind.width), WIDE) for kind in TOWERS] + [
-        chunk_shapes(plan, plan.local) for plan in plans
-    ]
-    blocks = ((16, 48, 256), LOW)
-    scratch = [
-        *rooms,
-        *rooms,
+        rooms[0],
+        rooms[1],
+        rooms[0],
+        rooms[1],
         ((SEQS, ROOM, WIDTH), WIDE),
         ROWS_WIDE,
         ROWS_WIDE,
@@ -1709,45 +1670,76 @@
         HEAD_ROWS,
         LANE_ROWS,
         LANE_ROWS,
-        ((2 * SEQS * HEADS, LANES), LOW),
         ((SEQS * HEADS, WIDTH), WIDE),
-        blocks,
-        blocks,
-        blocks,
-        blocks,
+        OUTER,
+        OUTER,
+        OUTER,
+        OUTER,
         ((SEQS, 3 * WIDTH + EMB), LOW),
         ((16, SEQS, 3 * WIDTH + EMB), LOW),
         ROWS_LOW,
         ((16, SEQS, WIDTH), LOW),
         ROWS_WIDE,
         ((16, SEQS, WIDTH), WIDE),
-        ((16, 48, PART), LOW),
+        ((8, 48, PART), LOW),
+        ((8, 48, PART), LOW),
+        ((8, 48, PART), LOW),
         ((192, WIDTH), LOW),
-        ((plans[0].slots * plans[0].rows, LANES), WIDE),
-        *[chunk_shapes(plan, plan.slots) for plan in plans],
+        chunk_shapes(plans[0], plans[0].slots),
+        chunk_shapes(plans[1], plans[1].slots),
         ((8, WIDTH), WIDE),
         ROWS_WIDE,
     ]
-    most = max(plan.slots for plan in plans)
     semaphores = [
-        dma(16),
-        dma(15),
-        dma(2),
-        *[dma(16), dma(15)] * 4,
-        dma(1),
-        dma(16),
-        dma(2),
-        dma(2, 2, most),
-        dma(2),
+        (2, most,),
+        (2, 6,),
+        (2, 2,),
+        (2,),
+        (16,),
+        (15,),
+        (16,),
+        (15,),
+        (16,),
+        (15,),
+        (9,),
+        (8,),
+        (3,),
+        (2,),
+        (17,),
+        (16,),
+        (4, 8,),
+        (4, 7,),
+        (17,),
+        (16,),
+        (4,),
+        (9,),
+        (8,),
+        (16,),
+        (15,),
+        (16,),
+        (15,),
+        (16,),
+        (15,),
+        (16,),
+        (15,),
+        (1,),
+        (16,),
+        (2,),
+        (2, 2, slots,),
+        (2,),
     ]
-    return call(
-        functools.partial(back_kernel, plans),
-        number,
-        operands,
-        [("vmem", *out) for out in outs],
-        scratch,
-        semaphores,
-    )
+    smem = pl.BlockSpec(memory_space=pltpu.SMEM)
+    vmem = pl.BlockSpec(memory_space=pltpu.VMEM)
+    like = jax.ShapeDtypeStruct
+    return pl.pallas_call(
+        functools.partial(step_kernel, plans),
+        out_shape=[like((1,), WIDE), like((3,), WIDE)] + [like(*out) for out in outs],
+        in_specs=[smem, smem, ANY, ANY, vmem, vmem, vmem],
+        out_specs=[smem, smem, vmem, vmem, vmem, vmem],
+        scratch_shapes=[pltpu.VMEM(*each) for each in scratch]
+        + [pltpu.SemaphoreType.DMA(shape) for shape in semaphores],
+        compiler_params=comm_params(0),
+    )(*scalars, *chunks, valid, *tokens)
 
 
 def to_chunks(flat, plan, me):
@@ -1782,74 +1774,12 @@
     )
     img_rows = jnp.pad(img_tokens, ((0, 0), (0, TOWERS[0].room - TOWERS[0].length), (0, 0)))
     txt_rows = jnp.pad(txt_tokens, ((0, 0), (0, TOWERS[1].room - TOWERS[1].length), (0, 0)))
-    (
-        second,
-        middle,
-        query,
-        keyed,
-        mixture,
-        weights,
-        first,
-        img_in,
-        txt_in,
-        ask,
-        mix,
-        emb_weight,
-        vec,
-        rise,
-        fall,
-        pairs,
-    ) = front(
-        txt_ends,
-        to_chunks(img_master, plans[0], me),
-        to_chunks(txt_master, plans[1], me),
+    loss, scale_new, img_grad, txt_grad, img_chunks, txt_chunks = run_step(
+        (txt_ends, scale_state),
+        (to_chunks(img_master, plans[0], me), to_chunks(txt_master, plans[1], me)),
         valid,
-        img_rows,
-        txt_rows,
+        (img_rows, txt_rows),
         plans,
-        0,
-    )
-    (
-        loss,
-        scale_new,
-        final_grad,
-        pooled,
-        proj_grad,
-        final_vec,
-        rise_grad,
-        fall_keep,
-        fall_send,
-        bias_grad,
-        backs,
-    ) = centre(scale_state, second, middle, emb_weight, vec, rise, fall, pairs, 1)
-    img_grad, txt_grad, img_chunks, txt_chunks = back(
-        txt_ends,
-        [
-            img_rows,
-            img_in,
-            txt_rows,
-            txt_in,
-            first,
-            ask,
-            mix,
-            vec,
-            backs,
-            final_grad,
-            middle,
-            query,
-            keyed,
-            mixture,
-            weights,
-            pooled,
-            proj_grad,
-            final_vec,
-            bias_grad,
-            rise_grad,
-            fall_keep,
-            fall_send,
-        ],
-        plans,
-        2,
     )
     img_new = advance(
         img_master, img_moment, img_average, from_chunks(img_chunks, plans[0], me), step_rate

time: 248 us -> 215 us (0.87)
  the two profiles are of different devices: /device:TPU:3 before, /device:TPU:9 now
where the time goes in v4:
time: 215 us
  Pallas kernels  196 us (91%)
  local copies, waits for them, and re-layouts  11.7 us (5%)
  other arithmetic  4.63 us (2%)
  between operations  2.62 us (1%)
    pallas_call x1, Pallas kernels, run_step(): pl.pallas_call(functools.partial(step_kernel, plans), out_shape=[like((1,...  196 us
    unnamed x33, local copies, waits for them, and re-layouts  5.56 us
    convert_element_type x2, local copies, waits for them, and re-layouts, to_chunks(): return piece.astype(LOW).reshape(plan.local, plan.rows, LANES)  4.34 us

profile of v4, /device:TPU:9, one launch (start us, length us, event | category | flops | bytes accessed | tf_op | source)
XLA Modules:
  0.0 214.7 jit_solution(9801951951230324906)
XLA Ops:
  0.6 0.0 copy-start.7
  0.7 2.0 fusion.3
  2.7 2.4 %fusion = bf16[245760]{0:T(1024)(128)(2,1)} fusion(s32[]{:T(128)S(6)} %select_n.28, f32[233808]{0:T(1024)} %param.15), kind=kLoop, calls=%fused_computation.3 | loop fusion | bytes 1426756 | tf_op jit(solution)/shard_map/convert_element_type | solution.py:1749
  5.0 0.0 copy-done.7
  5.0 0.2 copy.24
  5.2 0.9 pad.19.txt_own
  6.1 0.0 copy-done.8
  6.1 0.1 copy.23
  6.3 0.9 pad.18.img_own
  7.2 195.7 %shard_map.202 = (f32[1]{0:T(128)}, f32[3]{0:T(128)}, f32[8,50,768]{2,1,0:T(8,128)}, f32[8,77,512]{2,1,0:T(8,128)}, bf16[20,96,128]{2,1,0:T(8,128)(2,1)}, /*index=5*/bf16[14,64,128]{2,1,0:T(8,128)(2,1)}) custom-call(s32[256]{0:T(256)} %ends_ref.1, f32[3]{0:T(128)} %scale_ref.1, bf16[20,96,128]{2,1,0:T(8,128)(2,1)} %bitcast.5, bf16[14,64,128]{2,1,0:T(8,128)(2,1)} %bitcast.6, ...), custom_call_target="tpu_custom_call" | custom-call | tf_op jit(solution)/shard_map/pallas_call | solution.py:1734
  202.9 0.0 copy-start.3
  202.9 0.0 copy-start.11
  203.0 0.0 copy-start.12
  203.0 2.9 %copy.25 = f32[8,50,768]{2,0,1:T(8,128)} copy(f32[8,50,768]{2,1,0:T(8,128)} %get-tuple-element.25) | data formatting | bytes 2457600
  205.8 0.0 copy-done.3
  205.8 0.0 copy-done.11
  205.8 0.0 copy-done.12
  205.8 0.0 copy-start.10
  205.8 0.0 copy-start.4
  205.8 1.0 fusion.6
  206.9 0.0 copy-done.10
  206.9 0.9 add_multiply_fusion.1
  207.8 0.0 copy-done.4
  207.8 1.8 copy.26
  209.6 0.0 copy-done.2
  209.6 0.0 copy-done
  209.6 0.0 copy-done.5
  209.6 0.0 copy-start.6
  209.6 1.5 fusion.8
  211.1 1.2 add_multiply_fusion
  212.3 0.1 copy-done.1
  213.1 0.5 copy.30
  (10 shorter events, 0.0 us)
Async XLA Ops:
  0.6 4.4 %copy-start.7 = (bf16[8,77,512]{2,0,1:T(8,128)(2,1)S(1)}, bf16[8,77,512]{2,0,1:T(8,128)(2,1)}, u32[]{:S(2)}) copy-start(bf16[8,77,512]{2,0,1:T(8,128)(2,1)} %param.12) | copy-start | bytes 1892356
  5.0 1.1 copy-start.8
  202.9 2.9 %copy-start.3 = (f32[106720]{0:T(1024)S(1)}, f32[106720]{0:T(1024)}, u32[]{:S(2)}) copy-start(f32[106720]{0:T(1024)} %param.18) | copy-start | bytes 1280644
  202.9 2.9 %copy-start.11 = (f32[106720]{0:T(1024)S(1)}, f32[106720]{0:T(1024)}, u32[]{:S(2)}) copy-start(f32[106720]{0:T(1024)} %param.19) | copy-start | bytes 1280644
  203.0 2.9 %copy-start.12 = (bf16[14,64,128]{2,1,0:T(8,128)(2,1)S(1)}, bf16[14,64,128]{2,1,0:T(8,128)(2,1)}, u32[]{:S(2)}) copy-start(bf16[14,64,128]{2,1,0:T(8,128)(2,1)} %get-tuple-element.22) | copy-start | bytes 688132
  205.8 1.1 copy-start.10
  205.8 1.9 copy-start.4
  206.9 2.7 %copy-start.2 = (f32[106720]{0:T(1024)}, f32[106720]{0:T(1024)S(1)}, u32[]{:S(2)}) copy-start(f32[106720]{0:T(1024)S(1)} %get-tuple-element.61) | copy-start | bytes 1280644
  207.8 1.8 copy-start
  207.8 1.8 copy-start.5
  207.8 1.8 copy-start.9
  209.6 1.5 copy-start.6
  211.1 1.2 copy-start.1
  211.1 1.9 copy-start.13

commit v5 on v4

--- a/solution.py
+++ b/solution.py
@@ -193,8 +193,9 @@
 
 
 class Ring:
-    def __init__(self, src, dst, send, recv):
+    def __init__(self, src, dst, send, recv, only=None):
         self.src, self.dst, self.send, self.recv = src, dst, send, recv
+        self.only = only
         self.tower, self.at = here()
         self.deep, self.row, self.core = self.at // 4, self.at // 2 % 2, self.at % 2
         self.sibling = (self.tower, self.at + 1 - 2 * self.core)
@@ -204,15 +205,22 @@
     def spot(self, k, row):
         return (self.deep + k) % 4 * 4 + row * 2 + self.core
 
+    def act(self, action):
+        if self.only is None:
+            action()
+        else:
+            pl.when(self.tower == self.only)(action)
+
     def launch(self, src, slot, index, device):
         copy = remote(src, self.dst.at[slot], self.send.at[index], self.recv.at[index], device)
-        copy.start()
+        self.act(copy.start)
         self.sent.append(copy)
 
     def arrived(self, slot, index):
-        remote(
+        copy = remote(
             self.src, self.dst.at[slot], self.send.at[index], self.recv.at[index], self.sibling
-        ).wait_recv()
+        )
+        self.act(copy.wait_recv)
 
     def start(self):
         for k in (1, 3, 2):
@@ -220,7 +228,7 @@
         self.launch(self.src, self.at, 3, self.beside)
         self.launch(self.src, self.at, 7, self.sibling)
         self.own = pltpu.make_async_copy(self.src, self.dst.at[self.at], self.send.at[15])
-        self.own.start()
+        self.act(self.own.start)
 
     def relay_deep(self):
         for k in (1, 3, 2):
@@ -240,11 +248,18 @@
             k, row = index % 4, self.row if index < 4 else 1 - self.row
             slot = (self.deep + 4 - k) % 4 * 4 + row * 2 + 1 - self.core
             self.arrived(slot, 7 + index)
-        self.own.wait()
+        self.act(self.own.wait)
 
     def drain(self):
         for copy in self.sent:
-            copy.wait_send()
+            self.act(copy.wait_send)
+
+
+def rings(src, dst, send, recv):
+    return [
+        Ring(src.at[part], dst.at[part], send.at[part], recv.at[part], 0 if part == 2 else None)
+        for part in range(3)
+    ]
 
 
 class Blocks:
@@ -310,6 +325,8 @@
 
 
 VECTORS = 5
+EXPAND = 2
+TURN = 8
 
 
 class Plan:
@@ -348,8 +365,9 @@
             base = jnp.where(inside, self.first_chunk[p], base)
             slot = jnp.where(inside, self.first_slot[p], slot)
             n = jnp.where(inside, self.per_device[p], n)
-        at = (g - base) // n
-        return piece, at, slot + (g - base) - at * n
+        block = (g - base) // n
+        at = jnp.where(piece == EXPAND, (block + TURN) % 16, block)
+        return piece, at, slot + (g - base) - block * n
 
 
 class Deal:
@@ -480,7 +498,8 @@
 
         def step(i, carry):
             slot = self.plan.first_slot[p] + i
-            g = self.plan.first_chunk[p] + self.at * n + i if p < VECTORS else self.plan.total - 1
+            block = (self.at + 16 - TURN) % 16 if p == EXPAND else self.at
+            g = self.plan.first_chunk[p] + block * n + i if p < VECTORS else self.plan.total - 1
             low = g * self.plan.chunk // self.plan.share
             high = jnp.minimum(((g + 1) * self.plan.chunk - 1) // self.plan.share, 31)
             self.one(low, slot, g, 0, wait)
@@ -607,7 +626,14 @@
 
 
 def matrix(ref, kind, start, width):
-    return ref[:, : kind.block, start : start + width].reshape(kind.width, width)
+    return jnp.concatenate(
+        [
+            ref[part, at, :, start : start + width]
+            for at in range(16)
+            for part in range(kind.block // 16)
+        ],
+        axis=0,
+    )
 
 
 def vector(vec_ref, kind, row):
@@ -651,7 +677,11 @@
 
 def expand_matrix(ref, kind):
     return jnp.concatenate(
-        [ref[at % 2, at // 2, : kind.block, : kind.part] for at in range(16)], axis=0
+        [
+            ref[at % 2, at // 2, : kind.block, : kind.part]
+            for at in ((block + TURN) % 16 for block in range(16))
+        ],
+        axis=0,
     )
 
 
@@ -709,8 +739,9 @@
         back = dot_nt(low_grad, expand_matrix(raise_ref, kind))
         back_ref[:, :, :width] = back.reshape(8, SEQS, width).astype(LOW)
         raise_grad = dot_tn(rows, low_grad).reshape(16, kind.block, part).astype(LOW)
-        for at in range(16):
-            raise_grad_ref[at % 2, at // 2, : kind.block, :part] = raise_grad[at]
+        for block in range(16):
+            at = (block + TURN) % 16
+            raise_grad_ref[at % 2, at // 2, : kind.block, :part] = raise_grad[block]
         whole[:part, :width] = dot_tn(active, grads)
         core = lax.axis_index("dp") % 2
         n = kind.reduce_rows
@@ -982,9 +1013,9 @@
         Deal(plans[1], 1, txt_src, txt_slots, txt_extra, txt_last, deal_sems),
     ]
     pair = Pair(txt_own, txt_in, img_own, img_in, pair_sems)
-    ask = Ring(ask_block, ask_ref, ask_send, ask_recv)
-    mix = Ring(mix_block, mix_ref, mix_send, mix_recv)
-    embed = Ring(emb_block, emb_ref, emb_send, emb_recv)
+    asks = rings(ask_block, ask_ref, ask_send, ask_recv)
+    mixes = rings(mix_block, mix_ref, mix_send, mix_recv)
+    embeds = rings(emb_block, emb_ref, emb_send, emb_recv)
     rise = Group(raise_block, raise_ref, raise_send, raise_recv)
     fall = remote(
         reduce_block, reduce_ref.at[core], reduce_sems.at[0], reduce_sems.at[1], sibling
@@ -1000,15 +1031,24 @@
         deal.vectors(False)
     for deal in deals:
         deal.whole(True, False)
+    for deal in deals:
+        deal.whole(False, False)
     pair.start()
     for deal in deals:
         deal.join()
+
+    def put(ref, lane, value):
+        if len(ref.shape) == 2:
+            ref[: value.shape[0], lane : lane + LANES] = value
+        else:
+            for part in range(value.shape[0] // 16):
+                ref[part, :, lane : lane + LANES] = value[part * 16 : (part + 1) * 16]
 
     def lift_to(kind, p, ref, start):
         slots = (img_slots, txt_slots)[kind.index]
         for c, value in lift(kind, plans[kind.index], p, slots, flat):
             lane = start + c * LANES
-            ref[: value.shape[0], lane : lane + LANES] = value.astype(ref.dtype)
+            put(ref, lane, value.astype(ref.dtype))
 
     def normalise(kind, half):
         width, room = kind.width, kind.room
@@ -1048,10 +1088,22 @@
             ref = ask_block
             if lane >= 2 * WIDTH:
                 ref, lane = mix_block, lane - 2 * WIDTH
-            ref[: value.shape[0], lane : lane + LANES] = value.astype(LOW)
+            put(ref, lane, value.astype(LOW))
 
     each_tower(place_inputs)
-    ask.start()
+    for ring in asks:
+        ring.start()
+
+    def place_hidden(kind):
+        deal, plan = deals[kind.index], plans[kind.index]
+        slots = (img_slots, txt_slots)[kind.index]
+        deal.arrived(2)
+        per = kind.part // LANES
+        for c, value in lift(kind, plan, 2, slots, flat):
+            lane = c % per * LANES
+            raise_block[c // per, : kind.block, lane : lane + LANES] = value.astype(LOW)
+        deal.arrived(3)
+        lift_to(kind, 3, reduce_block, 0)
 
     def place_rest(kind):
         deals[kind.index].arrived(1)
@@ -1060,16 +1112,22 @@
         lift_to(kind, 4, emb_block, 0)
 
     each_tower(place_rest)
-    mix.start()
-    embed.start()
-    for deal in deals:
-        deal.whole(False, False)
+    each_tower(place_hidden)
+    rise.start()
+    fall.start()
+    fall_own.start()
     pair.finish()
     each_tower(lambda kind: normalise(kind, 1 - kind.index))
     masks.start()
-    ask.relay_deep()
-    ask.relay_row()
-    ask.finish()
+    for ask, mix in zip(asks, mixes):
+        ask.relay_deep()
+        mix.start()
+    for embed in embeds:
+        embed.start()
+    for ask in asks:
+        ask.relay_row()
+    for ask in asks:
+        ask.finish()
 
     def question(kind):
         width = kind.width
@@ -1088,8 +1146,8 @@
         put_rows(keyed_ref, pl.ds(kind.heads * SEQS, dead), jnp.zeros((dead, width), WIDE))
 
     each_tower(question)
-    mix.relay_deep()
-    embed.relay_deep()
+    for ring in (*mixes, *embeds):
+        ring.relay_deep()
 
     def score(kind):
         width, room = kind.width, kind.room
@@ -1111,8 +1169,8 @@
         low_scr[: SEQS * HEADS, :room] = weights.astype(LOW)
 
     each_tower(score)
-    mix.relay_row()
-    embed.relay_row()
+    for ring in (*mixes, *embeds):
+        ring.relay_row()
 
     def mixture(kind):
         width, room = kind.width, kind.room
@@ -1128,22 +1186,8 @@
 
     each_tower(mixture)
 
-    def place_hidden(kind):
-        deal, plan = deals[kind.index], plans[kind.index]
-        slots = (img_slots, txt_slots)[kind.index]
-        deal.arrived(2)
-        per = kind.part // LANES
-        for c, value in lift(kind, plan, 2, slots, flat):
-            lane = c % per * LANES
-            raise_block[c // per, : kind.block, lane : lane + LANES] = value.astype(LOW)
-        deal.arrived(3)
-        lift_to(kind, 3, reduce_block, 0)
-
-    each_tower(place_hidden)
-    rise.start()
-    fall.start()
-    fall_own.start()
-    mix.finish()
+    for mix in mixes:
+        mix.finish()
 
     def answer(kind):
         width = kind.width
@@ -1175,7 +1219,8 @@
     each_tower(answer)
     rise.relay()
     masks.relay()
-    embed.finish()
+    for embed in embeds:
+        embed.finish()
     rise.finish()
     fall_own.wait()
     remote(
@@ -1570,7 +1615,7 @@
     for copy in (*sent, fall, fallen, halves):
         copy.wait_send()
     pl.when(at > 0)(line_copy.wait_send)
-    for group in (pair, ask, mix, embed, rise, masks, embs, *deals):
+    for group in (pair, *asks, *mixes, *embeds, rise, masks, embs, *deals):
         group.drain()
     for group in (risen_group, lefts, turns, early, late, home_pair):
         group.drain()
@@ -1613,9 +1658,9 @@
         ((SEQS, ROOM, WIDTH), LOW),
         rooms[0],
         rooms[1],
-        ((16, 48, 2 * WIDTH), LOW),
-        ((16, 48, 2 * WIDTH), LOW),
-        ((16, 48, EMB), LOW),
+        ((3, 16, 16, 2 * WIDTH), LOW),
+        ((3, 16, 16, 2 * WIDTH), LOW),
+        ((3, 16, 16, EMB), LOW),
         ROWS_WIDE,
         HIDDEN_BLOCKS,
         ((2, 192, WIDTH), LOW),
@@ -1627,9 +1672,9 @@
         edges[0],
         edges[1],
         ((plans[0].slots * plans[0].rows, LANES), WIDE),
-        ((48, 2 * WIDTH), LOW),
-        ((48, 2 * WIDTH), LOW),
-        ((48, EMB), LOW),
+        ((3, 16, 2 * WIDTH), LOW),
+        ((3, 16, 2 * WIDTH), LOW),
+        ((3, 16, EMB), LOW),
         ((8, 48, PART), LOW),
         ((192, WIDTH), LOW),
         ((16, LANES), LOW),
@@ -1695,12 +1740,12 @@
         (2, 6,),
         (2, 2,),
         (2,),
-        (16,),
-        (15,),
-        (16,),
-        (15,),
-        (16,),
-        (15,),
+        (3, 16),
+        (3, 15),
+        (3, 16),
+        (3, 15),
+        (3, 16),
+        (3, 15),
         (9,),
         (8,),
         (3,),

time: 215 us -> 195 us (0.907)
  the two profiles are of different devices: /device:TPU:9 before, /device:TPU:3 now
where the time goes in v5:
time: 195 us; the launch traced here: 193 us
  Pallas kernels  174 us (89%)
  local copies, waits for them, and re-layouts  11.7 us (6%)
  other arithmetic  4.63 us (2%)
  between operations  2.62 us (1%)
    pallas_call x1, Pallas kernels, run_step(): pl.pallas_call(functools.partial(step_kernel, plans), out_shape=[like((1,...  174 us
    unnamed x33, local copies, waits for them, and re-layouts  5.56 us
    convert_element_type x2, local copies, waits for them, and re-layouts, to_chunks(): return piece.astype(LOW).reshape(plan.local, plan.rows, LANES)  4.34 us

profile of v5, /device:TPU:3, one launch (start us, length us, event | category | flops | bytes accessed | tf_op | source)
XLA Modules:
  0.0 193.3 jit_solution(16717577408566220878)
XLA Ops:
  0.6 0.0 copy-start.7
  0.7 2.0 %fusion.3 = bf16[114688]{0:T(1024)(128)(2,1)} fusion(s32[]{:T(128)S(6)} %select_n.30, f32[106720]{0:T(1024)} %param.18), kind=kLoop, calls=%fused_computation.10 | loop fusion | bytes 656260 | tf_op jit(solution)/shard_map/convert_element_type | solution.py:1794
  2.7 2.4 %fusion = bf16[245760]{0:T(1024)(128)(2,1)} fusion(s32[]{:T(128)S(6)} %select_n.28, f32[233808]{0:T(1024)} %param.15), kind=kLoop, calls=%fused_computation.3 | loop fusion | bytes 1426756 | tf_op jit(solution)/shard_map/convert_element_type | solution.py:1794
  5.0 0.0 copy-done.7
  5.0 0.2 copy.24
  5.2 0.9 pad.19.txt_own
  6.1 0.0 copy-done.8
  6.1 0.1 copy.23
  6.3 0.9 pad.18.img_own
  7.2 174.3 %shard_map.202 = (f32[1]{0:T(128)}, f32[3]{0:T(128)}, f32[8,50,768]{2,1,0:T(8,128)}, f32[8,77,512]{2,1,0:T(8,128)}, bf16[20,96,128]{2,1,0:T(8,128)(2,1)}, /*index=5*/bf16[14,64,128]{2,1,0:T(8,128)(2,1)}) custom-call(s32[256]{0:T(256)} %ends_ref.1, f32[3]{0:T(128)} %scale_ref.1, bf16[20,96,128]{2,1,0:T(8,128)(2,1)} %bitcast.5, bf16[14,64,128]{2,1,0:T(8,128)(2,1)} %bitcast.6, ...), custom_call_target="tpu_custom_call" | custom-call | tf_op jit(solution)/shard_map/pallas_call | solution.py:1779
  181.5 0.0 copy-start.3
  181.5 0.0 copy-start.11
  181.6 0.0 copy-start.12
  181.6 2.9 %copy.25 = f32[8,50,768]{2,0,1:T(8,128)} copy(f32[8,50,768]{2,1,0:T(8,128)} %get-tuple-element.25) | data formatting | bytes 2457600
  184.4 0.0 copy-done.3
  184.4 0.0 copy-done.11
  184.4 0.0 copy-done.12
  184.4 0.0 copy-start.10
  184.4 0.0 copy-start.4
  184.5 1.0 fusion.6
  185.5 0.0 copy-done.10
  185.5 0.9 add_multiply_fusion.1
  186.4 0.0 copy-done.4
  186.4 1.8 copy.26
  188.2 0.0 copy-done.2
  188.2 0.0 copy-done
  188.2 0.0 copy-done.5
  188.2 0.0 copy-start.6
  188.2 1.5 fusion.8
  189.7 1.2 add_multiply_fusion
  190.9 0.1 copy-done.1
  191.7 0.5 copy.30
  (10 shorter events, 0.0 us)
Async XLA Ops:
  0.6 4.4 %copy-start.7 = (bf16[8,77,512]{2,0,1:T(8,128)(2,1)S(1)}, bf16[8,77,512]{2,0,1:T(8,128)(2,1)}, u32[]{:S(2)}) copy-start(bf16[8,77,512]{2,0,1:T(8,128)(2,1)} %param.12) | copy-start | bytes 1892356
  5.0 1.1 copy-start.8
  181.5 2.9 %copy-start.3 = (f32[106720]{0:T(1024)S(1)}, f32[106720]{0:T(1024)}, u32[]{:S(2)}) copy-start(f32[106720]{0:T(1024)} %param.18) | copy-start | bytes 1280644
  181.5 2.9 %copy-start.11 = (f32[106720]{0:T(1024)S(1)}, f32[106720]{0:T(1024)}, u32[]{:S(2)}) copy-start(f32[106720]{0:T(1024)} %param.19) | copy-start | bytes 1280644
  181.6 2.9 %copy-start.12 = (bf16[14,64,128]{2,1,0:T(8,128)(2,1)S(1)}, bf16[14,64,128]{2,1,0:T(8,128)(2,1)}, u32[]{:S(2)}) copy-start(bf16[14,64,128]{2,1,0:T(8,128)(2,1)} %get-tuple-element.22) | copy-start | bytes 688132
  184.4 1.1 copy-start.10
  184.4 1.9 %copy-start.4 = (f32[8,77,512]{2,1,0:T(8,128)S(1)}, f32[8,77,512]{2,1,0:T(8,128)}, u32[]{:S(2)}) copy-start(f32[8,77,512]{2,1,0:T(8,128)} %get-tuple-element.26) | copy-start | bytes 3784708
  185.5 2.7 %copy-start.2 = (f32[106720]{0:T(1024)}, f32[106720]{0:T(1024)S(1)}, u32[]{:S(2)}) copy-start(f32[106720]{0:T(1024)S(1)} %get-tuple-element.61) | copy-start | bytes 1280644
  186.4 1.8 copy-start
  186.4 1.8 copy-start.5
  186.4 1.8 copy-start.9
  188.2 1.5 copy-start.6
  189.7 1.2 copy-start.1
  189.7 1.9 copy-start.13

commit v6 on v5

--- a/solution.py
+++ b/solution.py
@@ -255,9 +255,86 @@
             self.act(copy.wait_send)
 
 
-def rings(src, dst, send, recv):
+class Chain:
+    def __init__(self, src, dst, send, recv, only=None):
+        self.src, self.dst, self.send, self.recv = src, dst, send, recv
+        self.only = only
+        self.tower, self.at = here()
+        self.deep, self.row, self.core = self.at // 4, self.at // 2 % 2, self.at % 2
+        self.mate = self.deep + 1 - 2 * (self.deep % 2)
+        self.half = self.deep // 2
+        self.inner = jnp.logical_or(self.deep == 1, self.deep == 2)
+        self.sibling = (self.tower, self.at + 1 - 2 * self.core)
+        self.beside = (self.tower, self.spot(self.deep, 1 - self.row))
+        self.sent = []
+
+    def spot(self, deep, row):
+        return deep * 4 + row * 2 + self.core
+
+    def sources(self):
+        return self.deep, self.mate, 2 - 2 * self.half, 3 - 2 * self.half
+
+    def act(self, action, when=None):
+        if self.only is not None:
+            right = self.tower == self.only
+            when = right if when is None else jnp.logical_and(when, right)
+        if when is None:
+            action()
+        else:
+            pl.when(when)(action)
+
+    def launch(self, src, slot, sent, landed, device, when=None):
+        copy = remote(src, self.dst.at[slot], self.send.at[sent], self.recv.at[landed], device)
+        self.act(copy.start, when)
+        self.sent.append((copy, when))
+
+    def arrived(self, slot, index):
+        copy = remote(
+            self.src, self.dst.at[slot], self.send.at[0], self.recv.at[index], self.sibling
+        )
+        self.act(copy.wait_recv)
+
+    def start(self):
+        mate = (self.tower, self.spot(self.mate, self.row))
+        far = (self.tower, self.spot(2 - self.half, self.row))
+        self.launch(self.src, self.at, 1, 1 + self.deep % 2, far)
+        self.launch(self.src, self.at, 0, 0, mate)
+        self.launch(self.src, self.at, 2, 3, self.beside)
+        self.launch(self.src, self.at, 3, 7, self.sibling)
+        self.own = pltpu.make_async_copy(self.src, self.dst.at[self.at], self.send.at[16])
+        self.act(self.own.start)
+
+    def relay_deep(self):
+        mate = (self.tower, self.spot(self.mate, self.row))
+        for k in (1, 2, 3):
+            slot = self.spot(self.sources()[k], self.row)
+            self.arrived(slot, k - 1)
+            block = self.dst.at[slot]
+            if k > 1:
+                self.launch(block, slot, 4 + k, k - 1, mate, self.inner)
+            self.launch(block, slot, 7 + k, 3 + k, self.beside)
+            self.launch(block, slot, 16 + k, 7 + k, self.sibling)
+
+    def relay_row(self):
+        for k, deep in enumerate(self.sources()):
+            slot = self.spot(deep, 1 - self.row)
+            self.arrived(slot, 3 + k)
+            self.launch(self.dst.at[slot], slot, 11 + k, 11 + k, self.sibling)
+
+    def finish(self):
+        for k, deep in enumerate(self.sources()):
+            for row, base in ((self.row, 7), (1 - self.row, 11)):
+                self.arrived(deep * 4 + row * 2 + 1 - self.core, base + k)
+        self.act(self.own.wait)
+
+    def drain(self):
+        for copy, when in self.sent:
+            self.act(copy.wait_send, when)
+
+
+def rings(src, dst, send, recv, way=Ring):
     return [
-        Ring(src.at[part], dst.at[part], send.at[part], recv.at[part], 0 if part == 2 else None)
+        way(src.at[part], dst.at[part], send.at[part], recv.at[part], 0 if part == 2 else None)
         for part in range(3)
     ]
 
@@ -532,12 +609,13 @@
 
 
 class Tower:
-    def __init__(self, index, width, hidden, length, room, causal):
+    def __init__(self, index, width, hidden, length, room, run, causal):
         self.index = index
         self.width = width
         self.hidden = hidden
         self.length = length
         self.room = room
+        self.run = run
         self.causal = causal
         self.heads = width // HEAD
         self.block = width // 16
@@ -546,8 +624,8 @@
 
 
 TOWERS = (
-    Tower(0, D_IMG, FF_IMG, 50, 64, False),
-    Tower(1, D_TXT, FF_TXT, 77, 80, True),
+    Tower(0, D_IMG, FF_IMG, 50, 64, 10, False),
+    Tower(1, D_TXT, FF_TXT, 77, 80, 11, True),
 )
 ROOM = 80
 WIDTH = D_IMG
@@ -887,6 +965,7 @@
     mixture_ref,
     weight_ref,
     first_ref,
+    first_rows,
     img_in,
     txt_in,
     ask_ref,
@@ -1015,7 +1094,7 @@
     pair = Pair(txt_own, txt_in, img_own, img_in, pair_sems)
     asks = rings(ask_block, ask_ref, ask_send, ask_recv)
     mixes = rings(mix_block, mix_ref, mix_send, mix_recv)
-    embeds = rings(emb_block, emb_ref, emb_send, emb_recv)
+    embeds = rings(emb_block, emb_ref, emb_send, emb_recv, Chain)
     rise = Group(raise_block, raise_ref, raise_send, raise_recv)
     fall = remote(
         reduce_block, reduce_ref.at[core], reduce_sems.at[0], reduce_sems.at[1], sibling
@@ -1050,26 +1129,44 @@
             lane = start + c * LANES
             put(ref, lane, value.astype(ref.dtype))
 
+    def tokens_of(kind, half):
+        own, arrived = ((img_own, img_in), (txt_own, txt_in))[kind.index]
+        return own if half == kind.index else arrived
+
+    def steps(kind):
+        return [(t, kind.run) for t in range(0, kind.length, kind.run)]
+
+    def is_end(kind, half, t, n):
+        row = lax.broadcasted_iota(jnp.int32, (8, 1), 0)
+        ends = jnp.zeros((8, 1), jnp.int32)
+        for i in range(8):
+            ends = jnp.where(row == i, ends_ref[(half * 16 + at) * 8 + i], ends)
+        position = lax.broadcasted_iota(jnp.int32, (n, 8, 1), 0) + t
+        return (position == ends[None]).astype(WIDE)
+
     def normalise(kind, half):
         width, room = kind.width, kind.room
-        own, arrived = ((img_own, img_in), (txt_own, txt_in))[kind.index]
-        ref = own if half == kind.index else arrived
+        ref = tokens_of(kind, half)
         gain, shift = vector(vec_ref, kind, 0), vector(vec_ref, kind, 1)
-        positions = lax.broadcasted_iota(jnp.int32, (room, 1), 0)
+        tops, raws = jnp.zeros((8, width), WIDE), jnp.zeros((8, width), WIDE)
+        for t, n in steps(kind):
+            rows = ref[t : t + n].astype(WIDE).reshape(n * 8, width)
+            hat, _ = standardise(rows)
+            first = (hat * gain + shift).astype(LOW).astype(WIDE)
+            put_rows(first_rows, pl.ds(t * 8, n * 8), first)
+            if kind.causal:
+                chosen = is_end(kind, half, t, n)
+                tops = tops + jnp.sum(first.reshape(n, 8, width) * chosen, axis=0)
+                raws = raws + jnp.sum(rows.reshape(n, 8, width) * chosen, axis=0)
+            elif t == 0:
+                tops, raws = first[:8], rows[:8]
+        top_scr[half * 8 : half * 8 + 8, :width] = tops
+        at_scr[half * 8 : half * 8 + 8, :width] = raws
+        spare = (room - kind.length) * 8
+        put_rows(first_rows, pl.ds(kind.length * 8, spare), jnp.zeros((spare, width), WIDE))
         for i in range(8):
-            rows = ref[i].astype(WIDE)
-            hat, _ = standardise(rows)
-            first = (hat * gain + shift).astype(LOW)
-            s = half * 8 + i
-            first_ref[s, :room, :width] = first
-            if kind.causal:
-                chosen = positions == ends_ref[(half * 16 + at) * 8 + i]
-                top = jnp.sum(jnp.where(chosen, first.astype(WIDE), 0.0), axis=0, keepdims=True)
-                raw = jnp.sum(jnp.where(chosen, rows, 0.0), axis=0, keepdims=True)
-            else:
-                top, raw = first[:1].astype(WIDE), rows[:1]
-            top_scr[s : s + 1, :width] = top
-            at_scr[s : s + 1, :width] = raw
+            line = get_rows(first_rows, pl.ds(i, room, stride=8), width)
+            first_ref[half * 8 + i, :room, :width] = line.astype(LOW)
 
     def begin(kind):
         deal = deals[kind.index]
@@ -1112,22 +1209,6 @@
         lift_to(kind, 4, emb_block, 0)
 
     each_tower(place_rest)
-    each_tower(place_hidden)
-    rise.start()
-    fall.start()
-    fall_own.start()
-    pair.finish()
-    each_tower(lambda kind: normalise(kind, 1 - kind.index))
-    masks.start()
-    for ask, mix in zip(asks, mixes):
-        ask.relay_deep()
-        mix.start()
-    for embed in embeds:
-        embed.start()
-    for ask in asks:
-        ask.relay_row()
-    for ask in asks:
-        ask.finish()
 
     def question(kind):
         width = kind.width
@@ -1145,6 +1226,22 @@
         dead = (HEADS - kind.heads) * SEQS
         put_rows(keyed_ref, pl.ds(kind.heads * SEQS, dead), jnp.zeros((dead, width), WIDE))
 
+    for ask, mix in zip(asks, mixes):
+        ask.relay_deep()
+        mix.start()
+    for embed in embeds:
+        embed.start()
+    for ask in asks:
+        ask.relay_row()
+    each_tower(place_hidden)
+    rise.start()
+    fall.start()
+    fall_own.start()
+    pair.finish()
+    each_tower(lambda kind: normalise(kind, 1 - kind.index))
+    masks.start()
+    for ask in asks:
+        ask.finish()
     each_tower(question)
     for ring in (*mixes, *embeds):
         ring.relay_deep()
@@ -1277,7 +1374,7 @@
 
     lefts = Blocks(left_block, left_all, left_send, left_recv)
     turns = Blocks(turn_block, turn_all, turn_send, turn_recv)
-    early = Ring(early_block, early_all, early_send, early_recv)
+    early = Chain(early_block, early_all, early_send, early_recv)
     late = Ring(late_block, late_all, late_send, late_recv)
     home_pair = Pair(img_send, img_home, txt_send, txt_home, home_pair_sems)
     collects = [
@@ -1365,7 +1462,11 @@
             right = jnp.concatenate(
                 [get_rows(keyed_ref, line, width), get_rows(valued_scr, line, width)], axis=0
             )
-            rows_grad[s, :room, :width] = dot_tn(both, right.astype(LOW))
+            put_rows(
+                rows_grad.at[s // 8],
+                pl.ds(s % 8, room, stride=8),
+                dot_tn(both, right.astype(LOW)),
+            )
 
     each_tower(tokens)
     early.relay_row()
@@ -1391,30 +1492,34 @@
     gains[...] = jnp.zeros_like(gains)
 
     def finish(kind, half):
-        width, room, length = kind.width, kind.room, kind.length
-        own, arrived = ((img_own, img_in), (txt_own, txt_in))[kind.index]
-        ref = own if half == kind.index else arrived
+        width = kind.width
+        ref = tokens_of(kind, half)
         keep, send = ((img_keep, img_send), (txt_keep, txt_send))[kind.index]
         gain = vector(vec_ref, kind, 0)
-        positions = lax.broadcasted_iota(jnp.int32, (room, 1), 0)
+        top = top_grad_scr[half * 8 : half * 8 + 8, :width]
+        low = middle_scr[half * 8 : half * 8 + 8, :width]
         gain_sum = jnp.zeros((1, width), WIDE)
         shift_sum = jnp.zeros((1, width), WIDE)
-        for i in range(8):
-            s = half * 8 + i
-            hat, rate = standardise(ref[i].astype(WIDE))
+        for t, n in steps(kind):
+            hat, rate = standardise(ref[t : t + n].astype(WIDE).reshape(n * 8, width))
+            grad = get_rows(rows_grad.at[half], pl.ds(t * 8, n * 8), width)
+            chosen = None
             if kind.causal:
-                chosen = positions == ends_ref[(half * 16 + at) * 8 + i]
-            else:
-                chosen = positions == 0
-            chosen = chosen.astype(WIDE)
-            grad = rows_grad[s, :room, :width] + chosen * top_grad_scr[s : s + 1, :width]
+                chosen = is_end(kind, half, t, n)
+            elif t == 0:
+                chosen = (lax.broadcasted_iota(jnp.int32, (n, 8, 1), 0) == 0).astype(WIDE)
+            if chosen is not None:
+                grad = grad + (chosen * top[None]).reshape(n * 8, width)
             gain_sum += jnp.sum(grad * hat, axis=0, keepdims=True)
             shift_sum += jnp.sum(grad, axis=0, keepdims=True)
-            result = norm_back(grad, gain, hat, rate) + chosen * middle_scr[s : s + 1, :width]
+            result = norm_back(grad, gain, hat, rate)
+            if chosen is not None:
+                result = result + (chosen * low[None]).reshape(n * 8, width)
+            result = result.reshape(n, 8, width)
             if half == kind.index:
-                keep[i] = result[:length]
+                keep[t : t + n] = result
             else:
-                send[i] = result.astype(LOW)
+                send[t : t + n] = result.astype(LOW)
         gains[0:1, :width] += gain_sum
         gains[1:2, :width] += shift_sum
 
@@ -1604,11 +1709,11 @@
 
     @pl.when(tower == 1)
     def _():
-        img_keep[...] = img_home[:, : TOWERS[0].length].astype(WIDE)
+        img_keep[...] = img_home[...].astype(WIDE)
 
     @pl.when(tower == 0)
     def _():
-        txt_keep[...] = txt_home[:, : TOWERS[1].length].astype(WIDE)
+        txt_keep[...] = txt_home[...].astype(WIDE)
 
     for collect in collects:
         collect.finish()
@@ -1644,8 +1749,8 @@
     most = max(plan.local for plan in plans) + 17
     slots = max(plan.slots for plan in plans)
     edges = [((plan.rows, LANES), LOW) for plan in plans]
-    rooms = [((8, kind.room, kind.width), LOW) for kind in TOWERS]
-    outs = [((8, kind.length, kind.width), WIDE) for kind in TOWERS] + [
+    rooms = [((kind.length, 8, kind.width), LOW) for kind in TOWERS]
+    outs = [((kind.length, 8, kind.width), WIDE) for kind in TOWERS] + [
         chunk_shapes(plan, plan.local) for plan in plans
     ]
     scratch = [
@@ -1656,6 +1761,7 @@
         HEAD_ROWS,
         LANE_ROWS,
         ((SEQS, ROOM, WIDTH), LOW),
+        ((WIDTH // LANES, ROOM * 8, LANES), WIDE),
         rooms[0],
         rooms[1],
         ((3, 16, 16, 2 * WIDTH), LOW),
@@ -1708,7 +1814,7 @@
         rooms[1],
         rooms[0],
         rooms[1],
-        ((SEQS, ROOM, WIDTH), WIDE),
+        ((2, WIDTH // LANES, ROOM * 8, LANES), WIDE),
         ROWS_WIDE,
         ROWS_WIDE,
         HEAD_ROWS,
@@ -1744,7 +1850,7 @@
         (3, 15),
         (3, 16),
         (3, 15),
-        (3, 16),
+        (3, 20),
         (3, 15),
         (9,),
         (8,),
@@ -1763,7 +1869,7 @@
         (15,),
         (16,),
         (15,),
-        (16,),
+        (20,),
         (15,),
         (16,),
         (15,),
@@ -1817,13 +1923,11 @@
         Plan(0, img_master.shape[0], 96, (9, 3, 12, 12, 2)),
         Plan(1, txt_master.shape[0], 64, (6, 2, 8, 8, 2)),
     )
-    img_rows = jnp.pad(img_tokens, ((0, 0), (0, TOWERS[0].room - TOWERS[0].length), (0, 0)))
-    txt_rows = jnp.pad(txt_tokens, ((0, 0), (0, TOWERS[1].room - TOWERS[1].length), (0, 0)))
     loss, scale_new, img_grad, txt_grad, img_chunks, txt_chunks = run_step(
         (txt_ends, scale_state),
         (to_chunks(img_master, plans[0], me), to_chunks(txt_master, plans[1], me)),
         valid,
-        (img_rows, txt_rows),
+        (jnp.transpose(img_tokens, (1, 0, 2)), jnp.transpose(txt_tokens, (1, 0, 2))),
         plans,
     )
     img_new = advance(
@@ -1834,8 +1938,8 @@
     )
     return (
         loss[0],
-        img_grad,
-        txt_grad,
+        jnp.transpose(img_grad, (1, 0, 2)),
+        jnp.transpose(txt_grad, (1, 0, 2)),
         img_new[0],
         img_new[1],
         img_new[2],

time: 195 us -> 184 us (0.944)
  Pallas kernels: 174 us -> 168 us
  local copies, waits for them, and re-layouts: 11.7 us -> 7.08 us
    pallas_call x1, Pallas kernels: 174 us -> 168 us  [run_step(): pl.pallas_call(functools.partial(step_kernel, plans), out_shape=[like((1,...]
    unnamed x33 -> x27, local copies, waits for them, and re-layouts: 5.56 us -> 2.8 us
where the time goes in v6:
time: 184 us; the launch traced here: 183 us
  Pallas kernels  168 us (91%)
  local copies, waits for them, and re-layouts  7.08 us (4%)
  other arithmetic  5.62 us (3%)
  between operations  2.65 us (1%)
    pallas_call x1, Pallas kernels, run_step(): pl.pallas_call(functools.partial(step_kernel, plans), out_shape=[like((1,...  168 us
    convert_element_type x2, local copies, waits for them, and re-layouts, to_chunks(): return piece.astype(LOW).reshape(plan.local, plan.rows, LANES)  4.29 us

profile of v6, /device:TPU:3, one launch (start us, length us, event | category | flops | bytes accessed | tf_op | source)
XLA Modules:
  0.0 183.3 jit_solution(9643588424641528952)
XLA Ops:
  0.7 1.9 %fusion.3 = bf16[114688]{0:T(1024)(128)(2,1)} fusion(s32[]{:T(128)S(6)} %select_n.30, f32[106720]{0:T(1024)} %param.18), kind=kLoop, calls=%fused_computation.10 | loop fusion | bytes 656260 | tf_op jit(solution)/shard_map/convert_element_type | solution.py:1900
  2.6 2.4 %fusion = bf16[245760]{0:T(1024)(128)(2,1)} fusion(s32[]{:T(128)S(6)} %select_n.28, f32[233808]{0:T(1024)} %param.15), kind=kLoop, calls=%fused_computation.3 | loop fusion | bytes 1426756 | tf_op jit(solution)/shard_map/convert_element_type | solution.py:1900
  5.0 0.0 copy-start.3
  5.0 0.0 copy-start.10
  5.0 167.9 %shard_map.202 = (f32[1]{0:T(128)}, f32[3]{0:T(128)}, f32[50,8,768]{2,1,0:T(8,128)}, f32[77,8,512]{2,1,0:T(8,128)}, bf16[20,96,128]{2,1,0:T(8,128)(2,1)}, /*index=5*/bf16[14,64,128]{2,1,0:T(8,128)(2,1)}) custom-call(s32[256]{0:T(256)} %ends_ref.1, f32[3]{0:T(128)} %scale_ref.1, bf16[20,96,128]{2,1,0:T(8,128)(2,1)} %bitcast.9, bf16[14,64,128]{2,1,0:T(8,128)(2,1)} %bitcast.12, ...), custom_call_target="tpu_custom_call" | custom-call | tf_op jit(solution)/shard_map/pallas_call | solution.py:1885
  172.9 0.0 copy-start.9
  172.9 0.0 copy-done.3
  172.9 0.0 copy-done.10
  172.9 0.0 copy-start
  173.0 0.0 copy-start.6
  173.0 0.0 copy-start.8
  173.0 2.1 %fusion.6 = (bf16[106720]{0:T(1024)(128)(2,1)}, f32[106720]{0:T(1024)S(1)}, f32[106720]{0:T(1024)}) fusion(f32[106720]{0:T(1024)S(1)} %copy-done.3, bf16[114688]{0:T(1024)(128)(2,1)} %bitcast.16, s32[]{:T(128)S(6)} %select_n.32, f32[106720]{0:T(1024)S(1)} %copy-done.10), kind=kLoop, calls=%fused_computation.14 | loop fusion | flops 853760 | bytes 2134404 | tf_op jit(solution)/shard_map/convert_element_type | solution.py:1950
  175.1 0.0 copy-start.2
  175.1 0.0 copy-done.9
  175.1 0.9 add_multiply_fusion.1
  176.0 0.0 copy-done
  176.0 0.0 copy-done.6
  176.0 0.0 copy-done.8
  176.0 0.0 copy-start.7
  176.0 1.5 fusion.8
  177.6 0.0 copy-done.2
  177.6 0.0 copy-start.1
  177.6 0.0 copy-done.7
  177.6 0.0 copy-start.5
  177.6 1.1 add_multiply_fusion
  178.6 0.2 copy-done.1
  179.5 0.0 copy-done.5
  179.5 1.0 copy.28
  180.6 0.0 copy-done.4
  180.6 1.0 copy.29
  181.6 0.0 copy-done.11
  181.6 0.5 copy.30
  (2 shorter events, 0.0 us)
Async XLA Ops:
  5.0 167.9 %copy-start.3 = (f32[106720]{0:T(1024)S(1)}, f32[106720]{0:T(1024)}, u32[]{:S(2)}) copy-start(f32[106720]{0:T(1024)} %param.18) | copy-start | bytes 1280644
  5.0 168.0 %copy-start.10 = (f32[106720]{0:T(1024)S(1)}, f32[106720]{0:T(1024)}, u32[]{:S(2)}) copy-start(f32[106720]{0:T(1024)} %param.19) | copy-start | bytes 1280644
  172.9 2.2 %copy-start.9 = (f32[106720]{0:T(1024)S(1)}, f32[106720]{0:T(1024)}, u32[]{:S(2)}) copy-start(f32[106720]{0:T(1024)} %param.20) | copy-start | bytes 1280644
  172.9 3.1 %copy-start = (f32[233808]{0:T(1024)S(1)}, f32[233808]{0:T(1024)}, u32[]{:S(2)}) copy-start(f32[233808]{0:T(1024)} %param.15) | copy-start | bytes 2805700
  173.0 3.1 %copy-start.6 = (f32[233808]{0:T(1024)S(1)}, f32[233808]{0:T(1024)}, u32[]{:S(2)}) copy-start(f32[233808]{0:T(1024)} %param.16) | copy-start | bytes 2805700
  173.0 3.1 %copy-start.8 = (bf16[20,96,128]{2,1,0:T(8,128)(2,1)S(1)}, bf16[20,96,128]{2,1,0:T(8,128)(2,1)}, u32[]{:S(2)}) copy-start(bf16[20,96,128]{2,1,0:T(8,128)(2,1)} %get-tuple-element.21) | copy-start | bytes 1474564
  175.1 2.5 %copy-start.2 = (f32[106720]{0:T(1024)}, f32[106720]{0:T(1024)S(1)}, u32[]{:S(2)}) copy-start(f32[106720]{0:T(1024)S(1)} %get-tuple-element.49) | copy-start | bytes 1280644
  176.0 1.5 copy-start.7
  177.6 1.2 copy-start.1
  177.6 2.0 %copy-start.5 = (f32[50,8,768]{2,1,0:T(8,128)S(1)}, f32[50,8,768]{2,1,0:T(8,128)}, u32[]{:S(2)}) copy-start(f32[50,8,768]{2,1,0:T(8,128)} %get-tuple-element.19) | copy-start | bytes 3686404
  178.8 1.8 copy-start.4
  180.6 1.0 copy-start.11

commit v7 on v6

--- a/solution.py
+++ b/solution.py
@@ -447,25 +447,27 @@
         return piece, at, slot + (g - base) - block * n
 
 
+def before(me):
+    device = (me + 31) % 32
+    return device // 16, device % 16
+
+
 class Deal:
-    def __init__(self, plan, s, src, dst, extra, last, sems):
+    def __init__(self, plan, s, src, dst, extra, last, sems, only=None, me=None):
         self.plan, self.s, self.src, self.dst = plan, s, src, dst
         self.extra, self.last = extra, last
         self.chunk_send, self.recv, self.edge, self.fetch = sems
         self.tower, self.at = here()
-        self.me = self.tower * 16 + self.at
+        self.only = only
+        self.me = self.tower * 16 + self.at if me is None else me
         self.first, self.last_chunk = plan.bounds(self.me)
-        before = (self.me + 31) % 32
-        self.head = remote(
-            src.at[0], extra, self.edge.at[s, 0], self.edge.at[s, 1], (before // 16, before % 16)
-        )
-
-    def send_head(self):
-        pl.when(self.me > 0)(self.head.start)
+
+    def runs(self, condition):
+        return condition if self.only is None else jnp.logical_and(condition, self.tower == self.only)
 
     def move(self, src, i, piece, at_to, slot, wait):
         far = jnp.logical_or(self.tower != self.plan.tower, at_to != self.at)
-        recv = self.recv.at[self.s, piece]
+        recv = self.recv.at[self.plan.tower, piece]
         copy = remote(
             src,
             self.dst.at[slot],
@@ -495,7 +497,7 @@
                 hidden = jnp.logical_and(piece >= 2, piece <= 3)
                 inside = jnp.logical_and(inside, jnp.logical_not(hidden) if early else hidden)
 
-            @pl.when(inside)
+            @pl.when(self.runs(inside))
             def _():
                 self.move(self.src.at[i], i, piece, at_to, slot, wait)
 
@@ -504,7 +506,7 @@
         lax.fori_loop(0, self.plan.local, step, 0)
 
     def vectors(self, wait):
-        @pl.when(self.me == 31)
+        @pl.when(self.runs(self.me == 31))
         def _():
             src = self.src.at[self.last_chunk - self.first]
 
@@ -520,27 +522,33 @@
         )
 
     def join(self):
-        @pl.when(self.me < 31)
+        @pl.when(self.runs(self.me < 31))
         def _():
             self.fetch_last().wait()
-            self.head.wait_recv()
+            edge = self.edge
+            remote(
+                self.last,
+                self.extra,
+                edge.at[self.s, 0],
+                edge.at[self.s, 1],
+                (self.tower, self.at),
+            ).wait_recv()
             self.last[...] = self.last[...] + self.extra[...]
             piece, at_to, slot = self.plan.target(self.last_chunk)
             self.move(self.last, self.plan.local + 16, piece, at_to, slot, False)
 
     def start_fetch(self):
-        pl.when(self.me < 31)(self.fetch_last().start)
+        pl.when(self.runs(self.me < 31))(self.fetch_last().start)
 
     def arrived(self, p):
         part = self.dst.at[pl.ds(self.plan.first_slot[p], self.plan.pieces(p))]
-        pltpu.make_async_copy(part, part, self.recv.at[self.s, p]).wait()
+        pltpu.make_async_copy(part, part, self.recv.at[self.plan.tower, p]).wait()
 
     def drain(self):
-        pl.when(self.me > 0)(self.head.wait_send)
         self.whole(None, True)
         self.vectors(True)
 
-        @pl.when(self.me < 31)
+        @pl.when(self.runs(self.me < 31))
         def _():
             piece, at_to, slot = self.plan.target(self.last_chunk)
             self.move(self.last, self.plan.local + 16, piece, at_to, slot, True)
@@ -981,6 +989,9 @@
     txt_extra,
     img_last,
     txt_last,
+    txt_relay,
+    txt_over,
+    txt_ending,
     flat,
     ask_block,
     mix_block,
@@ -1048,6 +1059,7 @@
     deal_recv,
     deal_edge,
     deal_fetch,
+    relay_sems,
     ask_send,
     ask_recv,
     mix_send,
@@ -1089,8 +1101,19 @@
     deal_sems = (deal_send, deal_recv, deal_edge, deal_fetch)
     deals = [
         Deal(plans[0], 0, img_src, img_slots, img_extra, img_last, deal_sems),
-        Deal(plans[1], 1, txt_src, txt_slots, txt_extra, txt_last, deal_sems),
+        Deal(plans[1], 1, txt_src, txt_slots, txt_extra, txt_last, deal_sems, 1, 16 + at),
+        Deal(plans[1], 2, txt_relay, txt_slots, txt_over, txt_ending, deal_sems, 1, at),
     ]
+    relay = remote(txt_src, txt_relay, relay_sems.at[0], relay_sems.at[1], (1 - tower, at))
+    behind = (jnp.int32(1), (at + 15) % 16)
+    head = remote(img_src.at[0], img_extra, deal_edge.at[0, 0], deal_edge.at[0, 1], before(me))
+    kept = remote(txt_src.at[0], txt_extra, deal_edge.at[1, 0], deal_edge.at[1, 1], behind)
+    over = remote(txt_src.at[0], txt_over, deal_edge.at[2, 0], deal_edge.at[2, 1], behind)
+    heads = (
+        (me > 0, head),
+        (me > 16, kept),
+        (jnp.logical_and(me > 0, me <= 16), over),
+    )
     pair = Pair(txt_own, txt_in, img_own, img_in, pair_sems)
     asks = rings(ask_block, ask_ref, ask_send, ask_recv)
     mixes = rings(mix_block, mix_ref, mix_send, mix_recv)
@@ -1104,17 +1127,24 @@
     rows = valid_ref[...].astype(WIDE)
     mask_block[...] = jnp.concatenate([rows[:, :LANES], rows[:, LANES:]], axis=0).astype(LOW)
 
-    for deal in deals:
-        deal.send_head()
+    for when, copy in heads:
+        pl.when(when)(copy.start)
+    pl.when(tower == 0)(relay.start)
+    for deal in deals[:2]:
         deal.start_fetch()
         deal.vectors(False)
-    for deal in deals:
-        deal.whole(True, False)
-    for deal in deals:
-        deal.whole(False, False)
+    deals[0].whole(True, False)
+    deals[1].whole(True, False)
+    deals[0].whole(False, False)
+    deals[1].whole(False, False)
     pair.start()
-    for deal in deals:
-        deal.join()
+    deals[0].join()
+    deals[1].join()
+    pl.when(tower == 1)(relay.wait_recv)
+    deals[2].start_fetch()
+    deals[2].whole(True, False)
+    deals[2].join()
+    deals[2].whole(False, False)
 
     def put(ref, lane, value):
         if len(ref.shape) == 2:
@@ -1720,6 +1750,9 @@
     for copy in (*sent, fall, fallen, halves):
         copy.wait_send()
     pl.when(at > 0)(line_copy.wait_send)
+    for when, copy in heads:
+        pl.when(when)(copy.wait_send)
+    pl.when(tower == 0)(relay.wait_send)
     for group in (pair, *asks, *mixes, *embeds, rise, masks, embs, *deals):
         group.drain()
     for group in (risen_group, lefts, turns, early, late, home_pair):
@@ -1776,6 +1809,9 @@
         edges[0],
         edges[1],
         edges[0],
+        edges[1],
+        chunk_shapes(plans[1], plans[1].local),
+        edges[1],
         edges[1],
         ((plans[0].slots * plans[0].rows, LANES), WIDE),
         ((3, 16, 2 * WIDTH), LOW),
@@ -1842,9 +1878,10 @@
         ROWS_WIDE,
     ]
     semaphores = [
-        (2, most,),
+        (3, most),
         (2, 6,),
-        (2, 2,),
+        (3, 2),
+        (3,),
         (2,),
         (3, 16),
         (3, 15),

time: 184 us -> 175 us (0.951)
  Pallas kernels: 168 us -> 160 us
    pallas_call x1, Pallas kernels: 168 us -> 160 us  [run_step(): pl.pallas_call(functools.partial(step_kernel, plans), out_shape=[like((1,...]
where the time goes in v7:
time: 175 us
  Pallas kernels  160 us (91%)
  local copies, waits for them, and re-layouts  7.08 us (4%)
  other arithmetic  5.62 us (3%)
  between operations  2.65 us (2%)
    pallas_call x1, Pallas kernels, run_step(): pl.pallas_call(functools.partial(step_kernel, plans), out_shape=[like((1,...  160 us
    convert_element_type x2, local copies, waits for them, and re-layouts, to_chunks(): return piece.astype(LOW).reshape(plan.local, plan.rows, LANES)  4.29 us

profile of v7, /device:TPU:3, one launch (start us, length us, event | category | flops | bytes accessed | tf_op | source)
XLA Modules:
  0.0 175.1 jit_solution(5424656375452797723)
XLA Ops:
  0.7 1.9 %fusion.3 = bf16[114688]{0:T(1024)(128)(2,1)} fusion(s32[]{:T(128)S(6)} %select_n.30, f32[106720]{0:T(1024)} %param.18), kind=kLoop, calls=%fused_computation.10 | loop fusion | bytes 656260 | tf_op jit(solution)/shard_map/convert_element_type | solution.py:1937
  2.6 2.4 %fusion = bf16[245760]{0:T(1024)(128)(2,1)} fusion(s32[]{:T(128)S(6)} %select_n.28, f32[233808]{0:T(1024)} %param.15), kind=kLoop, calls=%fused_computation.3 | loop fusion | bytes 1426756 | tf_op jit(solution)/shard_map/convert_element_type | solution.py:1937
  5.0 0.0 copy-start.3
  5.0 0.0 copy-start.10
  5.0 159.8 %shard_map.202 = (f32[1]{0:T(128)}, f32[3]{0:T(128)}, f32[50,8,768]{2,1,0:T(8,128)}, f32[77,8,512]{2,1,0:T(8,128)}, bf16[20,96,128]{2,1,0:T(8,128)(2,1)}, /*index=5*/bf16[14,64,128]{2,1,0:T(8,128)(2,1)}) custom-call(s32[256]{0:T(256)} %ends_ref.1, f32[3]{0:T(128)} %scale_ref.1, bf16[20,96,128]{2,1,0:T(8,128)(2,1)} %bitcast.9, bf16[14,64,128]{2,1,0:T(8,128)(2,1)} %bitcast.12, ...), custom_call_target="tpu_custom_call" | custom-call | tf_op jit(solution)/shard_map/pallas_call | solution.py:1922
  164.8 0.0 copy-start.9
  164.8 0.0 copy-done.3
  164.8 0.0 copy-done.10
  164.8 0.0 copy-start
  164.8 0.0 copy-start.6
  164.8 0.0 copy-start.8
  164.8 2.1 %fusion.6 = (bf16[106720]{0:T(1024)(128)(2,1)}, f32[106720]{0:T(1024)S(1)}, f32[106720]{0:T(1024)}) fusion(f32[106720]{0:T(1024)S(1)} %copy-done.3, bf16[114688]{0:T(1024)(128)(2,1)} %bitcast.16, s32[]{:T(128)S(6)} %select_n.32, f32[106720]{0:T(1024)S(1)} %copy-done.10), kind=kLoop, calls=%fused_computation.14 | loop fusion | flops 853760 | bytes 2134404 | tf_op jit(solution)/shard_map/convert_element_type | solution.py:1987
  167.0 0.0 copy-start.2
  167.0 0.0 copy-done.9
  167.0 0.9 add_multiply_fusion.1
  167.9 0.0 copy-done
  167.9 0.0 copy-done.6
  167.9 0.0 copy-done.8
  167.9 0.0 copy-start.7
  167.9 1.5 fusion.8
  169.4 0.0 copy-done.2
  169.4 0.0 copy-start.1
  169.4 0.0 copy-done.7
  169.4 0.0 copy-start.5
  169.4 1.1 add_multiply_fusion
  170.5 0.2 copy-done.1
  171.4 0.0 copy-done.5
  171.4 1.0 copy.28
  172.4 0.0 copy-done.4
  172.4 1.0 copy.29
  173.5 0.0 copy-done.11
  173.5 0.5 copy.30
  (2 shorter events, 0.0 us)
Async XLA Ops:
  5.0 159.8 %copy-start.3 = (f32[106720]{0:T(1024)S(1)}, f32[106720]{0:T(1024)}, u32[]{:S(2)}) copy-start(f32[106720]{0:T(1024)} %param.18) | copy-start | bytes 1280644
  5.0 159.8 %copy-start.10 = (f32[106720]{0:T(1024)S(1)}, f32[106720]{0:T(1024)}, u32[]{:S(2)}) copy-start(f32[106720]{0:T(1024)} %param.19) | copy-start | bytes 1280644
  164.8 2.2 %copy-start.9 = (f32[106720]{0:T(1024)S(1)}, f32[106720]{0:T(1024)}, u32[]{:S(2)}) copy-start(f32[106720]{0:T(1024)} %param.20) | copy-start | bytes 1280644
  164.8 3.1 %copy-start = (f32[233808]{0:T(1024)S(1)}, f32[233808]{0:T(1024)}, u32[]{:S(2)}) copy-start(f32[233808]{0:T(1024)} %param.15) | copy-start | bytes 2805700
  164.8 3.1 %copy-start.6 = (f32[233808]{0:T(1024)S(1)}, f32[233808]{0:T(1024)}, u32[]{:S(2)}) copy-start(f32[233808]{0:T(1024)} %param.16) | copy-start | bytes 2805700
  164.8 3.1 %copy-start.8 = (bf16[20,96,128]{2,1,0:T(8,128)(2,1)S(1)}, bf16[20,96,128]{2,1,0:T(8,128)(2,1)}, u32[]{:S(2)}) copy-start(bf16[20,96,128]{2,1,0:T(8,128)(2,1)} %get-tuple-element.21) | copy-start | bytes 1474564
  167.0 2.5 %copy-start.2 = (f32[106720]{0:T(1024)}, f32[106720]{0:T(1024)S(1)}, u32[]{:S(2)}) copy-start(f32[106720]{0:T(1024)S(1)} %get-tuple-element.49) | copy-start | bytes 1280644
  167.9 1.5 copy-start.7
  169.4 1.2 copy-start.1
  169.4 2.0 %copy-start.5 = (f32[50,8,768]{2,1,0:T(8,128)S(1)}, f32[50,8,768]{2,1,0:T(8,128)}, u32[]{:S(2)}) copy-start(f32[50,8,768]{2,1,0:T(8,128)} %get-tuple-element.19) | copy-start | bytes 3686404
  170.7 1.8 %copy-start.4 = (f32[77,8,512]{2,1,0:T(8,128)S(1)}, f32[77,8,512]{2,1,0:T(8,128)}, u32[]{:S(2)}) copy-start(f32[77,8,512]{2,1,0:T(8,128)} %get-tuple-element.20) | copy-start | bytes 3784708
  172.4 1.0 copy-start.11

commit v8 on v7

--- a/solution.py
+++ b/solution.py
@@ -193,9 +193,9 @@
 
 
 class Ring:
-    def __init__(self, src, dst, send, recv, only=None):
+    def __init__(self, src, dst, send, recv, only=None, narrow=None):
         self.src, self.dst, self.send, self.recv = src, dst, send, recv
-        self.only = only
+        self.only, self.narrow = only, narrow
         self.tower, self.at = here()
         self.deep, self.row, self.core = self.at // 4, self.at // 2 % 2, self.at % 2
         self.sibling = (self.tower, self.at + 1 - 2 * self.core)
@@ -205,30 +205,53 @@
     def spot(self, k, row):
         return (self.deep + k) % 4 * 4 + row * 2 + self.core
 
-    def act(self, action):
-        if self.only is None:
-            action()
-        else:
-            pl.when(self.tower == self.only)(action)
+    def forms(self, make):
+        def whole(block):
+            return block
+
+        def part(block):
+            return block.at[:, pl.ds(0, self.narrow)]
+
+        if self.only is not None:
+            return [(self.tower == self.only, make(whole))]
+        if self.narrow is None:
+            return [(None, make(whole))]
+        return [(self.tower == 0, make(whole)), (self.tower == 1, make(part))]
+
+    def act(self, forms, name):
+        for when, copy in forms:
+            action = getattr(copy, name)
+            if when is None:
+                action()
+            else:
+                pl.when(when)(action)
+
+    def remote(self, src, slot, sent, landed, device):
+        return self.forms(
+            lambda cut: remote(
+                cut(src), cut(self.dst.at[slot]), self.send.at[sent], self.recv.at[landed], device
+            )
+        )
 
     def launch(self, src, slot, index, device):
-        copy = remote(src, self.dst.at[slot], self.send.at[index], self.recv.at[index], device)
-        self.act(copy.start)
-        self.sent.append(copy)
+        forms = self.remote(src, slot, index, index, device)
+        self.act(forms, "start")
+        self.sent.append(forms)
 
     def arrived(self, slot, index):
-        copy = remote(
-            self.src, self.dst.at[slot], self.send.at[index], self.recv.at[index], self.sibling
-        )
-        self.act(copy.wait_recv)
+        self.act(self.remote(self.src, slot, index, index, self.sibling), "wait_recv")
 
     def start(self):
         for k in (1, 3, 2):
             self.launch(self.src, self.at, k - 1, (self.tower, self.spot(k, self.row)))
         self.launch(self.src, self.at, 3, self.beside)
         self.launch(self.src, self.at, 7, self.sibling)
-        self.own = pltpu.make_async_copy(self.src, self.dst.at[self.at], self.send.at[15])
-        self.act(self.own.start)
+        self.own = self.forms(
+            lambda cut: pltpu.make_async_copy(
+                cut(self.src), cut(self.dst.at[self.at]), self.send.at[15]
+            )
+        )
+        self.act(self.own, "start")
 
     def relay_deep(self):
         for k in (1, 3, 2):
@@ -248,11 +271,11 @@
             k, row = index % 4, self.row if index < 4 else 1 - self.row
             slot = (self.deep + 4 - k) % 4 * 4 + row * 2 + 1 - self.core
             self.arrived(slot, 7 + index)
-        self.act(self.own.wait)
+        self.act(self.own, "wait")
 
     def drain(self):
-        for copy in self.sent:
-            self.act(copy.wait_send)
+        for forms in self.sent:
+            self.act(forms, "wait_send")
 
 
 class Chain:
@@ -332,9 +355,85 @@
             self.act(copy.wait_send, when)
 
 
-def rings(src, dst, send, recv, way=Ring):
+class Plane:
+    def __init__(self, src, via, dst, send, recv):
+        self.src, self.via, self.dst, self.send, self.recv = src, via, dst, send, recv
+        self.tower, self.at = here()
+        self.deep, self.row, self.core = self.at // 4, self.at // 2 % 2, self.at % 2
+        self.partner = (1 - self.tower, self.at)
+        self.sibling = (self.tower, self.at + 1 - 2 * self.core)
+        self.beside = (self.tower, self.at + 2 - 4 * self.row)
+        self.sent = []
+
+    def spot(self, k, row):
+        return (self.deep + k) % 4 * 2 + row
+
+    def launch(self, src, slot, index, device):
+        copy = remote(src, self.via.at[slot], self.send.at[index], self.recv.at[index], device)
+        pl.when(self.tower == 1)(copy.start)
+        self.sent.append(copy)
+
+    def arrived(self, slot, index):
+        copy = remote(
+            self.src, self.via.at[slot], self.send.at[index], self.recv.at[index], self.sibling
+        )
+        pl.when(self.tower == 1)(copy.wait_recv)
+
+    def start(self):
+        own = self.spot(0, self.row)
+        for k in (1, 3, 2):
+            there = self.spot(k, self.row) * 2 + self.core
+            self.launch(self.src, own, k - 1, (self.tower, there))
+        self.launch(self.src, own, 3, self.beside)
+        self.own = pltpu.make_async_copy(self.src, self.via.at[own], self.send.at[7])
+        pl.when(self.tower == 1)(self.own.start)
+
+    def relay_deep(self):
+        for k in (1, 3, 2):
+            slot = self.spot(4 - k, self.row)
+            self.arrived(slot, k - 1)
+            self.launch(self.via.at[slot], slot, 3 + k, self.beside)
+
+    def relay_row(self):
+        for k in range(4):
+            self.arrived(self.spot(4 - k, 1 - self.row), 3 + k)
+        pl.when(self.tower == 1)(self.own.wait)
+        pl.when(self.tower == 1)(self.down().start)
+
+    def down(self):
+        return remote(
+            self.via, self.dst.at[self.core], self.send.at[8], self.recv.at[7], self.partner
+        )
+
+    def across(self, core):
+        return remote(
+            self.dst.at[core], self.dst.at[core], self.send.at[9], self.recv.at[8], self.sibling
+        )
+
+    def land(self):
+        pl.when(self.tower == 0)(self.down().wait_recv)
+        pl.when(self.tower == 0)(self.across(self.core).start)
+
+    def finish(self):
+        pl.when(self.tower == 0)(self.across(1 - self.core).wait_recv)
+
+    def drain(self):
+        for copy in self.sent:
+            pl.when(self.tower == 1)(copy.wait_send)
+        pl.when(self.tower == 1)(self.down().wait_send)
+        pl.when(self.tower == 0)(self.across(self.core).wait_send)
+
+
+def rings(src, dst, send, recv, way=Ring, *narrow):
     return [
-        way(src.at[part], dst.at[part], send.at[part], recv.at[part], 0 if part == 2 else None)
+        way(
+            src.at[part],
+            dst.at[part],
+            send.at[part],
+            recv.at[part],
+            0 if part == 2 else None,
+            *narrow,
+        )
         for part in range(3)
     ]
 
@@ -403,6 +502,7 @@
 
 VECTORS = 5
 EXPAND = 2
+EMBED = 4
 TURN = 8
 
 
@@ -466,14 +566,17 @@
         return condition if self.only is None else jnp.logical_and(condition, self.tower == self.only)
 
     def move(self, src, i, piece, at_to, slot, wait):
-        far = jnp.logical_or(self.tower != self.plan.tower, at_to != self.at)
+        tower_to = self.plan.tower
+        if not isinstance(piece, int):
+            tower_to = jnp.where(piece == EMBED, 1, tower_to)
+        far = jnp.logical_or(self.tower != tower_to, at_to != self.at)
         recv = self.recv.at[self.plan.tower, piece]
         copy = remote(
             src,
             self.dst.at[slot],
             self.chunk_send.at[self.s, i],
             recv,
-            (jnp.int32(self.plan.tower), at_to),
+            (tower_to, at_to),
         )
         pl.when(far)(copy.wait_send if wait else copy.start)
         if not wait:
@@ -720,6 +823,12 @@
         ],
         axis=0,
     )
+
+
+def embed_matrix(refs, kind):
+    if kind.index == 1:
+        return matrix(refs[1], kind, 0, EMB)
+    return jnp.concatenate([refs[0][at % 2, at // 2] for at in range(16)], axis=0)
 
 
 def vector(vec_ref, kind, row):
@@ -851,7 +960,7 @@
         hat, _ = standardise(final)
         pooled = (hat * vector(vec_ref, kind, 8) + vector(vec_ref, kind, 9)).astype(LOW)
         pooled_ref[:, :width] = pooled
-        proj = dot_nn(pooled, matrix(gat_ref, kind, 0, EMB))
+        proj = dot_nn(pooled, embed_matrix(gat_ref, kind))
         proj_ref[...] = proj
         size = jnp.sum(proj * proj, axis=-1, keepdims=True) + 1e-06
         emb_ref[...] = (proj * lax.rsqrt(size)).astype(LOW)
@@ -938,7 +1047,7 @@
         along = jnp.sum(proj * mine, axis=-1, keepdims=True)
         proj_grad = ((mine - proj * along / size) * lax.rsqrt(size)).astype(LOW)
         proj_grad_ref[...] = proj_grad
-        pooled_grad = dot_nt(proj_grad, matrix(gat_ref, kind, 0, EMB))
+        pooled_grad = dot_nt(proj_grad, embed_matrix(gat_ref, kind))
         hat, rate = standardise(final_ref[:, :width])
         final_vec_ref[0:1, :width] = jnp.sum(pooled_grad * hat, axis=0, keepdims=True)
         final_vec_ref[1:2, :width] = jnp.sum(pooled_grad, axis=0, keepdims=True)
@@ -996,6 +1105,9 @@
     ask_block,
     mix_block,
     emb_block,
+    plane_block,
+    plane_via,
+    plane_ref,
     raise_block,
     reduce_block,
     mask_block,
@@ -1066,6 +1178,8 @@
     mix_recv,
     emb_send,
     emb_recv,
+    plane_send,
+    plane_recv,
     raise_send,
     raise_recv,
     reduce_sems,
@@ -1115,9 +1229,13 @@
         (jnp.logical_and(me > 0, me <= 16), over),
     )
     pair = Pair(txt_own, txt_in, img_own, img_in, pair_sems)
-    asks = rings(ask_block, ask_ref, ask_send, ask_recv)
-    mixes = rings(mix_block, mix_ref, mix_send, mix_recv)
-    embeds = rings(emb_block, emb_ref, emb_send, emb_recv, Chain)
+    asks = rings(ask_block, ask_ref, ask_send, ask_recv, Ring, 2 * D_TXT)
+    mixes = rings(mix_block, mix_ref, mix_send, mix_recv, Ring, 2 * D_TXT)
+    embeds = [
+        Chain(emb_block.at[part], emb_ref.at[part], emb_send.at[part], emb_recv.at[part], 1)
+        for part in range(2)
+    ]
+    plane = Plane(plane_block, plane_via, plane_ref, plane_send, plane_recv)
     rise = Group(raise_block, raise_ref, raise_send, raise_recv)
     fall = remote(
         reduce_block, reduce_ref.at[core], reduce_sems.at[0], reduce_sems.at[1], sibling
@@ -1211,10 +1329,9 @@
         slots = (img_slots, txt_slots)[kind.index]
         per = kind.width // LANES
         for c, value in lift(kind, plans[kind.index], 0, slots, flat):
-            lane = c // per * WIDTH + c % per * LANES
-            ref = ask_block
-            if lane >= 2 * WIDTH:
-                ref, lane = mix_block, lane - 2 * WIDTH
+            ref, lane = ask_block, c * LANES
+            if c >= 2 * per:
+                ref, lane = mix_block, lane - 2 * kind.width
             put(ref, lane, value.astype(LOW))
 
     each_tower(place_inputs)
@@ -1234,9 +1351,13 @@
 
     def place_rest(kind):
         deals[kind.index].arrived(1)
-        lift_to(kind, 1, mix_block, WIDTH)
-        deals[kind.index].arrived(4)
-        lift_to(kind, 4, emb_block, 0)
+        lift_to(kind, 1, mix_block, kind.width)
+        if kind.index == 1:
+            deals[1].arrived(EMBED)
+            lift_to(kind, EMBED, emb_block, 0)
+            deals[0].arrived(EMBED)
+            for c, value in lift(TOWERS[0], plans[0], EMBED, img_slots, flat):
+                plane_block[:, c * LANES : (c + 1) * LANES] = value.astype(LOW)
 
     each_tower(place_rest)
 
@@ -1251,16 +1372,18 @@
             put_rows(
                 keyed_ref,
                 pl.ds(first_head * SEQS, n * SEQS),
-                dot_nt(head_rows(query, span), matrix(ask_ref, kind, WIDTH + lo, hi - lo)) * 0.125,
+                dot_nt(head_rows(query, span), matrix(ask_ref, kind, width + lo, hi - lo)) * 0.125,
             )
         dead = (HEADS - kind.heads) * SEQS
         put_rows(keyed_ref, pl.ds(kind.heads * SEQS, dead), jnp.zeros((dead, width), WIDE))
 
-    for ask, mix in zip(asks, mixes):
+    for ask in asks:
         ask.relay_deep()
+    for mix in mixes:
         mix.start()
     for embed in embeds:
         embed.start()
+    plane.start()
     for ask in asks:
         ask.relay_row()
     each_tower(place_hidden)
@@ -1275,6 +1398,7 @@
     each_tower(question)
     for ring in (*mixes, *embeds):
         ring.relay_deep()
+    plane.relay_deep()
 
     def score(kind):
         width, room = kind.width, kind.room
@@ -1298,6 +1422,7 @@
     each_tower(score)
     for ring in (*mixes, *embeds):
         ring.relay_row()
+    plane.relay_row()
 
     def mixture(kind):
         width, room = kind.width, kind.room
@@ -1332,7 +1457,7 @@
         mixed = side_by_side(mixed).astype(LOW)
         middle = (
             at_scr[:, :width]
-            + dot_nn(mixed, matrix(mix_ref, kind, WIDTH, width))
+            + dot_nn(mixed, matrix(mix_ref, kind, width, width))
             + vector(vec_ref, kind, 4)
         )
         middle_ref[:, :width] = middle
@@ -1356,8 +1481,10 @@
 
     sent = group_exchange(False, second_ref, seconds, group_send.at[0], group_recv.at[0])
     hidden_kernel(seconds, raise_ref, reduce_ref, vec_ref, part, raised)
+    plane.land()
     sent += group_exchange(True, part, parts, group_send.at[1], group_recv.at[1])
-    embed_kernel(parts, middle_ref, emb_ref, vec_ref, emb, final, pooled_ref, proj)
+    plane.finish()
+    embed_kernel(parts, middle_ref, (plane_ref, emb_ref), vec_ref, emb, final, pooled_ref, proj)
     embs = Spread(emb, all_embs, embs_send, embs_recv)
     embs.start()
     masks.finish()
@@ -1369,7 +1496,7 @@
         pairs_ref,
         final,
         proj,
-        emb_ref,
+        (plane_ref, emb_ref),
         vec_ref,
         low,
         grad_ref,
@@ -1422,7 +1549,7 @@
         )
         middle_scr[:, :width] = middle_grad
         output_grad = middle_grad.astype(LOW)
-        mixed_grad = dot_nt(output_grad, matrix(mix_ref, kind, WIDTH, width)).astype(LOW)
+        mixed_grad = dot_nt(output_grad, matrix(mix_ref, kind, width, width)).astype(LOW)
         early_block[:, 0:width] = query_ref[:, :width]
         early_block[:, WIDTH : WIDTH + width] = mixed_grad
         early_block[:, 2 * WIDTH : 2 * WIDTH + width] = output_grad
@@ -1507,7 +1634,7 @@
         for span in spans(kind):
             lo, hi, first_head, n = span
             rows = get_rows(turn_scr, pl.ds(first_head * SEQS, n * SEQS), width).astype(LOW)
-            back = dot_nn(rows, matrix(ask_ref, kind, WIDTH + lo, hi - lo)) * 0.125
+            back = dot_nn(rows, matrix(ask_ref, kind, width + lo, hi - lo)) * 0.125
             grads.append(from_head_rows(back, span))
         query_grad = side_by_side(grads).astype(LOW)
         late_block[:, :width] = query_grad
@@ -1753,7 +1880,7 @@
     for when, copy in heads:
         pl.when(when)(copy.wait_send)
     pl.when(tower == 0)(relay.wait_send)
-    for group in (pair, *asks, *mixes, *embeds, rise, masks, embs, *deals):
+    for group in (pair, *asks, *mixes, *embeds, plane, rise, masks, embs, *deals):
         group.drain()
     for group in (risen_group, lefts, turns, early, late, home_pair):
         group.drain()
@@ -1817,6 +1944,9 @@
         ((3, 16, 2 * WIDTH), LOW),
         ((3, 16, 2 * WIDTH), LOW),
         ((3, 16, EMB), LOW),
+        ((48, EMB), LOW),
+        ((8, 48, EMB), LOW),
+        ((2, 8, 48, EMB), LOW),
         ((8, 48, PART), LOW),
         ((192, WIDTH), LOW),
         ((16, LANES), LOW),
@@ -1889,6 +2019,8 @@
         (3, 15),
         (3, 20),
         (3, 15),
+        (10,),
+        (9,),
         (9,),
         (8,),
         (3,),

time: 175 us -> 173 us (0.989)
  Pallas kernels: 160 us -> 157 us
    pallas_call x1, Pallas kernels: 160 us -> 157 us  [run_step(): pl.pallas_call(functools.partial(step_kernel, plans), out_shape=[like((1,...]
where the time goes in v8:
time: 173 us
  Pallas kernels  157 us (91%)
  local copies, waits for them, and re-layouts  7.08 us (4%)
  other arithmetic  5.62 us (3%)
  between operations  2.65 us (2%)
    pallas_call x1, Pallas kernels, run_step(): pl.pallas_call(functools.partial(step_kernel, plans), out_shape=[like((1,...  157 us
    convert_element_type x2, local copies, waits for them, and re-layouts, to_chunks(): return piece.astype(LOW).reshape(plan.local, plan.rows, LANES)  4.29 us

profile of v8, /device:TPU:3, one launch (start us, length us, event | category | flops | bytes accessed | tf_op | source)
XLA Modules:
  0.0 172.5 jit_solution(10698850994430737909)
XLA Ops:
  0.7 1.9 %fusion.3 = bf16[114688]{0:T(1024)(128)(2,1)} fusion(s32[]{:T(128)S(6)} %select_n.30, f32[106720]{0:T(1024)} %param.18), kind=kLoop, calls=%fused_computation.10 | loop fusion | bytes 656260 | tf_op jit(solution)/shard_map/convert_element_type | solution.py:2069
  2.6 2.4 %fusion = bf16[245760]{0:T(1024)(128)(2,1)} fusion(s32[]{:T(128)S(6)} %select_n.28, f32[233808]{0:T(1024)} %param.15), kind=kLoop, calls=%fused_computation.3 | loop fusion | bytes 1426756 | tf_op jit(solution)/shard_map/convert_element_type | solution.py:2069
  5.0 0.0 copy-start.3
  5.0 0.0 copy-start.10
  5.0 157.2 %shard_map.202 = (f32[1]{0:T(128)}, f32[3]{0:T(128)}, f32[50,8,768]{2,1,0:T(8,128)}, f32[77,8,512]{2,1,0:T(8,128)}, bf16[20,96,128]{2,1,0:T(8,128)(2,1)}, /*index=5*/bf16[14,64,128]{2,1,0:T(8,128)(2,1)}) custom-call(s32[256]{0:T(256)} %ends_ref.1, f32[3]{0:T(128)} %scale_ref.1, bf16[20,96,128]{2,1,0:T(8,128)(2,1)} %bitcast.9, bf16[14,64,128]{2,1,0:T(8,128)(2,1)} %bitcast.12, ...), custom_call_target="tpu_custom_call" | custom-call | tf_op jit(solution)/shard_map/pallas_call | solution.py:2054
  162.2 0.0 copy-start.9
  162.2 0.0 copy-done.3
  162.2 0.0 copy-done.10
  162.2 0.0 copy-start
  162.2 0.0 copy-start.6
  162.2 0.0 copy-start.8
  162.3 2.1 %fusion.6 = (bf16[106720]{0:T(1024)(128)(2,1)}, f32[106720]{0:T(1024)S(1)}, f32[106720]{0:T(1024)}) fusion(f32[106720]{0:T(1024)S(1)} %copy-done.3, bf16[114688]{0:T(1024)(128)(2,1)} %bitcast.16, s32[]{:T(128)S(6)} %select_n.32, f32[106720]{0:T(1024)S(1)} %copy-done.10), kind=kLoop, calls=%fused_computation.14 | loop fusion | flops 853760 | bytes 2134404 | tf_op jit(solution)/shard_map/convert_element_type | solution.py:2119
  164.4 0.0 copy-start.2
  164.4 0.0 copy-done.9
  164.4 0.9 add_multiply_fusion.1
  165.3 0.0 copy-done
  165.3 0.0 copy-done.6
  165.3 0.0 copy-done.8
  165.3 1.5 fusion.8
  166.8 0.0 copy-done.2
  166.8 0.0 copy-start.1
  166.8 0.0 copy-done.7
  166.8 0.0 copy-start.5
  166.8 1.1 add_multiply_fusion
  167.9 0.2 copy-done.1
  168.1 0.0 copy-start.4
  168.8 0.0 copy-done.5
  168.8 1.0 copy.28
  169.9 0.0 copy-done.4
  169.9 1.0 copy.29
  170.9 0.0 copy-done.11
  170.9 0.5 copy.30
  (2 shorter events, 0.0 us)
Async XLA Ops:
  5.0 157.2 %copy-start.3 = (f32[106720]{0:T(1024)S(1)}, f32[106720]{0:T(1024)}, u32[]{:S(2)}) copy-start(f32[106720]{0:T(1024)} %param.18) | copy-start | bytes 1280644
  5.0 157.2 %copy-start.10 = (f32[106720]{0:T(1024)S(1)}, f32[106720]{0:T(1024)}, u32[]{:S(2)}) copy-start(f32[106720]{0:T(1024)} %param.19) | copy-start | bytes 1280644
  162.2 2.2 %copy-start.9 = (f32[106720]{0:T(1024)S(1)}, f32[106720]{0:T(1024)}, u32[]{:S(2)}) copy-start(f32[106720]{0:T(1024)} %param.20) | copy-start | bytes 1280644
  162.2 3.1 %copy-start = (f32[233808]{0:T(1024)S(1)}, f32[233808]{0:T(1024)}, u32[]{:S(2)}) copy-start(f32[233808]{0:T(1024)} %param.15) | copy-start | bytes 2805700
  162.2 3.1 %copy-start.6 = (f32[233808]{0:T(1024)S(1)}, f32[233808]{0:T(1024)}, u32[]{:S(2)}) copy-start(f32[233808]{0:T(1024)} %param.16) | copy-start | bytes 2805700
  162.2 3.1 %copy-start.8 = (bf16[20,96,128]{2,1,0:T(8,128)(2,1)S(1)}, bf16[20,96,128]{2,1,0:T(8,128)(2,1)}, u32[]{:S(2)}) copy-start(bf16[20,96,128]{2,1,0:T(8,128)(2,1)} %get-tuple-element.21) | copy-start | bytes 1474564
  164.4 2.5 %copy-start.2 = (f32[106720]{0:T(1024)}, f32[106720]{0:T(1024)S(1)}, u32[]{:S(2)}) copy-start(f32[106720]{0:T(1024)S(1)} %get-tuple-element.49) | copy-start | bytes 1280644
  165.3 1.5 copy-start.7
  166.8 1.2 copy-start.1
  166.8 2.0 %copy-start.5 = (f32[50,8,768]{2,1,0:T(8,128)S(1)}, f32[50,8,768]{2,1,0:T(8,128)}, u32[]{:S(2)}) copy-start(f32[50,8,768]{2,1,0:T(8,128)} %get-tuple-element.19) | copy-start | bytes 3686404
  168.1 1.8 %copy-start.4 = (f32[77,8,512]{2,1,0:T(8,128)S(1)}, f32[77,8,512]{2,1,0:T(8,128)}, u32[]{:S(2)}) copy-start(f32[77,8,512]{2,1,0:T(8,128)} %get-tuple-element.20) | copy-start | bytes 3784708
  169.9 1.0 copy-start.11

commit v9 on v8

--- a/solution.py
+++ b/solution.py
@@ -1791,6 +1791,11 @@
         left_scr[:block, :256] = gathered(12).astype(WIDE)
 
     each_tower(from_early)
+    for when, copy in heads:
+        pl.when(when)(copy.wait_send)
+    pl.when(tower == 0)(relay.wait_send)
+    for group in (pair, *asks, *mixes, *embeds, plane, rise, masks, embs, *deals):
+        group.drain()
     late.finish()
     turns.finish()
 
@@ -1872,16 +1877,9 @@
     def _():
         txt_keep[...] = txt_home[...].astype(WIDE)
 
-    for collect in collects:
-        collect.finish()
     for copy in (*sent, fall, fallen, halves):
         copy.wait_send()
     pl.when(at > 0)(line_copy.wait_send)
-    for when, copy in heads:
-        pl.when(when)(copy.wait_send)
-    pl.when(tower == 0)(relay.wait_send)
-    for group in (pair, *asks, *mixes, *embeds, plane, rise, masks, embs, *deals):
-        group.drain()
     for group in (risen_group, lefts, turns, early, late, home_pair):
         group.drain()
 
@@ -1890,6 +1888,8 @@
             collects[kind.index].piece(p, True)
 
     each_tower(drain)
+    for collect in collects:
+        collect.finish()
 
 
 ROWS_LOW = ((SEQS, WIDTH), LOW)

time: 173 us -> 170 us (0.983)
  Pallas kernels: 157 us -> 154 us
    pallas_call x1, Pallas kernels: 157 us -> 154 us  [run_step(): pl.pallas_call(functools.partial(step_kernel, plans), out_shape=[like((1,...]
where the time goes in v9:
time: 170 us
  Pallas kernels  154 us (91%)
  local copies, waits for them, and re-layouts  7.08 us (4%)
  other arithmetic  5.62 us (3%)
  between operations  2.65 us (2%)
    pallas_call x1, Pallas kernels, run_step(): pl.pallas_call(functools.partial(step_kernel, plans), out_shape=[like((1,...  154 us
    convert_element_type x2, local copies, waits for them, and re-layouts, to_chunks(): return piece.astype(LOW).reshape(plan.local, plan.rows, LANES)  4.29 us

profile of v9, /device:TPU:3, one launch (start us, length us, event | category | flops | bytes accessed | tf_op | source)
XLA Modules:
  0.0 169.6 jit_solution(16785769325630156757)
XLA Ops:
  0.7 1.9 %fusion.3 = bf16[114688]{0:T(1024)(128)(2,1)} fusion(s32[]{:T(128)S(6)} %select_n.30, f32[106720]{0:T(1024)} %param.18), kind=kLoop, calls=%fused_computation.10 | loop fusion | bytes 656260 | tf_op jit(solution)/shard_map/convert_element_type | solution.py:2069
  2.6 2.4 %fusion = bf16[245760]{0:T(1024)(128)(2,1)} fusion(s32[]{:T(128)S(6)} %select_n.28, f32[233808]{0:T(1024)} %param.15), kind=kLoop, calls=%fused_computation.3 | loop fusion | bytes 1426756 | tf_op jit(solution)/shard_map/convert_element_type | solution.py:2069
  5.0 0.0 copy-start.3
  5.0 0.0 copy-start.10
  5.0 154.2 %shard_map.202 = (f32[1]{0:T(128)}, f32[3]{0:T(128)}, f32[50,8,768]{2,1,0:T(8,128)}, f32[77,8,512]{2,1,0:T(8,128)}, bf16[20,96,128]{2,1,0:T(8,128)(2,1)}, /*index=5*/bf16[14,64,128]{2,1,0:T(8,128)(2,1)}) custom-call(s32[256]{0:T(256)} %ends_ref.1, f32[3]{0:T(128)} %scale_ref.1, bf16[20,96,128]{2,1,0:T(8,128)(2,1)} %bitcast.9, bf16[14,64,128]{2,1,0:T(8,128)(2,1)} %bitcast.12, ...), custom_call_target="tpu_custom_call" | custom-call | tf_op jit(solution)/shard_map/pallas_call | solution.py:2054
  159.2 0.0 copy-start.9
  159.2 0.0 copy-done.3
  159.3 0.0 copy-done.10
  159.3 0.0 copy-start
  159.3 0.0 copy-start.6
  159.3 0.0 copy-start.8
  159.3 2.1 %fusion.6 = (bf16[106720]{0:T(1024)(128)(2,1)}, f32[106720]{0:T(1024)S(1)}, f32[106720]{0:T(1024)}) fusion(f32[106720]{0:T(1024)S(1)} %copy-done.3, bf16[114688]{0:T(1024)(128)(2,1)} %bitcast.16, s32[]{:T(128)S(6)} %select_n.32, f32[106720]{0:T(1024)S(1)} %copy-done.10), kind=kLoop, calls=%fused_computation.14 | loop fusion | flops 853760 | bytes 2134404 | tf_op jit(solution)/shard_map/convert_element_type | solution.py:2119
  161.4 0.0 copy-done.9
  161.4 0.9 add_multiply_fusion.1
  162.3 0.0 copy-done
  162.3 0.0 copy-done.6
  162.3 0.0 copy-done.8
  162.3 0.0 copy-start.7
  162.4 1.5 fusion.8
  163.9 0.0 copy-done.2
  163.9 0.0 copy-done.7
  163.9 0.0 copy-start.5
  163.9 1.1 add_multiply_fusion
  165.0 0.2 copy-done.1
  165.1 0.0 copy-start.4
  165.9 0.0 copy-done.5
  165.9 1.0 copy.28
  166.9 0.0 copy-done.4
  166.9 0.0 copy-start.11
  166.9 1.0 copy.29
  168.0 0.0 copy-done.11
  168.0 0.5 copy.30
  (2 shorter events, 0.0 us)
Async XLA Ops:
  5.0 154.3 %copy-start.3 = (f32[106720]{0:T(1024)S(1)}, f32[106720]{0:T(1024)}, u32[]{:S(2)}) copy-start(f32[106720]{0:T(1024)} %param.18) | copy-start | bytes 1280644
  5.0 154.3 %copy-start.10 = (f32[106720]{0:T(1024)S(1)}, f32[106720]{0:T(1024)}, u32[]{:S(2)}) copy-start(f32[106720]{0:T(1024)} %param.19) | copy-start | bytes 1280644
  159.2 2.2 %copy-start.9 = (f32[106720]{0:T(1024)S(1)}, f32[106720]{0:T(1024)}, u32[]{:S(2)}) copy-start(f32[106720]{0:T(1024)} %param.20) | copy-start | bytes 1280644
  159.3 3.1 %copy-start = (f32[233808]{0:T(1024)S(1)}, f32[233808]{0:T(1024)}, u32[]{:S(2)}) copy-start(f32[233808]{0:T(1024)} %param.15) | copy-start | bytes 2805700
  159.3 3.1 %copy-start.6 = (f32[233808]{0:T(1024)S(1)}, f32[233808]{0:T(1024)}, u32[]{:S(2)}) copy-start(f32[233808]{0:T(1024)} %param.16) | copy-start | bytes 2805700
  159.3 3.1 %copy-start.8 = (bf16[20,96,128]{2,1,0:T(8,128)(2,1)S(1)}, bf16[20,96,128]{2,1,0:T(8,128)(2,1)}, u32[]{:S(2)}) copy-start(bf16[20,96,128]{2,1,0:T(8,128)(2,1)} %get-tuple-element.21) | copy-start | bytes 1474564
  161.4 2.5 %copy-start.2 = (f32[106720]{0:T(1024)}, f32[106720]{0:T(1024)S(1)}, u32[]{:S(2)}) copy-start(f32[106720]{0:T(1024)S(1)} %get-tuple-element.49) | copy-start | bytes 1280644
  162.3 1.5 copy-start.7
  163.9 1.2 copy-start.1
  163.9 2.0 %copy-start.5 = (f32[50,8,768]{2,1,0:T(8,128)S(1)}, f32[50,8,768]{2,1,0:T(8,128)}, u32[]{:S(2)}) copy-start(f32[50,8,768]{2,1,0:T(8,128)} %get-tuple-element.19) | copy-start | bytes 3686404
  165.1 1.8 %copy-start.4 = (f32[77,8,512]{2,1,0:T(8,128)S(1)}, f32[77,8,512]{2,1,0:T(8,128)}, u32[]{:S(2)}) copy-start(f32[77,8,512]{2,1,0:T(8,128)} %get-tuple-element.20) | copy-start | bytes 3784708
  166.9 1.0 copy-start.11

commit v10 on v9

--- a/solution.py
+++ b/solution.py
@@ -1255,10 +1255,10 @@
     deals[1].whole(True, False)
     deals[0].whole(False, False)
     deals[1].whole(False, False)
-    pair.start()
     deals[0].join()
     deals[1].join()
     pl.when(tower == 1)(relay.wait_recv)
+    pair.start()
     deals[2].start_fetch()
     deals[2].whole(True, False)
     deals[2].join()

time: 170 us -> 172 us (1.012)
  Pallas kernels: 154 us -> 156 us
    pallas_call x1, Pallas kernels: 154 us -> 156 us  [run_step(): pl.pallas_call(functools.partial(step_kernel, plans), out_shape=[like((1,...]
where the time goes in v10:
time: 172 us
  Pallas kernels  156 us (91%)
  local copies, waits for them, and re-layouts  7.08 us (4%)
  other arithmetic  5.62 us (3%)
  between operations  2.65 us (2%)
    pallas_call x1, Pallas kernels, run_step(): pl.pallas_call(functools.partial(step_kernel, plans), out_shape=[like((1,...  156 us
    convert_element_type x2, local copies, waits for them, and re-layouts, to_chunks(): return piece.astype(LOW).reshape(plan.local, plan.rows, LANES)  4.29 us

profile of v10, /device:TPU:3, one launch (start us, length us, event | category | flops | bytes accessed | tf_op | source)
XLA Modules:
  0.0 171.7 jit_solution(16993335983848110962)
XLA Ops:
  0.7 1.9 %fusion.3 = bf16[114688]{0:T(1024)(128)(2,1)} fusion(s32[]{:T(128)S(6)} %select_n.30, f32[106720]{0:T(1024)} %param.18), kind=kLoop, calls=%fused_computation.10 | loop fusion | bytes 656260 | tf_op jit(solution)/shard_map/convert_element_type | solution.py:2069
  2.6 2.4 %fusion = bf16[245760]{0:T(1024)(128)(2,1)} fusion(s32[]{:T(128)S(6)} %select_n.28, f32[233808]{0:T(1024)} %param.15), kind=kLoop, calls=%fused_computation.3 | loop fusion | bytes 1426756 | tf_op jit(solution)/shard_map/convert_element_type | solution.py:2069
  5.0 0.0 copy-start.3
  5.0 0.0 copy-start.10
  5.0 156.4 %shard_map.202 = (f32[1]{0:T(128)}, f32[3]{0:T(128)}, f32[50,8,768]{2,1,0:T(8,128)}, f32[77,8,512]{2,1,0:T(8,128)}, bf16[20,96,128]{2,1,0:T(8,128)(2,1)}, /*index=5*/bf16[14,64,128]{2,1,0:T(8,128)(2,1)}) custom-call(s32[256]{0:T(256)} %ends_ref.1, f32[3]{0:T(128)} %scale_ref.1, bf16[20,96,128]{2,1,0:T(8,128)(2,1)} %bitcast.9, bf16[14,64,128]{2,1,0:T(8,128)(2,1)} %bitcast.12, ...), custom_call_target="tpu_custom_call" | custom-call | tf_op jit(solution)/shard_map/pallas_call | solution.py:2054
  161.4 0.0 copy-start.9
  161.4 0.0 copy-done.3
  161.4 0.0 copy-done.10
  161.4 0.0 copy-start
  161.4 0.0 copy-start.6
  161.4 0.0 copy-start.8
  161.4 2.1 %fusion.6 = (bf16[106720]{0:T(1024)(128)(2,1)}, f32[106720]{0:T(1024)S(1)}, f32[106720]{0:T(1024)}) fusion(f32[106720]{0:T(1024)S(1)} %copy-done.3, bf16[114688]{0:T(1024)(128)(2,1)} %bitcast.16, s32[]{:T(128)S(6)} %select_n.32, f32[106720]{0:T(1024)S(1)} %copy-done.10), kind=kLoop, calls=%fused_computation.14 | loop fusion | flops 853760 | bytes 2134404 | tf_op jit(solution)/shard_map/convert_element_type | solution.py:2119
  163.6 0.0 copy-start.2
  163.6 0.0 copy-done.9
  163.6 0.9 add_multiply_fusion.1
  164.5 0.0 copy-done
  164.5 0.0 copy-done.6
  164.5 0.0 copy-done.8
  164.5 0.0 copy-start.7
  164.5 1.5 fusion.8
  166.0 0.0 copy-done.2
  166.0 0.0 copy-start.1
  166.0 0.0 copy-done.7
  166.0 0.0 copy-start.5
  166.0 1.1 add_multiply_fusion
  167.1 0.2 copy-done.1
  168.0 0.0 copy-done.5
  168.0 1.0 copy.28
  169.0 0.0 copy-done.4
  169.1 1.0 copy.29
  170.1 0.0 copy-done.11
  170.1 0.5 copy.30
  (2 shorter events, 0.0 us)
Async XLA Ops:
  5.0 156.4 %copy-start.3 = (f32[106720]{0:T(1024)S(1)}, f32[106720]{0:T(1024)}, u32[]{:S(2)}) copy-start(f32[106720]{0:T(1024)} %param.18) | copy-start | bytes 1280644
  5.0 156.4 %copy-start.10 = (f32[106720]{0:T(1024)S(1)}, f32[106720]{0:T(1024)}, u32[]{:S(2)}) copy-start(f32[106720]{0:T(1024)} %param.19) | copy-start | bytes 1280644
  161.4 2.2 %copy-start.9 = (f32[106720]{0:T(1024)S(1)}, f32[106720]{0:T(1024)}, u32[]{:S(2)}) copy-start(f32[106720]{0:T(1024)} %param.20) | copy-start | bytes 1280644
  161.4 3.1 %copy-start = (f32[233808]{0:T(1024)S(1)}, f32[233808]{0:T(1024)}, u32[]{:S(2)}) copy-start(f32[233808]{0:T(1024)} %param.15) | copy-start | bytes 2805700
  161.4 3.1 %copy-start.6 = (f32[233808]{0:T(1024)S(1)}, f32[233808]{0:T(1024)}, u32[]{:S(2)}) copy-start(f32[233808]{0:T(1024)} %param.16) | copy-start | bytes 2805700
  161.4 3.1 %copy-start.8 = (bf16[20,96,128]{2,1,0:T(8,128)(2,1)S(1)}, bf16[20,96,128]{2,1,0:T(8,128)(2,1)}, u32[]{:S(2)}) copy-start(bf16[20,96,128]{2,1,0:T(8,128)(2,1)} %get-tuple-element.21) | copy-start | bytes 1474564
  163.6 2.5 %copy-start.2 = (f32[106720]{0:T(1024)}, f32[106720]{0:T(1024)S(1)}, u32[]{:S(2)}) copy-start(f32[106720]{0:T(1024)S(1)} %get-tuple-element.49) | copy-start | bytes 1280644
  164.5 1.5 copy-start.7
  166.0 1.2 copy-start.1
  166.0 2.0 %copy-start.5 = (f32[50,8,768]{2,1,0:T(8,128)S(1)}, f32[50,8,768]{2,1,0:T(8,128)}, u32[]{:S(2)}) copy-start(f32[50,8,768]{2,1,0:T(8,128)} %get-tuple-element.19) | copy-start | bytes 3686404
  167.3 1.8 %copy-start.4 = (f32[77,8,512]{2,1,0:T(8,128)S(1)}, f32[77,8,512]{2,1,0:T(8,128)}, u32[]{:S(2)}) copy-start(f32[77,8,512]{2,1,0:T(8,128)} %get-tuple-element.20) | copy-start | bytes 3784708
  169.0 1.0 copy-start.11
